TPU v7x, 256 devices: a whole 4x4x8 slice. The times are simulated.
256 devices in a mesh: section: 16 (over y_hi, z), space: 16 (over x, y_lo, core).
Axes of the slice: x: 4, y: 4 (y_hi: 2, y_lo: 2; y = y_hi * 2 + y_lo), z: 8, core: 2. Of those that a mesh axis runs over, the one named last changes fastest.
Arguments:
- top_a: bfloat16 [16, 2048, 1536], P('section', 'space'), may hold values from -6 to 6
- top_b: bfloat16 [16, 2048, 1536], P('section', 'space'), may hold values from -6 to 6
- grad_a: bfloat16 [16, 2048, 1536], P('section', 'space'), may hold values from -6 to 6
- grad_b: bfloat16 [16, 2048, 1536], P('section', 'space'), may hold values from -6 to 6
- w_qkv: bfloat16 [16, 1536, 2304], P('section'), may hold values from -0.15625 to 0.15625
- w_out: bfloat16 [16, 768, 1536], P('section'), may hold values from -0.21875 to 0.21875
- kernel: float32 [16, 27, 1536], P('section'), may hold values from -1.75 to 1.75
- tau: float32 [16, 12], P('section'), may hold values from 4 to 20
- block_owner: int32 [16, 2], replicated, may hold values from 0 to 15, as said below
Outputs:
- rebuilt_a: bfloat16 [16, 2048, 1536], P('section', 'space')
- rebuilt_b: bfloat16 [16, 2048, 1536], P('section', 'space')
- passed_a: bfloat16 [16, 2048, 1536], P('section', 'space')
- passed_b: bfloat16 [16, 2048, 1536], P('section', 'space')
Inputs may be any that keep to these rules, and one draw needn't show every extreme that they name: `block_owner`: row i lists tile i and one tile beside it, i - 1 or i + 1, in either order; tile 0's other tile is 1 and tile 16 - 1's is 14.
All inputs are finite; a program needn't handle non-finite values.
Results may differ from a plain program's by a relative error of at most 0.039.
Values may be sent and summed in bfloat16 or wider, within the bound.
No kernel may reach another device: no remote copies, remote signals or barrier semaphores. Data moves between devices by JAX's collectives and lax.ppermute only.
A program may use at most 128 MiB of HBM per device.

v0:
```python
import functools

import jax
import jax.numpy as jnp
from jax import lax
from jax.experimental import pallas as pl
from jax.experimental.pallas import tpu as pltpu
from jax.sharding import PartitionSpec as P

HEADS = 12
HEAD = 64
FT = 4
FW = 16
STEPS = 2
PAIRS = HEADS // 2
PW = 2 * HEAD
ROW = FT * FW

EPS_NORM = 1e-05
EPS_HEAD = 1e-06

F32 = jnp.float32
BF16 = jnp.bfloat16
VMEM = pltpu.VMEM
SMEM = pltpu.SMEM


def dot(a, b):
    return jnp.dot(a, b, preferred_element_type=F32)


def dot_nt(a, b):
    return lax.dot_general(a, b, (((1,), (1,)), ((), ())), preferred_element_type=F32)


def normalize_rows(features):
    average = jnp.mean(features, axis=-1, keepdims=True)
    centred = features - average
    inverse = lax.rsqrt(jnp.mean(centred * centred, axis=-1, keepdims=True) + EPS_NORM)
    return centred * inverse, inverse


def first_half(shape):
    return lax.broadcasted_iota(jnp.int32, shape, 1) < HEAD


def pair_sums(values, first):
    low = jnp.sum(jnp.where(first, values, 0.0), axis=-1, keepdims=True)
    high = jnp.sum(jnp.where(first, 0.0, values), axis=-1, keepdims=True)
    return jnp.where(first, low, high)


def pair_unit(values, first):
    inverse = lax.rsqrt(pair_sums(values * values, first) + EPS_HEAD)
    return values * inverse, inverse


def pair_unit_back(unit, inverse, gradient, first):
    return inverse * (gradient - unit * pair_sums(unit * gradient, first))


def pool_lanes(ext_ref, taps, flip):
    column = lax.broadcasted_iota(jnp.int32, (FW, 128), 0)
    blocks = []
    for row in range(2):
        for frame in range(FT):
            parts = [None, None, None]
            for dr in range(3):
                for df in range(3):
                    source = frame + df - 1
                    if source < 0 or source >= FT:
                        continue
                    start = (row + dr) * ROW + source * FW
                    block = ext_ref[start : start + FW, :]
                    for dc in range(3):
                        tap = dr * 9 + df * 3 + dc
                        term = taps[26 - tap if flip else tap] * block
                        parts[dc] = term if parts[dc] is None else parts[dc] + term
            left = jnp.where(column == 0, 0.0, pltpu.roll(parts[0], 1, 0))
            right = jnp.where(column == FW - 1, 0.0, pltpu.roll(parts[2], FW - 1, 0))
            blocks.append(parts[1] + left + right)
    return jnp.concatenate(blocks, axis=0)


def load_taps(kern_ref, lanes):
    return [jnp.broadcast_to(kern_ref[t : t + 1, lanes], (FW, 128)) for t in range(27)]


def project_kernel(a_ref, w_ref, out_ref):
    normalized, _ = normalize_rows(a_ref[...].astype(F32))
    low = normalized.astype(BF16)
    for c in range(0, w_ref.shape[1], 256):
        out_ref[:, c : c + 256] = dot(low, w_ref[:, c : c + 256]).astype(BF16)


def pool_kernel(prev_ref, next_ref, w_ref, proj_ref, kern_ref, kv_ref, pk_ref, ext_ref):
    hidden = pk_ref.shape[1]
    halo = jnp.concatenate([prev_ref[...], next_ref[...]], axis=0).astype(F32)
    low = normalize_rows(halo)[0].astype(BF16)
    first = first_half((128, 128))
    for c in range(0, 2 * hidden, 256):
        outer = dot(low, w_ref[:, hidden + c : hidden + c + 256]).astype(BF16).astype(F32)
        for j in (0, 128):
            at = c + j
            ext_ref[0:ROW, :] = outer[:ROW, j : j + 128]
            ext_ref[ROW : ROW + 128, :] = proj_ref[:, hidden + at : hidden + at + 128].astype(F32)
            ext_ref[ROW + 128 :, :] = outer[ROW:, j : j + 128]
            pooled = pool_lanes(ext_ref, load_taps(kern_ref, slice(at, at + 128)), False).astype(BF16)
            if at < hidden:
                pk_ref[:, at : at + 128] = pooled
                kv_ref[:, at : at + 128] = pair_unit(pooled.astype(F32), first)[0].astype(BF16)
            else:
                kv_ref[:, at : at + 128] = pooled


def attention_kernel(
    flags_ref, tau_ref, proj_ref, own_ref, prev_ref, next_ref, gb_ref, wout_ref,
    att_ref, gq_ref, part_own_ref, part_near_ref,
):
    hidden = att_ref.shape[1]
    from_prev = flags_ref[0] == 1
    first = first_half((128, 128))
    first_low = first_half((256, 128))
    gb = gb_ref[...]

    def both(at):
        near = jnp.where(from_prev, prev_ref[:, at : at + PW], next_ref[:, at : at + PW])
        return jnp.concatenate([own_ref[:, at : at + PW], near], axis=0)

    def masked(rows):
        zero = jnp.zeros_like(rows)
        return jnp.concatenate(
            [jnp.where(first_low, rows, zero), jnp.where(first_low, zero, rows)], axis=0
        )

    for p in range(PAIRS):
        at = p * PW
        g2 = dot_nt(gb, wout_ref[at : at + PW, :]).astype(BF16)
        q_unit, q_inverse = pair_unit(proj_ref[:, at : at + PW].astype(F32), first)
        q_low = q_unit.astype(BF16)
        keys = masked(both(at))
        values = masked(both(hidden + at))
        scores = dot_nt(q_low, keys)
        grad_probs = dot_nt(g2, values)
        probs, grads = [], []
        for half in range(2):
            scale = tau_ref[2 * p + half]
            cut = slice(half * 256, half * 256 + 256)
            exponent = jnp.exp(scores[:, cut] * scale)
            prob = exponent * (1.0 / jnp.sum(exponent, axis=-1, keepdims=True))
            gp = grad_probs[:, cut]
            delta = jnp.sum(prob * gp, axis=-1, keepdims=True)
            probs.append(prob.astype(BF16))
            grads.append((scale * prob * (gp - delta)).astype(BF16))
        prob_low = jnp.concatenate(probs, axis=1)
        grad_scores = jnp.concatenate(grads, axis=1)
        att_ref[:, at : at + PW] = dot(prob_low, values).astype(BF16)
        grad_q = dot(grad_scores, keys)
        gq_ref[:, at : at + PW] = pair_unit_back(q_unit, q_inverse, grad_q, first).astype(BF16)
        grad_k = dot(grad_scores.T, q_low)
        grad_v = dot(prob_low.T, g2)
        grad_k = jnp.where(first_low, grad_k[:256], grad_k[256:]).astype(BF16)
        grad_v = jnp.where(first_low, grad_v[:256], grad_v[256:]).astype(BF16)
        part_own_ref[:, at : at + PW] = grad_k[:128]
        part_near_ref[:, at : at + PW] = grad_k[128:]
        part_own_ref[:, hidden + at : hidden + at + PW] = grad_v[:128]
        part_near_ref[:, hidden + at : hidden + at + PW] = grad_v[128:]


def output_kernel(att_ref, wout_ref, b_ref, out_ref):
    att = att_ref[...]
    for c in range(0, out_ref.shape[1], 256):
        cut = slice(c, c + 256)
        out_ref[:, cut] = (b_ref[:, cut].astype(F32) - dot(att, wout_ref[:, cut])).astype(BF16)


def key_kernel(flags_ref, own_ref, prev_ref, next_ref, pk_ref, out_ref):
    hidden = pk_ref.shape[1]
    first = first_half((128, 128))
    use_prev = flags_ref[1] == 1
    use_next = flags_ref[2] == 1
    for at in range(0, 2 * hidden, 128):
        cut = slice(at, at + 128)
        total = own_ref[:, cut].astype(F32)
        total = total + jnp.where(use_prev, prev_ref[:, cut].astype(F32), 0.0)
        total = total + jnp.where(use_next, next_ref[:, cut].astype(F32), 0.0)
        if at < hidden:
            unit, inverse = pair_unit(pk_ref[:, cut].astype(F32), first)
            total = pair_unit_back(unit, inverse, total, first)
        out_ref[:, cut] = total.astype(BF16)


def final_kernel(
    prev_ref, own_ref, next_ref, gq_ref, w_ref, kern_ref, a_ref, ga_ref, out_ref, ext_ref, gp_ref, acc_ref
):
    hidden = gq_ref.shape[1]
    width = a_ref.shape[1]
    gp_ref[:, :hidden] = gq_ref[...]
    for at in range(0, 2 * hidden, 128):
        cut = slice(at, at + 128)
        ext_ref[0:ROW, :] = prev_ref[:, cut].astype(F32)
        ext_ref[ROW : ROW + 128, :] = own_ref[:, cut].astype(F32)
        ext_ref[ROW + 128 :, :] = next_ref[:, cut].astype(F32)
        pooled = pool_lanes(ext_ref, load_taps(kern_ref, cut), True)
        gp_ref[:, hidden + at : hidden + at + 128] = pooled.astype(BF16)
    grad_proj = gp_ref[...]
    for c in range(0, width, 256):
        acc_ref[:, c : c + 256] = dot_nt(grad_proj, w_ref[c : c + 256, :])
    normalized, inverse = normalize_rows(a_ref[...].astype(F32))
    grad = acc_ref[...]
    grad_mean = jnp.mean(grad, axis=-1, keepdims=True)
    cross_mean = jnp.mean(grad * normalized, axis=-1, keepdims=True)
    back = inverse * (grad - grad_mean - normalized * cross_mean)
    out_ref[...] = (ga_ref[...].astype(F32) + back).astype(BF16)


def call(kernel, name, outs, specs, flops, scratch=()):
    def run(*args):
        moved = sum(x.size * x.dtype.itemsize for x in args)
        return pl.pallas_call(
            kernel,
            name=name,
            out_shape=[jax.ShapeDtypeStruct(s, BF16) for s in outs],
            in_specs=[pl.BlockSpec(memory_space=s) for s in specs],
            out_specs=[pl.BlockSpec(memory_space=VMEM) for _ in outs],
            scratch_shapes=list(scratch),
            compiler_params=pltpu.CompilerParams(vmem_limit_bytes=40 * 1024 * 1024),
            cost_estimate=pl.CostEstimate(flops=flops, bytes_accessed=moved, transcendentals=0),
        )(*args)

    return run


def pass_on(value, by):
    count = lax.axis_size("space")
    pairs = [(i, i + by) for i in range(count) if 0 <= i + by < count]
    return lax.ppermute(value, "space", pairs)


def shift(value):
    count = lax.axis_size("section")
    return lax.ppermute(value, "section", [(i, (i - 1) % count) for i in range(count)])


def layer(state, w_qkv, w_out, kern, tau, flags):
    a, b, ga, gb = state
    block, width = a.shape
    hidden = w_out.shape[0]
    a_prev = pass_on(a[block - ROW :], 1)
    a_next = pass_on(a[:ROW], -1)
    (proj,) = call(
        project_kernel, "project", [(block, 3 * hidden)], [VMEM] * 2, 2 * block * width * 3 * hidden
    )(a, w_qkv)
    kv, pk = call(
        pool_kernel, "pool", [(block, 2 * hidden), (block, hidden)], [VMEM] * 5,
        2 * block * width * 2 * hidden, [pltpu.VMEM((256, 128), F32)],
    )(a_prev, a_next, w_qkv, proj, kern)
    kv_prev = pass_on(kv, 1)
    kv_next = pass_on(kv, -1)
    att, gq, part_own, part_near = call(
        attention_kernel, "attention",
        [(block, hidden), (block, hidden), (block, 2 * hidden), (block, 2 * hidden)],
        [SMEM] * 2 + [VMEM] * 6, 2 * block * width * hidden * 3,
    )(flags, tau, proj, kv, kv_prev, kv_next, gb, w_out)
    part_prev = pass_on(part_near, 1)
    part_next = pass_on(part_near, -1)
    (rebuilt,) = call(
        output_kernel, "output", [(block, width)], [VMEM] * 3, 2 * block * width * hidden
    )(att, w_out, b)
    (gpool,) = call(key_kernel, "keys", [(block, 2 * hidden)], [SMEM] + [VMEM] * 4, block * width * 40)(
        flags, part_own, part_prev, part_next, pk
    )
    g_prev = pass_on(gpool[block - ROW :], 1)
    g_next = pass_on(gpool[:ROW], -1)
    (new_grad,) = call(
        final_kernel, "final", [(block, width)], [VMEM] * 8, 2 * block * width * 3 * hidden,
        [
            pltpu.VMEM((256, 128), F32),
            pltpu.VMEM((block, 3 * hidden), BF16),
            pltpu.VMEM((block, width), F32),
        ],
    )(g_prev, gpool, g_next, gq, w_qkv, kern, a, ga)
    return rebuilt, a, gb, new_grad


def tile_flags(block_owner):
    tile = lax.axis_index("space")
    count = lax.axis_size("space")
    ids = jnp.arange(count, dtype=jnp.int32)
    lists_prev = jnp.any(block_owner == (ids - 1)[:, None], axis=1).astype(jnp.int32)
    lists_next = jnp.any(block_owner == (ids + 1)[:, None], axis=1).astype(jnp.int32)
    take = lambda v, i: jnp.sum(jnp.where(ids == i, v, 0))
    return jnp.stack([take(lists_prev, tile), take(lists_next, tile - 1), take(lists_prev, tile + 1)])


def body(top_a, top_b, grad_a, grad_b, w_qkv, w_out, kernel, tau, block_owner):
    flags = tile_flags(block_owner)
    state = (top_a[0], top_b[0], grad_a[0], grad_b[0])
    for _ in range(STEPS):
        result = layer(state, w_qkv[0], w_out[0], kernel[0], tau[0], flags)
        state = tuple(shift(member) for member in result)
    return tuple(member[None] for member in state)


def solution(mesh):
    state = P("section", "space", None)
    weights = P("section", None, None)
    return jax.shard_map(
        body,
        mesh=mesh,
        in_specs=(state,) * 4 + (weights,) * 3 + (P("section", None), P()),
        out_specs=(state,) * 4,
        check_vma=False,
    )
```

profile of v0, /device:TPU:11, one launch (start us, length us, event | category | flops | bytes accessed | tf_op | source)
XLA Modules:
  0.0 222.8 jit_solution(11786907477312778666)
XLA Ops:
  0.6 1.1 slice_bitcast_fusion
  1.7 3.6 %collective-permute-start = (bf16[64,1536]{1,0:T(8,128)(2,1)S(1)}, bf16[64,1536]{1,0:T(8,128)(2,1)S(1)}, u32[]{:S(2)}, u32[]{:S(2)}) collective-permute-start(bf16[64,1536]{1,0:T(8,128)(2,1)S(1)} %get-tuple-element.39), channel_id=1, source_target_pairs={{0,1},{1,2},{2,3},{3,4},{4,5},{5,6},{6,7},{7,8},{8,9},{9,10},{10,1... | collective-permute-start | bytes 589832 | tf_op jit(solution)/shard_map/ppermute | solution.py:237
  5.3 1.9 collective-permute-start.1
  7.2 0.9 copy.15
  8.1 0.0 copy-start.5
  8.1 3.1 %copy-done = bf16[1,1536,2304]{2,1,0:T(8,128)(2,1)S(1)} copy-done((bf16[1,1536,2304]{2,1,0:T(8,128)(2,1)S(1)}, bf16[1,1536,2304]{2,1,0:T(8,128)(2,1)}, u32[]{:S(2)}) %copy-start) | copy-done | bytes 7077912
  11.2 1.0 copy-done.7
  12.2 1.3 project.2.proj_ref
  13.6 1.6 copy-done.1
  15.2 3.0 %pool.2 = (bf16[128,1536]{1,0:T(8,128)(2,1)}, bf16[128,768]{1,0:T(8,128)(2,1)S(1)}) custom-call(bf16[64,1536]{1,0:T(8,128)(2,1)S(1)} %collective-permute-done.prev_ref, bf16[64,1536]{1,0:T(8,128)(2,1)S(1)} %collective-permute-done.1.next_ref, bf16[1536,2304]{1,0:T(8,128)(2,1)S(1)} %bitcast.22, bf16[128,2304]{1,0:T(8,128)(2,1)S(1)} %project.2.proj_ref, ...), custom_call_target="tpu_custom_call" | custom-call | flops 603979776 | bytes 8226816 | tf_op jit(solution)/shard_map/pool/pallas_call | solution.py:220
  18.2 0.7 copy-done.13
  18.9 4.5 %collective-permute-start.2 = (bf16[128,1536]{1,0:T(8,128)(2,1)}, bf16[128,1536]{1,0:T(8,128)(2,1)}, u32[]{:S(2)}, u32[]{:S(2)}) collective-permute-start(bf16[128,1536]{1,0:T(8,128)(2,1)} %get-tuple-element.16.own_ref), channel_id=1, source_target_pairs={{0,1},{1,2},{2,3},{3,4},{4,5},{5,6},{6,7},{7,8},{8,9},{9,10},{10,1... | collective-permute-start | bytes 1179656 | tf_op jit(solution)/shard_map/ppermute | solution.py:237
  23.5 1.9 collective-permute-start.3
  25.4 0.7 fusion
  26.1 2.0 pad_add_fusion.flags_ref
  28.1 0.4 collective-permute-done.2.prev_ref
  28.5 5.3 %collective-permute-done.3.next_ref = bf16[128,1536]{1,0:T(8,128)(2,1)} collective-permute-done((bf16[128,1536]{1,0:T(8,128)(2,1)}, bf16[128,1536]{1,0:T(8,128)(2,1)}, u32[]{:S(2)}, u32[]{:S(2)}) %collective-permute-start.3) | collective-permute-done | bytes 393248 | tf_op jit(solution)/shard_map/ppermute | solution.py:237
  33.8 1.7 copy-done.2
  35.4 1.0 copy-done.11
  36.4 5.5 %attention.2 = (bf16[128,768]{1,0:T(8,128)(2,1)S(1)}, bf16[128,768]{1,0:T(8,128)(2,1)S(1)}, bf16[128,1536]{1,0:T(8,128)(2,1)S(1)}, bf16[128,1536]{1,0:T(8,128)(2,1)S(1)}) custom-call(s32[3]{0:T(128)S(1)} %pad_add_fusion.flags_ref, f32[12]{0:T(128)S(1)} %bitcast.44, bf16[128,2304]{1,0:T(8,128)(2,1)S(1)} %project.2.proj_ref, ...), custom_call_target="tpu_custom_call" | custom-call | flops 905969664 | bytes 4522044 | tf_op jit(solution)/shard_map/attention/pallas_call | solution.py:220
  41.9 1.9 collective-permute-start.10
  43.8 4.5 %collective-permute-start.9 = (bf16[128,1536]{1,0:T(8,128)(2,1)S(1)}, bf16[128,1536]{1,0:T(8,128)(2,1)S(1)}, u32[]{:S(2)}, u32[]{:S(2)}) collective-permute-start(bf16[128,1536]{1,0:T(8,128)(2,1)S(1)} %get-tuple-element.20), channel_id=1, source_target_pairs={{0,1},{1,2},{2,3},{3,4},{4,5},{5,6},{6,7},{7,8},{8,9},{9,10},{10,1... | collective-permute-start | bytes 1179656 | tf_op jit(solution)/shard_map/ppermute | solution.py:237
  48.4 1.7 copy-done.3
  50.0 1.0 copy-done.10
  51.0 0.5 output.2
  51.5 7.7 %collective-permute-start.4 = (bf16[128,1536]{1,0:T(8,128)(2,1)S(1)}, bf16[128,1536]{1,0:T(8,128)(2,1)S(1)}, u32[]{:S(2)}, u32[]{:S(2)}) collective-permute-start(bf16[128,1536]{1,0:T(8,128)(2,1)S(1)} %output.2), channel_id=1, source_target_pairs={{0,240},{16,0},{32,16},{48,32},{64,48},{80,64},{96,80},{112,96},{1... | collective-permute-start | bytes 1179656 | tf_op jit(solution)/shard_map/ppermute | solution.py:242
  59.2 1.4 keys.2.own_ref
  60.7 2.8 %collective-permute-start.11 = (bf16[64,1536]{1,0:T(8,128)(2,1)S(1)}, bf16[64,1536]{1,0:T(8,128)(2,1)S(1)}, u32[]{:S(2)}, u32[]{:S(2)}) collective-permute-start(bf16[64,1536]{1,0:T(8,128)(2,1)S(1)} %get-tuple-element.35), channel_id=1, source_target_pairs={{0,1},{1,2},{2,3},{3,4},{4,5},{5,6},{6,7},{7,8},{8,9},{9,10},{10,1... | collective-permute-start | bytes 589832 | tf_op jit(solution)/shard_map/ppermute | solution.py:237
  63.5 1.9 collective-permute-start.12
  65.4 2.9 %collective-permute-done.4.a_ref = bf16[128,1536]{1,0:T(8,128)(2,1)S(1)} collective-permute-done((bf16[128,1536]{1,0:T(8,128)(2,1)S(1)}, bf16[128,1536]{1,0:T(8,128)(2,1)S(1)}, u32[]{:S(2)}, u32[]{:S(2)}) %collective-permute-start.4) | collective-permute-done | bytes 393248 | tf_op jit(solution)/shard_map/ppermute | solution.py:242
  68.3 3.0 %collective-permute-start.5 = (bf16[64,1536]{1,0:T(8,128)(2,1)S(1)}, bf16[64,1536]{1,0:T(8,128)(2,1)S(1)}, u32[]{:S(2)}, u32[]{:S(2)}) collective-permute-start(bf16[64,1536]{1,0:T(8,128)(2,1)S(1)} %get-tuple-element.37), channel_id=1, source_target_pairs={{0,1},{1,2},{2,3},{3,4},{4,5},{5,6},{6,7},{7,8},{8,9},{9,10},{10,1... | collective-permute-start | bytes 589832 | tf_op jit(solution)/shard_map/ppermute | solution.py:237
  71.4 2.1 collective-permute-start.6
  73.5 1.3 project.3.proj_ref
  74.9 3.7 %final.2 = bf16[128,1536]{1,0:T(8,128)(2,1)S(1)} custom-call(bf16[64,1536]{1,0:T(8,128)(2,1)S(1)} %collective-permute-done.11.prev_ref, bf16[128,1536]{1,0:T(8,128)(2,1)S(1)} %keys.2.own_ref, bf16[64,1536]{1,0:T(8,128)(2,1)S(1)} %collective-permute-done.12.next_ref, bf16[128,768]{1,0:T(8,128)(2,1)S(1)} %get-tuple-element.22.gq_ref, ...), custom_call_target="tpu_custom_call" | custom-call | flops 905969664 | bytes 9013248 | tf_op jit(solution)/shard_map/final/pallas_call | solution.py:220
  78.6 11.4 %collective-permute-start.13 = (bf16[128,1536]{1,0:T(8,128)(2,1)S(1)}, bf16[128,1536]{1,0:T(8,128)(2,1)S(1)}, u32[]{:S(2)}, u32[]{:S(2)}) collective-permute-start(bf16[128,1536]{1,0:T(8,128)(2,1)S(1)} %final.2), channel_id=1, source_target_pairs={{0,240},{16,0},{32,16},{48,32},{64,48},{80,64},{96,80},{112,96},{1... | collective-permute-start | bytes 1179656 | tf_op jit(solution)/shard_map/ppermute | solution.py:242
  90.0 2.3 %pool.3 = (bf16[128,1536]{1,0:T(8,128)(2,1)S(1)}, bf16[128,768]{1,0:T(8,128)(2,1)S(1)}) custom-call(bf16[64,1536]{1,0:T(8,128)(2,1)S(1)} %collective-permute-done.5.prev_ref, bf16[64,1536]{1,0:T(8,128)(2,1)S(1)} %collective-permute-done.6.next_ref, bf16[1536,2304]{1,0:T(8,128)(2,1)S(1)} %bitcast.27, bf16[128,2304]{1,0:T(8,128)(2,1)S(1)} %project.3.proj_ref, ...), custom_call_target="tpu_custom_call" | custom-call | flops 603979776 | bytes 8226816 | tf_op jit(solution)/shard_map/pool/pallas_call | solution.py:220
  92.4 5.4 %collective-permute-start.7 = (bf16[128,1536]{1,0:T(8,128)(2,1)S(1)}, bf16[128,1536]{1,0:T(8,128)(2,1)S(1)}, u32[]{:S(2)}, u32[]{:S(2)}) collective-permute-start(bf16[128,1536]{1,0:T(8,128)(2,1)S(1)} %get-tuple-element.18.own_ref), channel_id=1, source_target_pairs={{0,1},{1,2},{2,3},{3,4},{4,5},{5,6},{6,7},{7,8},{8,9},{9,10},{10,1... | collective-permute-start | bytes 1179656 | tf_op jit(solution)/shard_map/ppermute | solution.py:237
  97.8 1.9 collective-permute-start.8
  99.7 1.3 collective-permute-done.13.gb_ref
  101.1 1.5 collective-permute-done.7.prev_ref
  102.6 5.3 %collective-permute-done.8.next_ref = bf16[128,1536]{1,0:T(8,128)(2,1)S(1)} collective-permute-done((bf16[128,1536]{1,0:T(8,128)(2,1)S(1)}, bf16[128,1536]{1,0:T(8,128)(2,1)S(1)}, u32[]{:S(2)}, u32[]{:S(2)}) %collective-permute-start.8) | collective-permute-done | bytes 393248 | tf_op jit(solution)/shard_map/ppermute | solution.py:237
  107.8 4.6 %attention.3 = (bf16[128,768]{1,0:T(8,128)(2,1)S(1)}, bf16[128,768]{1,0:T(8,128)(2,1)S(1)}, bf16[128,1536]{1,0:T(8,128)(2,1)S(1)}, bf16[128,1536]{1,0:T(8,128)(2,1)S(1)}) custom-call(s32[3]{0:T(128)S(1)} %pad_add_fusion.flags_ref, f32[12]{0:T(128)S(1)} %bitcast.45, bf16[128,2304]{1,0:T(8,128)(2,1)S(1)} %project.3.proj_ref, ...), custom_call_target="tpu_custom_call" | custom-call | flops 905969664 | bytes 4522044 | tf_op jit(solution)/shard_map/attention/pallas_call | solution.py:220
  112.4 1.9 collective-permute-start.18
  114.4 2.4 %collective-permute-start.19 = (bf16[128,1536]{1,0:T(8,128)(2,1)S(1)}, bf16[128,1536]{1,0:T(8,128)(2,1)S(1)}, u32[]{:S(2)}, u32[]{:S(2)}) collective-permute-start(bf16[128,1536]{1,0:T(8,128)(2,1)S(1)} %get-tuple-element.25), channel_id=1, source_target_pairs={{1,0},{2,1},{3,2},{4,3},{5,4},{6,5},{7,6},{8,7},{9,8},{10,9},{11,1... | collective-permute-start | bytes 1179656 | tf_op jit(solution)/shard_map/ppermute | solution.py:237
  116.8 4.3 %collective-permute-start.22 = (bf16[128,1536]{1,0:T(8,128)(2,1)S(1)}, bf16[128,1536]{1,0:T(8,128)(2,1)S(1)}, u32[]{:S(2)}, u32[]{:S(2)}) collective-permute-start(bf16[128,1536]{1,0:T(8,128)(2,1)S(1)} %bitcast.43), channel_id=1, source_target_pairs={{0,240},{16,0},{32,16},{48,32},{64,48},{80,64},{96,80},{112,96},{1... | collective-permute-start | bytes 1179656 | tf_op jit(solution)/shard_map/ppermute | solution.py:242
  121.1 0.3 collective-permute-start.14
  121.4 3.0 %collective-permute-done.19.next_ref = bf16[128,1536]{1,0:T(8,128)(2,1)S(1)} collective-permute-done((bf16[128,1536]{1,0:T(8,128)(2,1)S(1)}, bf16[128,1536]{1,0:T(8,128)(2,1)S(1)}, u32[]{:S(2)}, u32[]{:S(2)}) %collective-permute-start.19) | collective-permute-done | bytes 393248 | tf_op jit(solution)/shard_map/ppermute | solution.py:237
  124.5 1.4 keys.3.own_ref
  125.9 1.9 collective-permute-start.20
  127.9 2.7 %collective-permute-start.21 = (bf16[64,1536]{1,0:T(8,128)(2,1)S(1)}, bf16[64,1536]{1,0:T(8,128)(2,1)S(1)}, u32[]{:S(2)}, u32[]{:S(2)}) collective-permute-start(bf16[64,1536]{1,0:T(8,128)(2,1)S(1)} %get-tuple-element.32), channel_id=1, source_target_pairs={{1,0},{2,1},{3,2},{4,3},{5,4},{6,5},{7,6},{8,7},{9,8},{10,9},{11,1... | collective-permute-start | bytes 589832 | tf_op jit(solution)/shard_map/ppermute | solution.py:237
  130.5 57.3 %collective-permute-start.16 = (bf16[128,1536]{1,0:T(8,128)(2,1)S(1)}, bf16[128,1536]{1,0:T(8,128)(2,1)S(1)}, u32[]{:S(2)}, u32[]{:S(2)}) collective-permute-start(bf16[128,1536]{1,0:T(8,128)(2,1)S(1)} %collective-permute-done.4.a_ref), channel_id=1, source_target_pairs={{0,240},{16,0},{32,16},{48,32},{64,48},{80,64},{96,80},{112,96},{1... | collective-permute-start | bytes 1179656 | tf_op jit(solution)/shard_map/ppermute | solution.py:242
  187.9 0.5 output.3
  188.4 0.1 collective-permute-start.15
  188.5 0.1 collective-permute-start.17
  188.6 3.7 %final.3 = bf16[128,1536]{1,0:T(8,128)(2,1)S(1)} custom-call(bf16[64,1536]{1,0:T(8,128)(2,1)S(1)} %collective-permute-done.20.prev_ref, bf16[128,1536]{1,0:T(8,128)(2,1)S(1)} %keys.3.own_ref, bf16[64,1536]{1,0:T(8,128)(2,1)S(1)} %collective-permute-done.21.next_ref, bf16[128,768]{1,0:T(8,128)(2,1)S(1)} %get-tuple-element.27.gq_ref, ...), custom_call_target="tpu_custom_call" | custom-call | flops 905969664 | bytes 9013248 | tf_op jit(solution)/shard_map/final/pallas_call | solution.py:220
  192.3 0.3 collective-permute-start.23
  192.6 2.0 collective-permute-done.16
  194.6 8.4 %collective-permute-done.15 = bf16[128,1536]{1,0:T(8,128)(2,1)S(1)} collective-permute-done((bf16[128,1536]{1,0:T(8,128)(2,1)S(1)}, bf16[128,1536]{1,0:T(8,128)(2,1)S(1)}, u32[]{:S(2)}, u32[]{:S(2)}) %collective-permute-start.15) | collective-permute-done | bytes 393248 | tf_op jit(solution)/shard_map/ppermute | solution.py:242
  203.0 8.4 %collective-permute-done.17 = bf16[128,1536]{1,0:T(8,128)(2,1)S(1)} collective-permute-done((bf16[128,1536]{1,0:T(8,128)(2,1)S(1)}, bf16[128,1536]{1,0:T(8,128)(2,1)S(1)}, u32[]{:S(2)}, u32[]{:S(2)}) %collective-permute-start.17) | collective-permute-done | bytes 393248 | tf_op jit(solution)/shard_map/ppermute | solution.py:242
  211.4 8.4 %collective-permute-done.23 = bf16[128,1536]{1,0:T(8,128)(2,1)S(1)} collective-permute-done((bf16[128,1536]{1,0:T(8,128)(2,1)S(1)}, bf16[128,1536]{1,0:T(8,128)(2,1)S(1)}, u32[]{:S(2)}, u32[]{:S(2)}) %collective-permute-start.23) | collective-permute-done | bytes 393248 | tf_op jit(solution)/shard_map/ppermute | solution.py:242
  219.8 0.7 copy.20
  220.6 0.7 copy.21
  221.3 0.7 copy.22
  222.1 0.7 copy.23
  (49 shorter events, 0.2 us)
Async XLA Ops:
  1.7 11.9 %collective-permute-start = (bf16[64,1536]{1,0:T(8,128)(2,1)S(1)}, bf16[64,1536]{1,0:T(8,128)(2,1)S(1)}, u32[]{:S(2)}, u32[]{:S(2)}) collective-permute-start(bf16[64,1536]{1,0:T(8,128)(2,1)S(1)} %get-tuple-element.39), channel_id=1, source_target_pairs={{0,1},{1,2},{2,3},{3,4},{4,5},{5,6},{6,7},{7,8},{8,9},{9,10},{10,1... | collective-permute-start | bytes 589832 | tf_op jit(solution)/shard_map/ppermute | solution.py:237
  5.3 8.3 %collective-permute-start.1 = (bf16[64,1536]{1,0:T(8,128)(2,1)S(1)}, bf16[64,1536]{1,0:T(8,128)(2,1)S(1)}, u32[]{:S(2)}, u32[]{:S(2)}) collective-permute-start(bf16[64,1536]{1,0:T(8,128)(2,1)S(1)} %get-tuple-element.38), channel_id=1, source_target_pairs={{1,0},{2,1},{3,2},{4,3},{5,4},{6,5},{7,6},{8,7},{9,8},{10,9},{11,1... | collective-permute-start | bytes 589832 | tf_op jit(solution)/shard_map/ppermute | solution.py:237
  8.1 10.1 %copy-start.5 = (f32[1,27,1536]{2,1,0:T(8,128)}, f32[1,27,1536]{2,1,0:T(8,128)S(1)}, u32[]{:S(2)}) copy-start(f32[1,27,1536]{2,1,0:T(8,128)S(1)} %copy.15) | copy-start | bytes 497668
  8.1 3.1 %copy-start = (bf16[1,1536,2304]{2,1,0:T(8,128)(2,1)S(1)}, bf16[1,1536,2304]{2,1,0:T(8,128)(2,1)}, u32[]{:S(2)}) copy-start(bf16[1,1536,2304]{2,1,0:T(8,128)(2,1)} %param.13) | copy-start | bytes 21233668
  11.2 1.0 copy-start.7
  12.2 3.0 %copy-start.1 = (bf16[1,1536,2304]{2,1,0:T(8,128)(2,1)S(1)}, bf16[1,1536,2304]{2,1,0:T(8,128)(2,1)}, u32[]{:S(2)}) copy-start(bf16[1,1536,2304]{2,1,0:T(8,128)(2,1)} %param.13) | copy-start | bytes 21233668
  12.2 13.2 %copy-start.16 = (s32[16,2]{0,1:T(2,128)S(1)}, s32[16,2]{0,1:T(2,128)}, u32[]{:S(2)}) copy-start(s32[16,2]{0,1:T(2,128)} %param.17) | copy-start | bytes 388
  12.2 21.5 %copy-start.15 = (f32[1,12]{1,0:T(1,128)S(1)}, f32[1,12]{1,0:T(1,128)}, u32[]{:S(2)}) copy-start(f32[1,12]{1,0:T(1,128)} %param.16) | copy-start | bytes 148
  15.2 58.3 %slice-start = ((s8[7077888]{0:T(1024)(128)(4,1)}), s8[2883584]{0:T(1024)(128)(4,1)S(1)}, s32[]{:S(2)}) async-start(s8[7077888]{0:T(1024)(128)(4,1)} %bitcast.23), calls=%async_computation | async-start | bytes 5767168
  18.2 0.7 copy-start.13
  18.9 9.6 %collective-permute-start.2 = (bf16[128,1536]{1,0:T(8,128)(2,1)}, bf16[128,1536]{1,0:T(8,128)(2,1)}, u32[]{:S(2)}, u32[]{:S(2)}) collective-permute-start(bf16[128,1536]{1,0:T(8,128)(2,1)} %get-tuple-element.16.own_ref), channel_id=1, source_target_pairs={{0,1},{1,2},{2,3},{3,4},{4,5},{5,6},{6,7},{7,8},{8,9},{9,10},{10,1... | collective-permute-start | bytes 1179656 | tf_op jit(solution)/shard_map/ppermute | solution.py:237
  23.5 10.3 %collective-permute-start.3 = (bf16[128,1536]{1,0:T(8,128)(2,1)}, bf16[128,1536]{1,0:T(8,128)(2,1)}, u32[]{:S(2)}, u32[]{:S(2)}) collective-permute-start(bf16[128,1536]{1,0:T(8,128)(2,1)} %get-tuple-element.16.own_ref), channel_id=1, source_target_pairs={{1,0},{2,1},{3,2},{4,3},{5,4},{6,5},{7,6},{8,7},{9,8},{10,9},{11,1... | collective-permute-start | bytes 1179656 | tf_op jit(solution)/shard_map/ppermute | solution.py:237
  33.8 1.7 copy-start.2
  35.4 1.0 copy-start.11
  36.4 22.8 %copy-start.14 = (bf16[128,768]{1,0:T(8,128)(2,1)S(1)}, bf16[128,768]{1,0:T(8,128)(2,1)}, u32[]{:S(2)}) copy-start(bf16[128,768]{1,0:T(8,128)(2,1)} %copy-done.13) | copy-start | bytes 589828
  36.4 37.1 %slice-start.1 = ((s8[7077888]{0:T(1024)(128)(4,1)}), s8[4194304]{0:T(1024)(128)(4,1)S(1)}, s32[]{:S(2)}) async-start(s8[7077888]{0:T(1024)(128)(4,1)} %bitcast.23), calls=%async_computation.1 | async-start | bytes 8388608
  41.9 17.3 %collective-permute-start.10 = (bf16[128,1536]{1,0:T(8,128)(2,1)S(1)}, bf16[128,1536]{1,0:T(8,128)(2,1)S(1)}, u32[]{:S(2)}, u32[]{:S(2)}) collective-permute-start(bf16[128,1536]{1,0:T(8,128)(2,1)S(1)} %get-tuple-element.20), channel_id=1, source_target_pairs={{1,0},{2,1},{3,2},{4,3},{5,4},{6,5},{7,6},{8,7},{9,8},{10,9},{11,1... | collective-permute-start | bytes 1179656 | tf_op jit(solution)/shard_map/ppermute | solution.py:237
  43.8 15.4 %collective-permute-start.9 = (bf16[128,1536]{1,0:T(8,128)(2,1)S(1)}, bf16[128,1536]{1,0:T(8,128)(2,1)S(1)}, u32[]{:S(2)}, u32[]{:S(2)}) collective-permute-start(bf16[128,1536]{1,0:T(8,128)(2,1)S(1)} %get-tuple-element.20), channel_id=1, source_target_pairs={{0,1},{1,2},{2,3},{3,4},{4,5},{5,6},{6,7},{7,8},{8,9},{9,10},{10,1... | collective-permute-start | bytes 1179656 | tf_op jit(solution)/shard_map/ppermute | solution.py:237
  48.4 1.7 copy-start.3
  50.0 1.0 copy-start.10
  51.0 23.8 %copy-start.6 = (f32[1,27,1536]{2,1,0:T(8,128)S(1)}, f32[1,27,1536]{2,1,0:T(8,128)}, u32[]{:S(2)}) copy-start(f32[1,27,1536]{2,1,0:T(8,128)} %copy-done.5) | copy-start | bytes 497668
  51.0 23.8 %copy-start.8 = (bf16[1,128,1536]{2,1,0:T(8,128)(2,1)S(1)}, bf16[1,128,1536]{2,1,0:T(8,128)(2,1)}, u32[]{:S(2)}) copy-start(bf16[1,128,1536]{2,1,0:T(8,128)(2,1)} %param.9) | copy-start | bytes 1179652
  51.0 23.8 %copy-start.9 = (bf16[1,128,1536]{2,1,0:T(8,128)(2,1)S(1)}, bf16[1,128,1536]{2,1,0:T(8,128)(2,1)}, u32[]{:S(2)}) copy-start(bf16[1,128,1536]{2,1,0:T(8,128)(2,1)} %param.11) | copy-start | bytes 1179652
  51.5 16.8 %collective-permute-start.4 = (bf16[128,1536]{1,0:T(8,128)(2,1)S(1)}, bf16[128,1536]{1,0:T(8,128)(2,1)S(1)}, u32[]{:S(2)}, u32[]{:S(2)}) collective-permute-start(bf16[128,1536]{1,0:T(8,128)(2,1)S(1)} %output.2), channel_id=1, source_target_pairs={{0,240},{16,0},{32,16},{48,32},{64,48},{80,64},{96,80},{112,96},{1... | collective-permute-start | bytes 1179656 | tf_op jit(solution)/shard_map/ppermute | solution.py:242
  60.7 14.1 %collective-permute-start.11 = (bf16[64,1536]{1,0:T(8,128)(2,1)S(1)}, bf16[64,1536]{1,0:T(8,128)(2,1)S(1)}, u32[]{:S(2)}, u32[]{:S(2)}) collective-permute-start(bf16[64,1536]{1,0:T(8,128)(2,1)S(1)} %get-tuple-element.35), channel_id=1, source_target_pairs={{0,1},{1,2},{2,3},{3,4},{4,5},{5,6},{6,7},{7,8},{8,9},{9,10},{10,1... | collective-permute-start | bytes 589832 | tf_op jit(solution)/shard_map/ppermute | solution.py:237
  63.5 11.3 %collective-permute-start.12 = (bf16[64,1536]{1,0:T(8,128)(2,1)S(1)}, bf16[64,1536]{1,0:T(8,128)(2,1)S(1)}, u32[]{:S(2)}, u32[]{:S(2)}) collective-permute-start(bf16[64,1536]{1,0:T(8,128)(2,1)S(1)} %get-tuple-element.34), channel_id=1, source_target_pairs={{1,0},{2,1},{3,2},{4,3},{5,4},{6,5},{7,6},{8,7},{9,8},{10,9},{11,1... | collective-permute-start | bytes 589832 | tf_op jit(solution)/shard_map/ppermute | solution.py:237
  68.3 21.7 %collective-permute-start.5 = (bf16[64,1536]{1,0:T(8,128)(2,1)S(1)}, bf16[64,1536]{1,0:T(8,128)(2,1)S(1)}, u32[]{:S(2)}, u32[]{:S(2)}) collective-permute-start(bf16[64,1536]{1,0:T(8,128)(2,1)S(1)} %get-tuple-element.37), channel_id=1, source_target_pairs={{0,1},{1,2},{2,3},{3,4},{4,5},{5,6},{6,7},{7,8},{8,9},{9,10},{10,1... | collective-permute-start | bytes 589832 | tf_op jit(solution)/shard_map/ppermute | solution.py:237
  71.4 18.7 %collective-permute-start.6 = (bf16[64,1536]{1,0:T(8,128)(2,1)S(1)}, bf16[64,1536]{1,0:T(8,128)(2,1)S(1)}, u32[]{:S(2)}, u32[]{:S(2)}) collective-permute-start(bf16[64,1536]{1,0:T(8,128)(2,1)S(1)} %get-tuple-element.36), channel_id=1, source_target_pairs={{1,0},{2,1},{3,2},{4,3},{5,4},{6,5},{7,6},{8,7},{9,8},{10,9},{11,1... | collective-permute-start | bytes 589832 | tf_op jit(solution)/shard_map/ppermute | solution.py:237
  74.9 32.9 %copy-start.4 = (bf16[1,768,1536]{2,1,0:T(8,128)(2,1)S(1)}, bf16[1,768,1536]{2,1,0:T(8,128)(2,1)}, u32[]{:S(2)}) copy-start(bf16[1,768,1536]{2,1,0:T(8,128)(2,1)} %param.14) | copy-start | bytes 7077892
  78.6 38.2 %copy-start.12 = (bf16[1,128,1536]{2,1,0:T(8,128)(2,1)S(1)}, bf16[1,128,1536]{2,1,0:T(8,128)(2,1)}, u32[]{:S(2)}) copy-start(bf16[1,128,1536]{2,1,0:T(8,128)(2,1)} %param.12) | copy-start | bytes 1179652
  78.6 22.5 %collective-permute-start.13 = (bf16[128,1536]{1,0:T(8,128)(2,1)S(1)}, bf16[128,1536]{1,0:T(8,128)(2,1)S(1)}, u32[]{:S(2)}, u32[]{:S(2)}) collective-permute-start(bf16[128,1536]{1,0:T(8,128)(2,1)S(1)} %final.2), channel_id=1, source_target_pairs={{0,240},{16,0},{32,16},{48,32},{64,48},{80,64},{96,80},{112,96},{1... | collective-permute-start | bytes 1179656 | tf_op jit(solution)/shard_map/ppermute | solution.py:242
  92.4 10.2 %collective-permute-start.7 = (bf16[128,1536]{1,0:T(8,128)(2,1)S(1)}, bf16[128,1536]{1,0:T(8,128)(2,1)S(1)}, u32[]{:S(2)}, u32[]{:S(2)}) collective-permute-start(bf16[128,1536]{1,0:T(8,128)(2,1)S(1)} %get-tuple-element.18.own_ref), channel_id=1, source_target_pairs={{0,1},{1,2},{2,3},{3,4},{4,5},{5,6},{6,7},{7,8},{8,9},{9,10},{10,1... | collective-permute-start | bytes 1179656 | tf_op jit(solution)/shard_map/ppermute | solution.py:237
  97.8 10.0 %collective-permute-start.8 = (bf16[128,1536]{1,0:T(8,128)(2,1)S(1)}, bf16[128,1536]{1,0:T(8,128)(2,1)S(1)}, u32[]{:S(2)}, u32[]{:S(2)}) collective-permute-start(bf16[128,1536]{1,0:T(8,128)(2,1)S(1)} %get-tuple-element.18.own_ref), channel_id=1, source_target_pairs={{1,0},{2,1},{3,2},{4,3},{5,4},{6,5},{7,6},{8,7},{9,8},{10,9},{11,1... | collective-permute-start | bytes 1179656 | tf_op jit(solution)/shard_map/ppermute | solution.py:237
  112.4 9.0 %collective-permute-start.18 = (bf16[128,1536]{1,0:T(8,128)(2,1)S(1)}, bf16[128,1536]{1,0:T(8,128)(2,1)S(1)}, u32[]{:S(2)}, u32[]{:S(2)}) collective-permute-start(bf16[128,1536]{1,0:T(8,128)(2,1)S(1)} %get-tuple-element.25), channel_id=1, source_target_pairs={{0,1},{1,2},{2,3},{3,4},{4,5},{5,6},{6,7},{7,8},{8,9},{9,10},{10,1... | collective-permute-start | bytes 1179656 | tf_op jit(solution)/shard_map/ppermute | solution.py:237
  114.4 10.1 %collective-permute-start.19 = (bf16[128,1536]{1,0:T(8,128)(2,1)S(1)}, bf16[128,1536]{1,0:T(8,128)(2,1)S(1)}, u32[]{:S(2)}, u32[]{:S(2)}) collective-permute-start(bf16[128,1536]{1,0:T(8,128)(2,1)S(1)} %get-tuple-element.25), channel_id=1, source_target_pairs={{1,0},{2,1},{3,2},{4,3},{5,4},{6,5},{7,6},{8,7},{9,8},{10,9},{11,1... | collective-permute-start | bytes 1179656 | tf_op jit(solution)/shard_map/ppermute | solution.py:237
  116.8 71.7 %collective-permute-start.22 = (bf16[128,1536]{1,0:T(8,128)(2,1)S(1)}, bf16[128,1536]{1,0:T(8,128)(2,1)S(1)}, u32[]{:S(2)}, u32[]{:S(2)}) collective-permute-start(bf16[128,1536]{1,0:T(8,128)(2,1)S(1)} %bitcast.43), channel_id=1, source_target_pairs={{0,240},{16,0},{32,16},{48,32},{64,48},{80,64},{96,80},{112,96},{1... | collective-permute-start | bytes 1179656 | tf_op jit(solution)/shard_map/ppermute | solution.py:242
  121.1 66.7 %collective-permute-start.14 = (bf16[128,1536]{1,0:T(8,128)(2,1)S(1)}, bf16[128,1536]{1,0:T(8,128)(2,1)S(1)}, u32[]{:S(2)}, u32[]{:S(2)}) collective-permute-start(bf16[128,1536]{1,0:T(8,128)(2,1)S(1)} %bitcast.39), channel_id=1, source_target_pairs={{0,240},{16,0},{32,16},{48,32},{64,48},{80,64},{96,80},{112,96},{1... | collective-permute-start | bytes 1179656 | tf_op jit(solution)/shard_map/ppermute | solution.py:242
  125.9 62.6 %collective-permute-start.20 = (bf16[64,1536]{1,0:T(8,128)(2,1)S(1)}, bf16[64,1536]{1,0:T(8,128)(2,1)S(1)}, u32[]{:S(2)}, u32[]{:S(2)}) collective-permute-start(bf16[64,1536]{1,0:T(8,128)(2,1)S(1)} %get-tuple-element.33), channel_id=1, source_target_pairs={{0,1},{1,2},{2,3},{3,4},{4,5},{5,6},{6,7},{7,8},{8,9},{9,10},{10,1... | collective-permute-start | bytes 589832 | tf_op jit(solution)/shard_map/ppermute | solution.py:237
  127.9 60.7 %collective-permute-start.21 = (bf16[64,1536]{1,0:T(8,128)(2,1)S(1)}, bf16[64,1536]{1,0:T(8,128)(2,1)S(1)}, u32[]{:S(2)}, u32[]{:S(2)}) collective-permute-start(bf16[64,1536]{1,0:T(8,128)(2,1)S(1)} %get-tuple-element.32), channel_id=1, source_target_pairs={{1,0},{2,1},{3,2},{4,3},{5,4},{6,5},{7,6},{8,7},{9,8},{10,9},{11,1... | collective-permute-start | bytes 589832 | tf_op jit(solution)/shard_map/ppermute | solution.py:237
  130.5 64.0 %collective-permute-start.16 = (bf16[128,1536]{1,0:T(8,128)(2,1)S(1)}, bf16[128,1536]{1,0:T(8,128)(2,1)S(1)}, u32[]{:S(2)}, u32[]{:S(2)}) collective-permute-start(bf16[128,1536]{1,0:T(8,128)(2,1)S(1)} %collective-permute-done.4.a_ref), channel_id=1, source_target_pairs={{0,240},{16,0},{32,16},{48,32},{64,48},{80,64},{96,80},{112,96},{1... | collective-permute-start | bytes 1179656 | tf_op jit(solution)/shard_map/ppermute | solution.py:242
  188.4 14.6 %collective-permute-start.15 = (bf16[128,1536]{1,0:T(8,128)(2,1)S(1)}, bf16[128,1536]{1,0:T(8,128)(2,1)S(1)}, u32[]{:S(2)}, u32[]{:S(2)}) collective-permute-start(bf16[128,1536]{1,0:T(8,128)(2,1)S(1)} %output.3), channel_id=1, source_target_pairs={{0,240},{16,0},{32,16},{48,32},{64,48},{80,64},{96,80},{112,96},{1... | collective-permute-start | bytes 1179656 | tf_op jit(solution)/shard_map/ppermute | solution.py:242
  188.5 22.9 %collective-permute-start.17 = (bf16[128,1536]{1,0:T(8,128)(2,1)S(1)}, bf16[128,1536]{1,0:T(8,128)(2,1)S(1)}, u32[]{:S(2)}, u32[]{:S(2)}) collective-permute-start(bf16[128,1536]{1,0:T(8,128)(2,1)S(1)} %collective-permute-done.13.gb_ref), channel_id=1, source_target_pairs={{0,240},{16,0},{32,16},{48,32},{64,48},{80,64},{96,80},{112,96},{1... | collective-permute-start | bytes 1179656 | tf_op jit(solution)/shard_map/ppermute | solution.py:242
  192.3 27.6 %collective-permute-start.23 = (bf16[128,1536]{1,0:T(8,128)(2,1)S(1)}, bf16[128,1536]{1,0:T(8,128)(2,1)S(1)}, u32[]{:S(2)}, u32[]{:S(2)}) collective-permute-start(bf16[128,1536]{1,0:T(8,128)(2,1)S(1)} %final.3), channel_id=1, source_target_pairs={{0,240},{16,0},{32,16},{48,32},{64,48},{80,64},{96,80},{112,96},{1... | collective-permute-start | bytes 1179656 | tf_op jit(solution)/shard_map/ppermute | solution.py:242
where the time goes:
time: 227 us; the launch traced here: 223 us
  starting transfers between devices  126 us (56%)
  waiting for transfers between devices  46.9 us (21%)
  Pallas kernels  29.2 us (13%)
  local copies, waits for them, and re-layouts  16.8 us (7%)
  other arithmetic  2.71 us (1%)
    ppermute x8, starting transfers between devices, shift(): lax.ppermute(value, 'section', [(i, (i - 1) % count) for i in range(count)])  81.7 us
    ppermute x16, starting transfers between devices, pass_on(): return lax.ppermute(value, 'space', pairs)  44.5 us
    ppermute x8, waiting for transfers between devices, shift(): lax.ppermute(value, 'section', [(i, (i - 1) % count) for i in range(count)])  31.4 us
    pallas_call x12, Pallas kernels, run(): pl.pallas_call(kernel, name=name, out_shape=[jax.ShapeDtypeStruct(s, BF16...  29.2 us
    unnamed x43, local copies, waits for them, and re-layouts  15.7 us
    ppermute x16, waiting for transfers between devices, pass_on(): return lax.ppermute(value, 'space', pairs)  15.4 us
  transfers between devices with their start and end apart: 24, of which 11 were waited for; matrix products, arithmetic and copies ran while one was open for 2% of the time, Pallas kernels for 7%

commit v1 on v0

--- a/solution.py
+++ b/solution.py
@@ -11,7 +11,6 @@
 HEAD = 64
 FT = 4
 FW = 16
-STEPS = 2
 PAIRS = HEADS // 2
 PW = 2 * HEAD
 ROW = FT * FW
@@ -93,9 +92,13 @@
         out_ref[:, c : c + 256] = dot(low, w_ref[:, c : c + 256]).astype(BF16)
 
 
-def pool_kernel(prev_ref, next_ref, w_ref, proj_ref, kern_ref, kv_ref, pk_ref, ext_ref):
+def pool_kernel(flags_ref, cross_ref, inner_ref, w_ref, proj_ref, kern_ref, kv_ref, pk_ref, ext_ref):
     hidden = pk_ref.shape[1]
-    halo = jnp.concatenate([prev_ref[...], next_ref[...]], axis=0).astype(F32)
+    odd = flags_ref[3] == 1
+    cross, inner = cross_ref[...], inner_ref[...]
+    halo = jnp.concatenate(
+        [jnp.where(odd, inner, cross), jnp.where(odd, cross, inner)], axis=0
+    ).astype(F32)
     low = normalize_rows(halo)[0].astype(BF16)
     first = first_half((128, 128))
     for c in range(0, 2 * hidden, 256):
@@ -114,17 +117,17 @@
 
 
 def attention_kernel(
-    flags_ref, tau_ref, proj_ref, own_ref, prev_ref, next_ref, gb_ref, wout_ref,
+    flags_ref, tau_ref, proj_ref, own_ref, cross_ref, inner_ref, gb_ref, wout_ref,
     att_ref, gq_ref, part_own_ref, part_near_ref,
 ):
     hidden = att_ref.shape[1]
-    from_prev = flags_ref[0] == 1
+    from_cross = flags_ref[0] == 1
     first = first_half((128, 128))
     first_low = first_half((256, 128))
     gb = gb_ref[...]
 
     def both(at):
-        near = jnp.where(from_prev, prev_ref[:, at : at + PW], next_ref[:, at : at + PW])
+        near = jnp.where(from_cross, cross_ref[:, at : at + PW], inner_ref[:, at : at + PW])
         return jnp.concatenate([own_ref[:, at : at + PW], near], axis=0)
 
     def masked(rows):
@@ -174,33 +177,40 @@
         out_ref[:, cut] = (b_ref[:, cut].astype(F32) - dot(att, wout_ref[:, cut])).astype(BF16)
 
 
-def key_kernel(flags_ref, own_ref, prev_ref, next_ref, pk_ref, out_ref):
+def key_kernel(flags_ref, own_ref, cross_ref, inner_ref, pk_ref, out_ref, cross_out_ref, inner_out_ref):
     hidden = pk_ref.shape[1]
     first = first_half((128, 128))
-    use_prev = flags_ref[1] == 1
-    use_next = flags_ref[2] == 1
+    use_cross = flags_ref[1] == 1
+    use_inner = flags_ref[2] == 1
+    odd = flags_ref[3] == 1
     for at in range(0, 2 * hidden, 128):
         cut = slice(at, at + 128)
         total = own_ref[:, cut].astype(F32)
-        total = total + jnp.where(use_prev, prev_ref[:, cut].astype(F32), 0.0)
-        total = total + jnp.where(use_next, next_ref[:, cut].astype(F32), 0.0)
+        total = total + jnp.where(use_cross, cross_ref[:, cut].astype(F32), 0.0)
+        total = total + jnp.where(use_inner, inner_ref[:, cut].astype(F32), 0.0)
         if at < hidden:
             unit, inverse = pair_unit(pk_ref[:, cut].astype(F32), first)
             total = pair_unit_back(unit, inverse, total, first)
-        out_ref[:, cut] = total.astype(BF16)
+        total = total.astype(BF16)
+        out_ref[:, cut] = total
+        cross_out_ref[:, cut] = jnp.where(odd, total[ROW:], total[:ROW])
+        inner_out_ref[:, cut] = jnp.where(odd, total[:ROW], total[ROW:])
 
 
 def final_kernel(
-    prev_ref, own_ref, next_ref, gq_ref, w_ref, kern_ref, a_ref, ga_ref, out_ref, ext_ref, gp_ref, acc_ref
+    flags_ref, cross_ref, own_ref, inner_ref, gq_ref, w_ref, kern_ref, a_ref, ga_ref,
+    out_ref, ext_ref, gp_ref, acc_ref,
 ):
+    odd = flags_ref[3] == 1
     hidden = gq_ref.shape[1]
     width = a_ref.shape[1]
     gp_ref[:, :hidden] = gq_ref[...]
     for at in range(0, 2 * hidden, 128):
         cut = slice(at, at + 128)
-        ext_ref[0:ROW, :] = prev_ref[:, cut].astype(F32)
+        cross, inner = cross_ref[:, cut], inner_ref[:, cut]
+        ext_ref[0:ROW, :] = jnp.where(odd, inner, cross).astype(F32)
         ext_ref[ROW : ROW + 128, :] = own_ref[:, cut].astype(F32)
-        ext_ref[ROW + 128 :, :] = next_ref[:, cut].astype(F32)
+        ext_ref[ROW + 128 :, :] = jnp.where(odd, cross, inner).astype(F32)
         pooled = pool_lanes(ext_ref, load_taps(kern_ref, cut), True)
         gp_ref[:, hidden + at : hidden + at + 128] = pooled.astype(BF16)
     grad_proj = gp_ref[...]
@@ -231,75 +241,188 @@
     return run
 
 
-def pass_on(value, by):
-    count = lax.axis_size("space")
-    pairs = [(i, i + by) for i in range(count) if 0 <= i + by < count]
-    return lax.ppermute(value, "space", pairs)
-
-
-def shift(value):
-    count = lax.axis_size("section")
-    return lax.ppermute(value, "section", [(i, (i - 1) % count) for i in range(count)])
-
-
-def layer(state, w_qkv, w_out, kern, tau, flags):
-    a, b, ga, gb = state
+SECTIONS = 16
+TILES = 16
+
+
+def start_layout(section, x):
+    return 0
+
+
+def first_layout(section, x):
+    return 0
+
+
+def second_layout(section, x):
+    return 1 if section in (7, 15) else 0
+
+
+def place(layout, section, tile):
+    return section * TILES + (tile ^ (2 * layout(section, tile // 4)))
+
+
+AXES = ("section", "space")
+
+
+def move(value, source, target, by):
+    pairs = [
+        (place(source, s, t), place(target, (s + by) % SECTIONS, t))
+        for s in range(SECTIONS)
+        for t in range(TILES)
+    ]
+    return lax.ppermute(value, AXES, pairs)
+
+
+def swap_cross(value, layout):
+    pairs = []
+    for s in range(SECTIONS):
+        for t in range(1, TILES - 1, 2):
+            one, two = place(layout, s, t), place(layout, s, t + 1)
+            pairs += [(one, two), (two, one)]
+    return lax.ppermute(value, AXES, pairs)
+
+
+def swap_inner(value, layout):
+    pairs = []
+    for s in range(SECTIONS):
+        for t in range(0, TILES, 2):
+            one, two = place(layout, s, t), place(layout, s, t + 1)
+            pairs += [(one, two), (two, one)]
+    return lax.ppermute(value, AXES, pairs)
+
+
+def exchange(cross, inner, layout):
+    return swap_cross(cross, layout), swap_inner(inner, layout)
+
+
+def together(*values):
+    return lax.optimization_barrier(values)
+
+
+def edges(value):
+    odd = lax.rem(lax.axis_index("space"), 2)
+    cross = lax.dynamic_slice_in_dim(value, odd * ROW, ROW, 0)
+    inner = lax.dynamic_slice_in_dim(value, (1 - odd) * ROW, ROW, 0)
+    return cross, inner
+
+
+def forward_project(a, w_qkv, layout):
+    cross, inner = exchange(*edges(a), layout)
     block, width = a.shape
+    (proj,) = call(
+        project_kernel, "project", [(block, w_qkv.shape[1])], [VMEM] * 2, 2 * block * width * w_qkv.shape[1]
+    )(a, w_qkv)
+    return proj, cross, inner
+
+
+def forward_pool(flags, proj, cross, inner, w_qkv, kern, layout):
+    block = proj.shape[0]
+    hidden = proj.shape[1] // 3
+    kv, pk = call(
+        pool_kernel, "pool", [(block, 2 * hidden), (block, hidden)], [SMEM] + [VMEM] * 5,
+        2 * block * w_qkv.shape[0] * 2 * hidden, [pltpu.VMEM((256, 128), F32)],
+    )(flags, cross, inner, w_qkv, proj, kern)
+    return kv, pk
+
+
+def attend(flags, tau, proj, kv, cross, inner, gb, w_out):
+    block, width = gb.shape
     hidden = w_out.shape[0]
-    a_prev = pass_on(a[block - ROW :], 1)
-    a_next = pass_on(a[:ROW], -1)
-    (proj,) = call(
-        project_kernel, "project", [(block, 3 * hidden)], [VMEM] * 2, 2 * block * width * 3 * hidden
-    )(a, w_qkv)
-    kv, pk = call(
-        pool_kernel, "pool", [(block, 2 * hidden), (block, hidden)], [VMEM] * 5,
-        2 * block * width * 2 * hidden, [pltpu.VMEM((256, 128), F32)],
-    )(a_prev, a_next, w_qkv, proj, kern)
-    kv_prev = pass_on(kv, 1)
-    kv_next = pass_on(kv, -1)
-    att, gq, part_own, part_near = call(
+    return call(
         attention_kernel, "attention",
         [(block, hidden), (block, hidden), (block, 2 * hidden), (block, 2 * hidden)],
         [SMEM] * 2 + [VMEM] * 6, 2 * block * width * hidden * 3,
-    )(flags, tau, proj, kv, kv_prev, kv_next, gb, w_out)
-    part_prev = pass_on(part_near, 1)
-    part_next = pass_on(part_near, -1)
-    (rebuilt,) = call(
-        output_kernel, "output", [(block, width)], [VMEM] * 3, 2 * block * width * hidden
-    )(att, w_out, b)
-    (gpool,) = call(key_kernel, "keys", [(block, 2 * hidden)], [SMEM] + [VMEM] * 4, block * width * 40)(
-        flags, part_own, part_prev, part_next, pk
-    )
-    g_prev = pass_on(gpool[block - ROW :], 1)
-    g_next = pass_on(gpool[:ROW], -1)
-    (new_grad,) = call(
-        final_kernel, "final", [(block, width)], [VMEM] * 8, 2 * block * width * 3 * hidden,
+    )(flags, tau, proj, kv, cross, inner, gb, w_out)
+
+
+def rebuild(att, w_out, b):
+    block, width = b.shape
+    return call(
+        output_kernel, "output", [(block, width)], [VMEM] * 3, 2 * block * width * w_out.shape[0]
+    )(att, w_out, b)[0]
+
+
+def key_sums(flags, own, cross, inner, pk):
+    block, channels = own.shape
+    return call(
+        key_kernel, "keys", [(block, channels), (ROW, channels), (ROW, channels)],
+        [SMEM] + [VMEM] * 4, block * channels * 40,
+    )(flags, own, cross, inner, pk)
+
+
+def finish(flags, cross, gpool, inner, gq, w_qkv, kern, a, ga):
+    block, width = a.shape
+    columns = w_qkv.shape[1]
+    return call(
+        final_kernel, "final", [(block, width)], [SMEM] + [VMEM] * 8, 2 * block * width * columns,
         [
             pltpu.VMEM((256, 128), F32),
-            pltpu.VMEM((block, 3 * hidden), BF16),
+            pltpu.VMEM((block, columns), BF16),
             pltpu.VMEM((block, width), F32),
         ],
-    )(g_prev, gpool, g_next, gq, w_qkv, kern, a, ga)
-    return rebuilt, a, gb, new_grad
-
-
-def tile_flags(block_owner):
-    tile = lax.axis_index("space")
-    count = lax.axis_size("space")
-    ids = jnp.arange(count, dtype=jnp.int32)
+    )(flags, cross, gpool, inner, gq, w_qkv, kern, a, ga)[0]
+
+
+def tile_flags(block_owner, layout):
+    section = lax.axis_index("section")
+    space = lax.axis_index("space")
+    turned = jnp.zeros((), jnp.int32)
+    for s in range(SECTIONS):
+        for x in range(4):
+            if layout(s, x):
+                turned = turned | ((section == s) & (space // 4 == x)).astype(jnp.int32)
+    tile = space ^ (2 * turned)
+    odd = lax.rem(tile, 2)
+    ids = jnp.arange(TILES, dtype=jnp.int32)
     lists_prev = jnp.any(block_owner == (ids - 1)[:, None], axis=1).astype(jnp.int32)
     lists_next = jnp.any(block_owner == (ids + 1)[:, None], axis=1).astype(jnp.int32)
     take = lambda v, i: jnp.sum(jnp.where(ids == i, v, 0))
-    return jnp.stack([take(lists_prev, tile), take(lists_next, tile - 1), take(lists_prev, tile + 1)])
+    near_prev = take(lists_prev, tile)
+    use_prev = take(lists_next, tile - 1)
+    use_next = take(lists_prev, tile + 1)
+    near_cross = jnp.where(odd == 1, 1 - near_prev, near_prev)
+    use_cross = jnp.where(odd == 1, use_next, use_prev)
+    use_inner = jnp.where(odd == 1, use_prev, use_next)
+    return jnp.stack([near_cross, use_cross, use_inner, odd])
 
 
 def body(top_a, top_b, grad_a, grad_b, w_qkv, w_out, kernel, tau, block_owner):
-    flags = tile_flags(block_owner)
-    state = (top_a[0], top_b[0], grad_a[0], grad_b[0])
-    for _ in range(STEPS):
-        result = layer(state, w_qkv[0], w_out[0], kernel[0], tau[0], flags)
-        state = tuple(shift(member) for member in result)
-    return tuple(member[None] for member in state)
+    a, b, ga, gb = top_a[0], top_b[0], grad_a[0], grad_b[0]
+    w_qkv, w_out, kern, tau = w_qkv[0], w_out[0], kernel[0], tau[0]
+    block = a.shape[0]
+    one, two, start = first_layout, second_layout, start_layout
+    flags1 = tile_flags(block_owner, one)
+    flags2 = tile_flags(block_owner, two)
+
+    proj1, cross, inner = forward_project(a, w_qkv, one)
+    b2 = move(a, one, two, -1)
+    ga2 = move(gb, one, two, -1)
+    kv1, pk1 = forward_pool(flags1, proj1, cross, inner, w_qkv, kern, one)
+    cross, inner = exchange(kv1, kv1, one)
+    cross, inner, b2, ga2 = together(cross, inner, b2, ga2)
+    att1, gq1, own1, near1 = attend(flags1, tau, proj1, kv1, cross, inner, gb, w_out)
+    cross, inner = exchange(near1, near1, one)
+    rebuilt1 = rebuild(att1, w_out, b)
+    a2 = move(rebuilt1, one, two, -1)
+    gpool1, cross, inner = key_sums(flags1, own1, cross, inner, pk1)
+    cross, inner = exchange(cross, inner, one)
+    new_grad1 = finish(flags1, cross, gpool1, inner, gq1, w_qkv, kern, a, ga)
+    gb2 = move(new_grad1, one, two, -1)
+
+    proj2, cross, inner = forward_project(a2, w_qkv, two)
+    kv2, pk2 = forward_pool(flags2, proj2, cross, inner, w_qkv, kern, two)
+    cross, inner = exchange(kv2, kv2, two)
+    rebuilt_b = move(a2, two, start, -1)
+    att2, gq2, own2, near2 = attend(flags2, tau, proj2, kv2, cross, inner, gb2, w_out)
+    cross, inner = exchange(near2, near2, two)
+    passed_a = move(gb2, two, start, -1)
+    rebuilt2 = rebuild(att2, w_out, b2)
+    rebuilt_a = move(rebuilt2, two, start, -1)
+    gpool2, cross, inner = key_sums(flags2, own2, cross, inner, pk2)
+    cross, inner = exchange(cross, inner, two)
+    new_grad2 = finish(flags2, cross, gpool2, inner, gq2, w_qkv, kern, a2, ga2)
+    passed_b = move(new_grad2, two, start, -1)
+    return rebuilt_a[None], rebuilt_b[None], passed_a[None], passed_b[None]
 
 
 def solution(mesh):

time: 227 us -> 172 us (0.76)
  the two profiles are of different devices: /device:TPU:11 before, /device:TPU:6 now
where the time goes in v1:
time: 172 us; the launch traced here: 171 us
  starting transfers between devices  87.2 us (51%)
  Pallas kernels  33.6 us (20%)
  waiting for transfers between devices  21.6 us (13%)
  local copies, waits for them, and re-layouts  18.8 us (11%)
  between operations  8.49 us (5%)
    ppermute x8, starting transfers between devices, move(): return lax.ppermute(value, AXES, pairs)  49.8 us
    pallas_call x12, Pallas kernels, run(): pl.pallas_call(kernel, name=name, out_shape=[jax.ShapeDtypeStruct(s, BF16...  33.6 us
    ppermute x8, starting transfers between devices, swap_cross(): return lax.ppermute(value, AXES, pairs)  27.2 us
    unnamed x51, local copies, waits for them, and re-layouts  16.7 us
    ppermute x8, waiting for transfers between devices, swap_cross(): return lax.ppermute(value, AXES, pairs)  12.1 us
    ppermute x8, starting transfers between devices, swap_inner(): return lax.ppermute(value, AXES, pairs)  10.2 us
    ppermute x8, waiting for transfers between devices, move(): return lax.ppermute(value, AXES, pairs)  9.49 us
  transfers between devices with their start and end apart: 24, of which 5 were waited for; matrix products, arithmetic and copies ran while one was open for 2% of the time, Pallas kernels for 13%

profile of v1, /device:TPU:6, one launch (start us, length us, event | category | flops | bytes accessed | tf_op | source)
XLA Modules:
  0.0 171.3 jit_solution(14403231684059083854)
XLA Ops:
  0.6 1.1 dynamic-slice_bitcast_fusion
  1.7 3.2 %collective-permute-start = (bf16[64,1536]{1,0:T(8,128)(2,1)S(1)}, bf16[64,1536]{1,0:T(8,128)(2,1)S(1)}, u32[]{:S(2)}, u32[]{:S(2)}) collective-permute-start(bf16[64,1536]{1,0:T(8,128)(2,1)S(1)} %get-tuple-element.59), channel_id=1, source_target_pairs={{1,2},{2,1},{3,4},{4,3},{5,6},{6,5},{7,8},{8,7},{9,10},{10,9},{11,... | collective-permute-start | bytes 589832 | tf_op jit(solution)/shard_map/ppermute | solution.py:282
  4.9 0.5 collective-permute-start.1
  5.4 6.9 %collective-permute-start.4 = (bf16[128,1536]{1,0:T(8,128)(2,1)}, bf16[128,1536]{1,0:T(8,128)(2,1)S(1)}, u32[]{:S(2)}, u32[]{:S(2)}) collective-permute-start(bf16[128,1536]{1,0:T(8,128)(2,1)} %bitcast.42), channel_id=1, source_target_pairs={{0,242},{1,243},{2,240},{3,241},{4,246},{5,247},{6,244},{7,245},{8... | collective-permute-start | bytes 1179656 | tf_op jit(solution)/shard_map/ppermute | solution.py:273
  12.3 1.0 collective-permute-start.5
  13.3 0.7 compare_reduce_fusion.1
  14.0 0.7 fusion.3
  18.6 0.9 copy.15
  19.5 0.0 copy-start
  19.5 3.0 %copy-done = bf16[1,1536,2304]{2,1,0:T(8,128)(2,1)S(1)} copy-done((bf16[1,1536,2304]{2,1,0:T(8,128)(2,1)S(1)}, bf16[1,1536,2304]{2,1,0:T(8,128)(2,1)}, u32[]{:S(2)}) %copy-start) | copy-done | bytes 7077912
  22.5 1.0 copy-done.5
  23.5 1.3 project.2.proj_ref
  24.9 0.0 copy-start.11
  24.9 0.1 pad_add_fusion.1.flags_ref
  25.0 1.6 copy-done.1
  26.5 2.9 %pool.2 = (bf16[128,1536]{1,0:T(8,128)(2,1)S(1)}, bf16[128,768]{1,0:T(8,128)(2,1)S(1)}) custom-call(s32[4]{0:T(128)S(1)} %pad_add_fusion.1.flags_ref, bf16[64,1536]{1,0:T(8,128)(2,1)S(1)} %collective-permute-done.cross_ref, bf16[64,1536]{1,0:T(8,128)(2,1)S(1)} %collective-permute-done.1.inner_ref, bf16[1536,2304]{1,0:T(8,128)(2,1)S(1)} %bitcast.27, ...), custom_call_target="tpu_custom_call" | custom-call | flops 603979776 | bytes 8226832 | tf_op jit(solution)/shard_map/pool/pallas_call | solution.py:230
  29.4 0.7 copy-done.16
  30.1 2.6 %collective-permute-start.2 = (bf16[128,1536]{1,0:T(8,128)(2,1)S(1)}, bf16[128,1536]{1,0:T(8,128)(2,1)S(1)}, u32[]{:S(2)}, u32[]{:S(2)}) collective-permute-start(bf16[128,1536]{1,0:T(8,128)(2,1)S(1)} %get-tuple-element.26.own_ref), channel_id=1, source_target_pairs={{1,2},{2,1},{3,4},{4,3},{5,6},{6,5},{7,8},{8,7},{9,10},{10,9},{11,... | collective-permute-start | bytes 1179656 | tf_op jit(solution)/shard_map/ppermute | solution.py:282
  32.7 0.8 collective-permute-start.3
  33.5 0.7 copy-done.12
  34.2 0.7 copy-done.8
  35.0 5.2 %collective-permute-done.2.cross_ref = bf16[128,1536]{1,0:T(8,128)(2,1)S(1)} collective-permute-done((bf16[128,1536]{1,0:T(8,128)(2,1)S(1)}, bf16[128,1536]{1,0:T(8,128)(2,1)S(1)}, u32[]{:S(2)}, u32[]{:S(2)}) %collective-permute-start.2) | collective-permute-done | bytes 393248 | tf_op jit(solution)/shard_map/ppermute | solution.py:282
  40.2 5.3 %attention.2 = (bf16[128,768]{1,0:T(8,128)(2,1)S(1)}, bf16[128,768]{1,0:T(8,128)(2,1)S(1)}, bf16[128,1536]{1,0:T(8,128)(2,1)S(1)}, bf16[128,1536]{1,0:T(8,128)(2,1)}) custom-call(s32[4]{0:T(128)S(1)} %pad_add_fusion.1.flags_ref, f32[12]{0:T(128)S(1)} %bitcast.49, bf16[128,2304]{1,0:T(8,128)(2,1)S(1)} %project.2.proj_ref, ...), custom_call_target="tpu_custom_call" | custom-call | flops 905969664 | bytes 4522048 | tf_op jit(solution)/shard_map/attention/pallas_call | solution.py:230
  45.6 2.8 %collective-permute-start.11 = (bf16[128,1536]{1,0:T(8,128)(2,1)}, bf16[128,1536]{1,0:T(8,128)(2,1)}, u32[]{:S(2)}, u32[]{:S(2)}) collective-permute-start(bf16[128,1536]{1,0:T(8,128)(2,1)} %get-tuple-element.32), channel_id=1, source_target_pairs={{1,2},{2,1},{3,4},{4,3},{5,6},{6,5},{7,8},{8,7},{9,10},{10,9},{11,... | collective-permute-start | bytes 1179656 | tf_op jit(solution)/shard_map/ppermute | solution.py:282
  48.4 2.5 %collective-permute-start.12 = (bf16[128,1536]{1,0:T(8,128)(2,1)}, bf16[128,1536]{1,0:T(8,128)(2,1)}, u32[]{:S(2)}, u32[]{:S(2)}) collective-permute-start(bf16[128,1536]{1,0:T(8,128)(2,1)} %get-tuple-element.32), channel_id=1, source_target_pairs={{0,1},{1,0},{2,3},{3,2},{4,5},{5,4},{6,7},{7,6},{8,9},{9,8},{10,11... | collective-permute-start | bytes 1179656 | tf_op jit(solution)/shard_map/ppermute | solution.py:291
  50.9 1.2 output.2
  52.2 2.2 %collective-permute-start.6 = (bf16[128,1536]{1,0:T(8,128)(2,1)}, bf16[128,1536]{1,0:T(8,128)(2,1)}, u32[]{:S(2)}, u32[]{:S(2)}) collective-permute-start(bf16[128,1536]{1,0:T(8,128)(2,1)} %output.2), channel_id=1, source_target_pairs={{0,242},{1,243},{2,240},{3,241},{4,246},{5,247},{6,244},{7,245},{8... | collective-permute-start | bytes 1179656 | tf_op jit(solution)/shard_map/ppermute | solution.py:273
  58.0 1.0 copy-done.15
  59.0 0.9 copy-done.17
  59.9 2.1 %keys.2 = (bf16[128,1536]{1,0:T(8,128)(2,1)S(1)}, bf16[64,1536]{1,0:T(8,128)(2,1)S(1)}, bf16[64,1536]{1,0:T(8,128)(2,1)S(1)}) custom-call(s32[4]{0:T(128)S(1)} %pad_add_fusion.1.flags_ref, bf16[128,1536]{1,0:T(8,128)(2,1)S(1)} %copy-done.15, bf16[128,1536]{1,0:T(8,128)(2,1)} %collective-permute-done.11.cross_ref, ...), custom_call_target="tpu_custom_call" | custom-call | flops 7864320 | bytes 1376272 | tf_op jit(solution)/shard_map/keys/pallas_call | solution.py:230
  62.0 3.2 %collective-permute-start.13 = (bf16[64,1536]{1,0:T(8,128)(2,1)S(1)}, bf16[64,1536]{1,0:T(8,128)(2,1)S(1)}, u32[]{:S(2)}, u32[]{:S(2)}) collective-permute-start(bf16[64,1536]{1,0:T(8,128)(2,1)S(1)} %get-tuple-element.34), channel_id=1, source_target_pairs={{1,2},{2,1},{3,4},{4,3},{5,6},{6,5},{7,8},{8,7},{9,10},{10,9},{11,... | collective-permute-start | bytes 589832 | tf_op jit(solution)/shard_map/ppermute | solution.py:282
  65.3 1.2 collective-permute-start.14
  66.5 1.0 constant_dynamic-slice_fusion
  67.6 5.1 %collective-permute-start.7 = (bf16[64,1536]{1,0:T(8,128)(2,1)S(1)}, bf16[64,1536]{1,0:T(8,128)(2,1)S(1)}, u32[]{:S(2)}, u32[]{:S(2)}) collective-permute-start(bf16[64,1536]{1,0:T(8,128)(2,1)S(1)} %get-tuple-element.57), channel_id=1, source_target_pairs={{1,2},{2,1},{3,4},{4,3},{5,6},{6,5},{7,8},{8,7},{9,10},{10,9},{11,... | collective-permute-start | bytes 589832 | tf_op jit(solution)/shard_map/ppermute | solution.py:282
  72.7 0.1 collective-permute-start.8
  72.8 0.1 pad_add_fusion.flags_ref
  72.9 3.0 %copy-done.2 = bf16[1,1536,2304]{2,1,0:T(8,128)(2,1)S(1)} copy-done((bf16[1,1536,2304]{2,1,0:T(8,128)(2,1)S(1)}, bf16[1,1536,2304]{2,1,0:T(8,128)(2,1)}, u32[]{:S(2)}) %copy-start.2) | copy-done | bytes 7077912
  75.9 2.5 %project.3.proj_ref = bf16[128,2304]{1,0:T(8,128)(2,1)S(1)} custom-call(bf16[128,1536]{1,0:T(8,128)(2,1)} %collective-permute-done.6.a_ref, bf16[1536,2304]{1,0:T(8,128)(2,1)S(1)} %bitcast.28), custom_call_target="tpu_custom_call" | custom-call | flops 905969664 | bytes 7471104 | tf_op jit(solution)/shard_map/project/pallas_call | solution.py:230
  78.5 0.0 copy-start.4
  78.5 4.2 %final.2 = bf16[128,1536]{1,0:T(8,128)(2,1)S(1)} custom-call(s32[4]{0:T(128)S(1)} %pad_add_fusion.1.flags_ref, bf16[64,1536]{1,0:T(8,128)(2,1)S(1)} %collective-permute-done.13.cross_ref, bf16[128,1536]{1,0:T(8,128)(2,1)S(1)} %get-tuple-element.35.own_ref, bf16[64,1536]{1,0:T(8,128)(2,1)S(1)} %collective-permute-done.14.inner_ref, ...), custom_call_target="tpu_custom_call" | custom-call | flops 905969664 | bytes 9013264 | tf_op jit(solution)/shard_map/final/pallas_call | solution.py:230
  82.7 0.7 collective-permute-start.15
  83.4 2.8 %pool.3 = (bf16[128,1536]{1,0:T(8,128)(2,1)S(1)}, bf16[128,768]{1,0:T(8,128)(2,1)S(1)}) custom-call(s32[4]{0:T(128)S(1)} %pad_add_fusion.flags_ref, bf16[64,1536]{1,0:T(8,128)(2,1)S(1)} %collective-permute-done.7.cross_ref, bf16[64,1536]{1,0:T(8,128)(2,1)S(1)} %collective-permute-done.8.inner_ref, bf16[1536,2304]{1,0:T(8,128)(2,1)S(1)} %bitcast.32, ...), custom_call_target="tpu_custom_call" | custom-call | flops 603979776 | bytes 8226832 | tf_op jit(solution)/shard_map/pool/pallas_call | solution.py:230
  86.2 0.3 collective-permute-start.10
  86.5 3.6 %collective-permute-start.9 = (bf16[128,1536]{1,0:T(8,128)(2,1)S(1)}, bf16[128,1536]{1,0:T(8,128)(2,1)S(1)}, u32[]{:S(2)}, u32[]{:S(2)}) collective-permute-start(bf16[128,1536]{1,0:T(8,128)(2,1)S(1)} %get-tuple-element.30.own_ref), channel_id=1, source_target_pairs={{1,2},{2,1},{3,4},{4,3},{5,6},{6,5},{7,8},{8,7},{9,10},{10,9},{11,... | collective-permute-start | bytes 1179656 | tf_op jit(solution)/shard_map/ppermute | solution.py:282
  90.1 4.2 %collective-permute-done.15.gb_ref = bf16[128,1536]{1,0:T(8,128)(2,1)S(1)} collective-permute-done((bf16[128,1536]{1,0:T(8,128)(2,1)S(1)}, bf16[128,1536]{1,0:T(8,128)(2,1)S(1)}, u32[]{:S(2)}, u32[]{:S(2)}) %collective-permute-start.15) | collective-permute-done | bytes 393248 | tf_op jit(solution)/shard_map/ppermute | solution.py:273
  94.3 2.3 %collective-permute-done.9.cross_ref = bf16[128,1536]{1,0:T(8,128)(2,1)S(1)} collective-permute-done((bf16[128,1536]{1,0:T(8,128)(2,1)S(1)}, bf16[128,1536]{1,0:T(8,128)(2,1)S(1)}, u32[]{:S(2)}, u32[]{:S(2)}) %collective-permute-start.9) | collective-permute-done | bytes 393248 | tf_op jit(solution)/shard_map/ppermute | solution.py:282
  96.6 4.6 %attention.3 = (bf16[128,768]{1,0:T(8,128)(2,1)S(1)}, bf16[128,768]{1,0:T(8,128)(2,1)S(1)}, bf16[128,1536]{1,0:T(8,128)(2,1)S(1)}, bf16[128,1536]{1,0:T(8,128)(2,1)S(1)}) custom-call(s32[4]{0:T(128)S(1)} %pad_add_fusion.flags_ref, f32[12]{0:T(128)S(1)} %bitcast.50, bf16[128,2304]{1,0:T(8,128)(2,1)S(1)} %project.3.proj_ref, ...), custom_call_target="tpu_custom_call" | custom-call | flops 905969664 | bytes 4522048 | tf_op jit(solution)/shard_map/attention/pallas_call | solution.py:230
  101.3 3.3 %collective-permute-start.19 = (bf16[128,1536]{1,0:T(8,128)(2,1)S(1)}, bf16[128,1536]{1,0:T(8,128)(2,1)S(1)}, u32[]{:S(2)}, u32[]{:S(2)}) collective-permute-start(bf16[128,1536]{1,0:T(8,128)(2,1)S(1)} %get-tuple-element.41), channel_id=1, source_target_pairs={{1,2},{2,1},{3,4},{4,3},{5,6},{6,5},{7,8},{8,7},{9,10},{10,9},{11,... | collective-permute-start | bytes 1179656 | tf_op jit(solution)/shard_map/ppermute | solution.py:282
  104.6 2.2 %collective-permute-start.20 = (bf16[128,1536]{1,0:T(8,128)(2,1)S(1)}, bf16[128,1536]{1,0:T(8,128)(2,1)S(1)}, u32[]{:S(2)}, u32[]{:S(2)}) collective-permute-start(bf16[128,1536]{1,0:T(8,128)(2,1)S(1)} %get-tuple-element.41), channel_id=1, source_target_pairs={{0,1},{1,0},{2,3},{3,2},{4,5},{5,4},{6,7},{7,6},{8,9},{9,8},{10,11... | collective-permute-start | bytes 1179656 | tf_op jit(solution)/shard_map/ppermute | solution.py:291
  106.8 4.6 %collective-permute-done.19.cross_ref = bf16[128,1536]{1,0:T(8,128)(2,1)S(1)} collective-permute-done((bf16[128,1536]{1,0:T(8,128)(2,1)S(1)}, bf16[128,1536]{1,0:T(8,128)(2,1)S(1)}, u32[]{:S(2)}, u32[]{:S(2)}) %collective-permute-start.19) | collective-permute-done | bytes 393248 | tf_op jit(solution)/shard_map/ppermute | solution.py:282
  111.4 1.5 keys.3
  112.9 3.3 %collective-permute-start.21 = (bf16[64,1536]{1,0:T(8,128)(2,1)S(1)}, bf16[64,1536]{1,0:T(8,128)(2,1)S(1)}, u32[]{:S(2)}, u32[]{:S(2)}) collective-permute-start(bf16[64,1536]{1,0:T(8,128)(2,1)S(1)} %get-tuple-element.43), channel_id=1, source_target_pairs={{1,2},{2,1},{3,4},{4,3},{5,6},{6,5},{7,8},{8,7},{9,10},{10,9},{11,... | collective-permute-start | bytes 589832 | tf_op jit(solution)/shard_map/ppermute | solution.py:282
  116.2 2.6 %collective-permute-start.22 = (bf16[64,1536]{1,0:T(8,128)(2,1)S(1)}, bf16[64,1536]{1,0:T(8,128)(2,1)S(1)}, u32[]{:S(2)}, u32[]{:S(2)}) collective-permute-start(bf16[64,1536]{1,0:T(8,128)(2,1)S(1)} %get-tuple-element.45), channel_id=1, source_target_pairs={{0,1},{1,0},{2,3},{3,2},{4,5},{5,4},{6,7},{7,6},{8,9},{9,8},{10,11... | collective-permute-start | bytes 589832 | tf_op jit(solution)/shard_map/ppermute | solution.py:291
  118.8 2.8 %collective-permute-start.17 = (bf16[128,1536]{1,0:T(8,128)(2,1)}, bf16[128,1536]{1,0:T(8,128)(2,1)S(1)}, u32[]{:S(2)}, u32[]{:S(2)}) collective-permute-start(bf16[128,1536]{1,0:T(8,128)(2,1)} %collective-permute-done.6.a_ref), channel_id=1, source_target_pairs={{0,240},{1,241},{2,242},{3,243},{4,244},{5,245},{6,246},{7,247},{8... | collective-permute-start | bytes 1179656 | tf_op jit(solution)/shard_map/ppermute | solution.py:273
  121.6 0.5 output.3
  122.0 0.3 collective-permute-start.16
  122.3 0.1 collective-permute-start.18
  122.4 4.7 %final.3 = bf16[128,1536]{1,0:T(8,128)(2,1)S(1)} custom-call(s32[4]{0:T(128)S(1)} %pad_add_fusion.flags_ref, bf16[64,1536]{1,0:T(8,128)(2,1)S(1)} %collective-permute-done.21.cross_ref, bf16[128,1536]{1,0:T(8,128)(2,1)S(1)} %get-tuple-element.44.own_ref, bf16[64,1536]{1,0:T(8,128)(2,1)S(1)} %collective-permute-done.22.inner_ref, ...), custom_call_target="tpu_custom_call" | custom-call | flops 905969664 | bytes 9013264 | tf_op jit(solution)/shard_map/final/pallas_call | solution.py:230
  127.1 35.9 %collective-permute-start.23 = (bf16[128,1536]{1,0:T(8,128)(2,1)S(1)}, bf16[128,1536]{1,0:T(8,128)(2,1)S(1)}, u32[]{:S(2)}, u32[]{:S(2)}) collective-permute-start(bf16[128,1536]{1,0:T(8,128)(2,1)S(1)} %final.3), channel_id=1, source_target_pairs={{0,240},{1,241},{2,242},{3,243},{4,244},{5,245},{6,246},{7,247},{8... | collective-permute-start | bytes 1179656 | tf_op jit(solution)/shard_map/ppermute | solution.py:273
  163.0 5.3 %collective-permute-done.23 = bf16[128,1536]{1,0:T(8,128)(2,1)S(1)} collective-permute-done((bf16[128,1536]{1,0:T(8,128)(2,1)S(1)}, bf16[128,1536]{1,0:T(8,128)(2,1)S(1)}, u32[]{:S(2)}, u32[]{:S(2)}) %collective-permute-start.23) | collective-permute-done | bytes 393248 | tf_op jit(solution)/shard_map/ppermute | solution.py:273
  168.3 0.7 copy.20
  169.1 0.7 copy.21
  169.8 0.7 copy.22
  170.6 0.7 copy.23
  (56 shorter events, 0.1 us)
Async XLA Ops:
  1.7 23.3 %collective-permute-start = (bf16[64,1536]{1,0:T(8,128)(2,1)S(1)}, bf16[64,1536]{1,0:T(8,128)(2,1)S(1)}, u32[]{:S(2)}, u32[]{:S(2)}) collective-permute-start(bf16[64,1536]{1,0:T(8,128)(2,1)S(1)} %get-tuple-element.59), channel_id=1, source_target_pairs={{1,2},{2,1},{3,4},{4,3},{5,6},{6,5},{7,8},{8,7},{9,10},{10,9},{11,... | collective-permute-start | bytes 589832 | tf_op jit(solution)/shard_map/ppermute | solution.py:282
  4.9 20.1 %collective-permute-start.1 = (bf16[64,1536]{1,0:T(8,128)(2,1)S(1)}, bf16[64,1536]{1,0:T(8,128)(2,1)S(1)}, u32[]{:S(2)}, u32[]{:S(2)}) collective-permute-start(bf16[64,1536]{1,0:T(8,128)(2,1)S(1)} %get-tuple-element.58), channel_id=1, source_target_pairs={{0,1},{1,0},{2,3},{3,2},{4,5},{5,4},{6,7},{7,6},{8,9},{9,8},{10,11... | collective-permute-start | bytes 589832 | tf_op jit(solution)/shard_map/ppermute | solution.py:291
  5.4 28.1 %collective-permute-start.4 = (bf16[128,1536]{1,0:T(8,128)(2,1)}, bf16[128,1536]{1,0:T(8,128)(2,1)S(1)}, u32[]{:S(2)}, u32[]{:S(2)}) collective-permute-start(bf16[128,1536]{1,0:T(8,128)(2,1)} %bitcast.42), channel_id=1, source_target_pairs={{0,242},{1,243},{2,240},{3,241},{4,246},{5,247},{6,244},{7,245},{8... | collective-permute-start | bytes 1179656 | tf_op jit(solution)/shard_map/ppermute | solution.py:273
  12.3 21.9 %collective-permute-start.5 = (bf16[128,1536]{1,0:T(8,128)(2,1)}, bf16[128,1536]{1,0:T(8,128)(2,1)S(1)}, u32[]{:S(2)}, u32[]{:S(2)}) collective-permute-start(bf16[128,1536]{1,0:T(8,128)(2,1)} %bitcast.46), channel_id=1, source_target_pairs={{0,242},{1,243},{2,240},{3,241},{4,246},{5,247},{6,244},{7,245},{8... | collective-permute-start | bytes 1179656 | tf_op jit(solution)/shard_map/ppermute | solution.py:273
  19.5 3.0 %copy-start = (bf16[1,1536,2304]{2,1,0:T(8,128)(2,1)S(1)}, bf16[1,1536,2304]{2,1,0:T(8,128)(2,1)}, u32[]{:S(2)}) copy-start(bf16[1,1536,2304]{2,1,0:T(8,128)(2,1)} %param.13) | copy-start | bytes 21233668
  22.5 1.0 copy-start.5
  23.5 3.0 %copy-start.1 = (bf16[1,1536,2304]{2,1,0:T(8,128)(2,1)S(1)}, bf16[1,1536,2304]{2,1,0:T(8,128)(2,1)}, u32[]{:S(2)}) copy-start(bf16[1,1536,2304]{2,1,0:T(8,128)(2,1)} %param.13) | copy-start | bytes 21233668
  23.5 16.6 %copy-start.3 = (bf16[1,768,1536]{2,1,0:T(8,128)(2,1)S(1)}, bf16[1,768,1536]{2,1,0:T(8,128)(2,1)}, u32[]{:S(2)}) copy-start(bf16[1,768,1536]{2,1,0:T(8,128)(2,1)} %param.14) | copy-start | bytes 7077892
  23.5 16.7 %copy-start.10 = (bf16[1,128,1536]{2,1,0:T(8,128)(2,1)S(1)}, bf16[1,128,1536]{2,1,0:T(8,128)(2,1)}, u32[]{:S(2)}) copy-start(bf16[1,128,1536]{2,1,0:T(8,128)(2,1)} %param.12) | copy-start | bytes 1179652
  23.5 16.7 %copy-start.20 = (f32[1,12]{1,0:T(1,128)S(1)}, f32[1,12]{1,0:T(1,128)}, u32[]{:S(2)}) copy-start(f32[1,12]{1,0:T(1,128)} %param.16) | copy-start | bytes 148
  24.9 26.1 %copy-start.11 = (bf16[1,128,1536]{2,1,0:T(8,128)(2,1)S(1)}, bf16[1,128,1536]{2,1,0:T(8,128)(2,1)}, u32[]{:S(2)}) copy-start(bf16[1,128,1536]{2,1,0:T(8,128)(2,1)} %param.10) | copy-start | bytes 1179652
  29.4 0.7 copy-start.16
  30.1 10.1 %collective-permute-start.2 = (bf16[128,1536]{1,0:T(8,128)(2,1)S(1)}, bf16[128,1536]{1,0:T(8,128)(2,1)S(1)}, u32[]{:S(2)}, u32[]{:S(2)}) collective-permute-start(bf16[128,1536]{1,0:T(8,128)(2,1)S(1)} %get-tuple-element.26.own_ref), channel_id=1, source_target_pairs={{1,2},{2,1},{3,4},{4,3},{5,6},{6,5},{7,8},{8,7},{9,10},{10,9},{11,... | collective-permute-start | bytes 1179656 | tf_op jit(solution)/shard_map/ppermute | solution.py:282
  32.7 7.5 %collective-permute-start.3 = (bf16[128,1536]{1,0:T(8,128)(2,1)S(1)}, bf16[128,1536]{1,0:T(8,128)(2,1)S(1)}, u32[]{:S(2)}, u32[]{:S(2)}) collective-permute-start(bf16[128,1536]{1,0:T(8,128)(2,1)S(1)} %get-tuple-element.26.own_ref), channel_id=1, source_target_pairs={{0,1},{1,0},{2,3},{3,2},{4,5},{5,4},{6,7},{7,6},{8,9},{9,8},{10,11... | collective-permute-start | bytes 1179656 | tf_op jit(solution)/shard_map/ppermute | solution.py:291
  33.5 0.7 copy-start.12
  34.2 0.7 copy-start.8
  45.6 6.6 %copy-start.14 = (bf16[128,1536]{1,0:T(8,128)(2,1)}, bf16[128,1536]{1,0:T(8,128)(2,1)S(1)}, u32[]{:S(2)}) copy-start(bf16[128,1536]{1,0:T(8,128)(2,1)S(1)} %get-tuple-element.31.own_ref) | copy-start | bytes 1179652
  45.6 6.6 %copy-start.18 = (bf16[128,768]{1,0:T(8,128)(2,1)}, bf16[128,768]{1,0:T(8,128)(2,1)S(1)}, u32[]{:S(2)}) copy-start(bf16[128,768]{1,0:T(8,128)(2,1)S(1)} %get-tuple-element.37.gq_ref) | copy-start | bytes 589828
  45.6 32.8 %slice-start = ((s8[7077888]{0:T(1024)(128)(4,1)}), s8[2883584]{0:T(1024)(128)(4,1)S(1)}, s32[]{:S(2)}) async-start(s8[7077888]{0:T(1024)(128)(4,1)} %bitcast.29), calls=%async_computation | async-start | bytes 5767168
  45.6 32.9 %copy-start.6 = (bf16[1,128,1536]{2,1,0:T(8,128)(2,1)S(1)}, bf16[1,128,1536]{2,1,0:T(8,128)(2,1)}, u32[]{:S(2)}) copy-start(bf16[1,128,1536]{2,1,0:T(8,128)(2,1)} %param.9) | copy-start | bytes 1179652
  45.6 12.4 %collective-permute-start.11 = (bf16[128,1536]{1,0:T(8,128)(2,1)}, bf16[128,1536]{1,0:T(8,128)(2,1)}, u32[]{:S(2)}, u32[]{:S(2)}) collective-permute-start(bf16[128,1536]{1,0:T(8,128)(2,1)} %get-tuple-element.32), channel_id=1, source_target_pairs={{1,2},{2,1},{3,4},{4,3},{5,6},{6,5},{7,8},{8,7},{9,10},{10,9},{11,... | collective-permute-start | bytes 1179656 | tf_op jit(solution)/shard_map/ppermute | solution.py:282
  48.4 9.5 %collective-permute-start.12 = (bf16[128,1536]{1,0:T(8,128)(2,1)}, bf16[128,1536]{1,0:T(8,128)(2,1)}, u32[]{:S(2)}, u32[]{:S(2)}) collective-permute-start(bf16[128,1536]{1,0:T(8,128)(2,1)} %get-tuple-element.32), channel_id=1, source_target_pairs={{0,1},{1,0},{2,3},{3,2},{4,5},{5,4},{6,7},{7,6},{8,9},{9,8},{10,11... | collective-permute-start | bytes 1179656 | tf_op jit(solution)/shard_map/ppermute | solution.py:291
  52.2 14.3 %collective-permute-start.6 = (bf16[128,1536]{1,0:T(8,128)(2,1)}, bf16[128,1536]{1,0:T(8,128)(2,1)}, u32[]{:S(2)}, u32[]{:S(2)}) collective-permute-start(bf16[128,1536]{1,0:T(8,128)(2,1)} %output.2), channel_id=1, source_target_pairs={{0,242},{1,243},{2,240},{3,241},{4,246},{5,247},{6,244},{7,245},{8... | collective-permute-start | bytes 1179656 | tf_op jit(solution)/shard_map/ppermute | solution.py:273
  57.9 20.5 %copy-start.7 = (bf16[1,128,1536]{2,1,0:T(8,128)(2,1)S(1)}, bf16[1,128,1536]{2,1,0:T(8,128)(2,1)}, u32[]{:S(2)}) copy-start(bf16[1,128,1536]{2,1,0:T(8,128)(2,1)} %param.11) | copy-start | bytes 1179652
  58.0 1.0 copy-start.15
  59.0 0.9 copy-start.17
  59.9 18.5 %copy-start.19 = (bf16[128,768]{1,0:T(8,128)(2,1)S(1)}, bf16[128,768]{1,0:T(8,128)(2,1)}, u32[]{:S(2)}) copy-start(bf16[128,768]{1,0:T(8,128)(2,1)} %copy-done.18) | copy-start | bytes 589828
  62.0 16.3 %collective-permute-start.13 = (bf16[64,1536]{1,0:T(8,128)(2,1)S(1)}, bf16[64,1536]{1,0:T(8,128)(2,1)S(1)}, u32[]{:S(2)}, u32[]{:S(2)}) collective-permute-start(bf16[64,1536]{1,0:T(8,128)(2,1)S(1)} %get-tuple-element.34), channel_id=1, source_target_pairs={{1,2},{2,1},{3,4},{4,3},{5,6},{6,5},{7,8},{8,7},{9,10},{10,9},{11,... | collective-permute-start | bytes 589832 | tf_op jit(solution)/shard_map/ppermute | solution.py:282
  65.3 13.1 %collective-permute-start.14 = (bf16[64,1536]{1,0:T(8,128)(2,1)S(1)}, bf16[64,1536]{1,0:T(8,128)(2,1)S(1)}, u32[]{:S(2)}, u32[]{:S(2)}) collective-permute-start(bf16[64,1536]{1,0:T(8,128)(2,1)S(1)} %get-tuple-element.36), channel_id=1, source_target_pairs={{0,1},{1,0},{2,3},{3,2},{4,5},{5,4},{6,7},{7,6},{8,9},{9,8},{10,11... | collective-permute-start | bytes 589832 | tf_op jit(solution)/shard_map/ppermute | solution.py:291
  67.6 15.8 %collective-permute-start.7 = (bf16[64,1536]{1,0:T(8,128)(2,1)S(1)}, bf16[64,1536]{1,0:T(8,128)(2,1)S(1)}, u32[]{:S(2)}, u32[]{:S(2)}) collective-permute-start(bf16[64,1536]{1,0:T(8,128)(2,1)S(1)} %get-tuple-element.57), channel_id=1, source_target_pairs={{1,2},{2,1},{3,4},{4,3},{5,6},{6,5},{7,8},{8,7},{9,10},{10,9},{11,... | collective-permute-start | bytes 589832 | tf_op jit(solution)/shard_map/ppermute | solution.py:282
  72.7 10.7 %collective-permute-start.8 = (bf16[64,1536]{1,0:T(8,128)(2,1)S(1)}, bf16[64,1536]{1,0:T(8,128)(2,1)S(1)}, u32[]{:S(2)}, u32[]{:S(2)}) collective-permute-start(bf16[64,1536]{1,0:T(8,128)(2,1)S(1)} %get-tuple-element.56), channel_id=1, source_target_pairs={{0,1},{1,0},{2,3},{3,2},{4,5},{5,4},{6,7},{7,6},{8,9},{9,8},{10,11... | collective-permute-start | bytes 589832 | tf_op jit(solution)/shard_map/ppermute | solution.py:291
  72.9 3.0 %copy-start.2 = (bf16[1,1536,2304]{2,1,0:T(8,128)(2,1)S(1)}, bf16[1,1536,2304]{2,1,0:T(8,128)(2,1)}, u32[]{:S(2)}) copy-start(bf16[1,1536,2304]{2,1,0:T(8,128)(2,1)} %param.13) | copy-start | bytes 21233668
  75.9 2.5 %slice-start.1 = ((s8[7077888]{0:T(1024)(128)(4,1)}), s8[4194304]{0:T(1024)(128)(4,1)S(1)}, s32[]{:S(2)}) async-start(s8[7077888]{0:T(1024)(128)(4,1)} %bitcast.29), calls=%async_computation.1 | async-start | bytes 8388608
  78.5 18.2 %copy-start.4 = (bf16[1,768,1536]{2,1,0:T(8,128)(2,1)S(1)}, bf16[1,768,1536]{2,1,0:T(8,128)(2,1)}, u32[]{:S(2)}) copy-start(bf16[1,768,1536]{2,1,0:T(8,128)(2,1)} %param.14) | copy-start | bytes 7077892
  82.7 38.9 %copy-start.13 = (bf16[128,1536]{1,0:T(8,128)(2,1)S(1)}, bf16[128,1536]{1,0:T(8,128)(2,1)}, u32[]{:S(2)}) copy-start(bf16[128,1536]{1,0:T(8,128)(2,1)} %copy-done.12) | copy-start | bytes 1179652
  82.7 39.7 %copy-start.9 = (bf16[128,1536]{1,0:T(8,128)(2,1)S(1)}, bf16[128,1536]{1,0:T(8,128)(2,1)}, u32[]{:S(2)}) copy-start(bf16[128,1536]{1,0:T(8,128)(2,1)} %copy-done.8) | copy-start | bytes 1179652
  82.7 11.6 %collective-permute-start.15 = (bf16[128,1536]{1,0:T(8,128)(2,1)S(1)}, bf16[128,1536]{1,0:T(8,128)(2,1)S(1)}, u32[]{:S(2)}, u32[]{:S(2)}) collective-permute-start(bf16[128,1536]{1,0:T(8,128)(2,1)S(1)} %final.2), channel_id=1, source_target_pairs={{0,242},{1,243},{2,240},{3,241},{4,246},{5,247},{6,244},{7,245},{8... | collective-permute-start | bytes 1179656 | tf_op jit(solution)/shard_map/ppermute | solution.py:273
  86.2 8.0 %collective-permute-start.10 = (bf16[128,1536]{1,0:T(8,128)(2,1)S(1)}, bf16[128,1536]{1,0:T(8,128)(2,1)S(1)}, u32[]{:S(2)}, u32[]{:S(2)}) collective-permute-start(bf16[128,1536]{1,0:T(8,128)(2,1)S(1)} %get-tuple-element.30.own_ref), channel_id=1, source_target_pairs={{0,1},{1,0},{2,3},{3,2},{4,5},{5,4},{6,7},{7,6},{8,9},{9,8},{10,11... | collective-permute-start | bytes 1179656 | tf_op jit(solution)/shard_map/ppermute | solution.py:291
  86.5 10.1 %collective-permute-start.9 = (bf16[128,1536]{1,0:T(8,128)(2,1)S(1)}, bf16[128,1536]{1,0:T(8,128)(2,1)S(1)}, u32[]{:S(2)}, u32[]{:S(2)}) collective-permute-start(bf16[128,1536]{1,0:T(8,128)(2,1)S(1)} %get-tuple-element.30.own_ref), channel_id=1, source_target_pairs={{1,2},{2,1},{3,4},{4,3},{5,6},{6,5},{7,8},{8,7},{9,10},{10,9},{11,... | collective-permute-start | bytes 1179656 | tf_op jit(solution)/shard_map/ppermute | solution.py:282
  101.3 10.1 %collective-permute-start.19 = (bf16[128,1536]{1,0:T(8,128)(2,1)S(1)}, bf16[128,1536]{1,0:T(8,128)(2,1)S(1)}, u32[]{:S(2)}, u32[]{:S(2)}) collective-permute-start(bf16[128,1536]{1,0:T(8,128)(2,1)S(1)} %get-tuple-element.41), channel_id=1, source_target_pairs={{1,2},{2,1},{3,4},{4,3},{5,6},{6,5},{7,8},{8,7},{9,10},{10,9},{11,... | collective-permute-start | bytes 1179656 | tf_op jit(solution)/shard_map/ppermute | solution.py:282
  104.6 6.7 %collective-permute-start.20 = (bf16[128,1536]{1,0:T(8,128)(2,1)S(1)}, bf16[128,1536]{1,0:T(8,128)(2,1)S(1)}, u32[]{:S(2)}, u32[]{:S(2)}) collective-permute-start(bf16[128,1536]{1,0:T(8,128)(2,1)S(1)} %get-tuple-element.41), channel_id=1, source_target_pairs={{0,1},{1,0},{2,3},{3,2},{4,5},{5,4},{6,7},{7,6},{8,9},{9,8},{10,11... | collective-permute-start | bytes 1179656 | tf_op jit(solution)/shard_map/ppermute | solution.py:291
  112.9 9.6 %collective-permute-start.21 = (bf16[64,1536]{1,0:T(8,128)(2,1)S(1)}, bf16[64,1536]{1,0:T(8,128)(2,1)S(1)}, u32[]{:S(2)}, u32[]{:S(2)}) collective-permute-start(bf16[64,1536]{1,0:T(8,128)(2,1)S(1)} %get-tuple-element.43), channel_id=1, source_target_pairs={{1,2},{2,1},{3,4},{4,3},{5,6},{6,5},{7,8},{8,7},{9,10},{10,9},{11,... | collective-permute-start | bytes 589832 | tf_op jit(solution)/shard_map/ppermute | solution.py:282
  116.2 6.2 %collective-permute-start.22 = (bf16[64,1536]{1,0:T(8,128)(2,1)S(1)}, bf16[64,1536]{1,0:T(8,128)(2,1)S(1)}, u32[]{:S(2)}, u32[]{:S(2)}) collective-permute-start(bf16[64,1536]{1,0:T(8,128)(2,1)S(1)} %get-tuple-element.45), channel_id=1, source_target_pairs={{0,1},{1,0},{2,3},{3,2},{4,5},{5,4},{6,7},{7,6},{8,9},{9,8},{10,11... | collective-permute-start | bytes 589832 | tf_op jit(solution)/shard_map/ppermute | solution.py:291
  118.8 44.2 %collective-permute-start.17 = (bf16[128,1536]{1,0:T(8,128)(2,1)}, bf16[128,1536]{1,0:T(8,128)(2,1)S(1)}, u32[]{:S(2)}, u32[]{:S(2)}) collective-permute-start(bf16[128,1536]{1,0:T(8,128)(2,1)} %collective-permute-done.6.a_ref), channel_id=1, source_target_pairs={{0,240},{1,241},{2,242},{3,243},{4,244},{5,245},{6,246},{7,247},{8... | collective-permute-start | bytes 1179656 | tf_op jit(solution)/shard_map/ppermute | solution.py:273
  122.0 41.0 %collective-permute-start.16 = (bf16[128,1536]{1,0:T(8,128)(2,1)S(1)}, bf16[128,1536]{1,0:T(8,128)(2,1)S(1)}, u32[]{:S(2)}, u32[]{:S(2)}) collective-permute-start(bf16[128,1536]{1,0:T(8,128)(2,1)S(1)} %output.3), channel_id=1, source_target_pairs={{0,240},{1,241},{2,242},{3,243},{4,244},{5,245},{6,246},{7,247},{8... | collective-permute-start | bytes 1179656 | tf_op jit(solution)/shard_map/ppermute | solution.py:273
  122.3 40.7 %collective-permute-start.18 = (bf16[128,1536]{1,0:T(8,128)(2,1)S(1)}, bf16[128,1536]{1,0:T(8,128)(2,1)S(1)}, u32[]{:S(2)}, u32[]{:S(2)}) collective-permute-start(bf16[128,1536]{1,0:T(8,128)(2,1)S(1)} %collective-permute-done.15.gb_ref), channel_id=1, source_target_pairs={{0,240},{1,241},{2,242},{3,243},{4,244},{5,245},{6,246},{7,247},{8... | collective-permute-start | bytes 1179656 | tf_op jit(solution)/shard_map/ppermute | solution.py:273
  127.1 41.2 %collective-permute-start.23 = (bf16[128,1536]{1,0:T(8,128)(2,1)S(1)}, bf16[128,1536]{1,0:T(8,128)(2,1)S(1)}, u32[]{:S(2)}, u32[]{:S(2)}) collective-permute-start(bf16[128,1536]{1,0:T(8,128)(2,1)S(1)} %final.3), channel_id=1, source_target_pairs={{0,240},{1,241},{2,242},{3,243},{4,244},{5,245},{6,246},{7,247},{8... | collective-permute-start | bytes 1179656 | tf_op jit(solution)/shard_map/ppermute | solution.py:273

commit v2 on v1

v2 whole, which is shorter than its diff:
```python
import functools

import jax
import jax.numpy as jnp
from jax import lax
from jax.experimental import pallas as pl
from jax.experimental.pallas import tpu as pltpu
from jax.sharding import PartitionSpec as P

HEADS = 12
HEAD = 64
FT = 4
FW = 16
PAIRS = HEADS // 2
PW = 2 * HEAD
ROW = FT * FW

EPS_NORM = 1e-05
EPS_HEAD = 1e-06

F32 = jnp.float32
BF16 = jnp.bfloat16
VMEM = pltpu.VMEM
SMEM = pltpu.SMEM
HBM = pltpu.HBM
DMA = pltpu.SemaphoreType.DMA


def dot(a, b):
    return jnp.dot(a, b, preferred_element_type=F32)


def dot_nt(a, b):
    return lax.dot_general(a, b, (((1,), (1,)), ((), ())), preferred_element_type=F32)


def normalize_rows(features):
    average = jnp.mean(features, axis=-1, keepdims=True)
    centred = features - average
    inverse = lax.rsqrt(jnp.mean(centred * centred, axis=-1, keepdims=True) + EPS_NORM)
    return centred * inverse, inverse


def first_half(shape):
    return lax.broadcasted_iota(jnp.int32, shape, 1) < HEAD


def pair_sums(values, first):
    low = jnp.sum(jnp.where(first, values, 0.0), axis=-1, keepdims=True)
    high = jnp.sum(jnp.where(first, 0.0, values), axis=-1, keepdims=True)
    return jnp.where(first, low, high)


def pair_unit(values, first):
    inverse = lax.rsqrt(pair_sums(values * values, first) + EPS_HEAD)
    return values * inverse, inverse


def pair_unit_back(unit, inverse, gradient, first):
    return inverse * (gradient - unit * pair_sums(unit * gradient, first))


def pool_lanes(ext_ref, taps, flip, rows):
    column = lax.broadcasted_iota(jnp.int32, (FW, 128), 0)
    blocks = []
    for row in range(2):
        for frame in range(FT):
            parts = [None, None, None]
            for dr in range(3):
                if row + dr not in rows:
                    continue
                for df in range(3):
                    source = frame + df - 1
                    if source < 0 or source >= FT:
                        continue
                    start = (row + dr) * ROW + source * FW
                    block = ext_ref[start : start + FW, :]
                    for dc in range(3):
                        tap = dr * 9 + df * 3 + dc
                        term = taps[26 - tap if flip else tap] * block
                        parts[dc] = term if parts[dc] is None else parts[dc] + term
            left = jnp.where(column == 0, 0.0, pltpu.roll(parts[0], 1, 0))
            right = jnp.where(column == FW - 1, 0.0, pltpu.roll(parts[2], FW - 1, 0))
            blocks.append(parts[1] + left + right)
    return jnp.concatenate(blocks, axis=0)


def load_taps(kern_ref, lanes):
    return [jnp.broadcast_to(kern_ref[t, :, lanes], (FW, 128)) for t in range(27)]


def is_odd():
    return (lax.axis_index("space") & 1) == 1


def lists(owner_ref, row, tile):
    return (owner_ref[row, 0] == tile) | (owner_ref[row, 1] == tile)


def this_tile(layout):
    space = lax.axis_index("space")
    return space ^ (2 * layout(lax.axis_index("section"), space >> 2))


def stream(ref, buf, sems, cuts):
    copies = [pltpu.make_async_copy(ref.at[cut], buf.at[cut], sems.at[k]) for k, cut in enumerate(cuts)]
    for copy in copies:
        copy.start()

    def get(k):
        copies[k].wait()
        return buf[cuts[k]]

    return get


WHOLE = [(slice(None), slice(None))]


def project_kernel(a_ref, w_ref, out_ref):
    low = normalize_rows(a_ref[...].astype(F32))[0].astype(BF16)
    for c in range(0, w_ref.shape[1], 256):
        cut = slice(c, c + 256)
        out_ref[:, cut] = dot(low, w_ref[:, cut]).astype(BF16)


def first_project_kernel(a_ref, w_ref, out_ref, a_buf, w_buf, acc_ref, sems, w_sems):
    get_a = stream(a_ref, a_buf, sems, WHOLE)
    cuts = [(slice(r, r + 256), slice(None)) for r in range(0, w_ref.shape[0], 256)]
    get = stream(w_ref, w_buf, w_sems, cuts)
    low = normalize_rows(get_a(0).astype(F32))[0].astype(BF16)
    for k, (rows, _) in enumerate(cuts):
        piece = get(k)
        for c in range(0, w_ref.shape[1], 256):
            cut = slice(c, c + 256)
            total = dot(low[:, rows], piece[:, cut])
            if k:
                total = total + acc_ref[:, cut]
            if k + 1 < len(cuts):
                acc_ref[:, cut] = total
            else:
                out_ref[:, cut] = total.astype(BF16)


def pool_kernel(cross_ref, inner_ref, w_ref, proj_ref, kern_ref, kv_ref, pk_ref, ext_ref):
    hidden = pk_ref.shape[1]
    odd = is_odd()
    cross, inner = cross_ref[...], inner_ref[...]
    halo = jnp.concatenate(
        [jnp.where(odd, inner, cross), jnp.where(odd, cross, inner)], axis=0
    ).astype(F32)
    low = normalize_rows(halo)[0].astype(BF16)
    first = first_half((128, 128))
    for c in range(0, 2 * hidden, 256):
        outer = dot(low, w_ref[:, hidden + c : hidden + c + 256]).astype(BF16).astype(F32)
        for j in (0, 128):
            at = c + j
            ext_ref[0:ROW, :] = outer[:ROW, j : j + 128]
            ext_ref[ROW : ROW + 128, :] = proj_ref[:, hidden + at : hidden + at + 128].astype(F32)
            ext_ref[ROW + 128 :, :] = outer[ROW:, j : j + 128]
            pooled = pool_lanes(ext_ref, load_taps(kern_ref, slice(at, at + 128)), False, (0, 1, 2, 3)).astype(BF16)
            if at < hidden:
                pk_ref[:, at : at + 128] = pooled
                kv_ref[:, at : at + 128] = pair_unit(pooled.astype(F32), first)[0].astype(BF16)
            else:
                kv_ref[:, at : at + 128] = pooled


def attention_kernel(
    layout, owner_ref, tau_ref, proj_ref, own_ref, cross_ref, inner_ref, grad_ref,
    att_ref, gq_ref, part_own_ref, part_near_ref,
):
    hidden = att_ref.shape[1]
    tile = this_tile(layout)
    from_cross = lists(owner_ref, tile, tile - 1) ^ is_odd()
    first = first_half((128, 128))
    first_low = first_half((256, 128))

    def both(at):
        near = jnp.where(from_cross, cross_ref[:, at : at + PW], inner_ref[:, at : at + PW])
        return jnp.concatenate([own_ref[:, at : at + PW], near], axis=0)

    def masked(rows):
        zero = jnp.zeros_like(rows)
        return jnp.concatenate(
            [jnp.where(first_low, rows, zero), jnp.where(first_low, zero, rows)], axis=0
        )

    for p in range(PAIRS):
        at = p * PW
        g2 = grad_ref[:, at : at + PW]
        q_unit, q_inverse = pair_unit(proj_ref[:, at : at + PW].astype(F32), first)
        q_low = q_unit.astype(BF16)
        keys = masked(both(at))
        values = masked(both(hidden + at))
        scores = dot_nt(q_low, keys)
        grad_probs = dot_nt(g2, values)
        probs, grads = [], []
        for half in range(2):
            scale = tau_ref[2 * p + half]
            cut = slice(half * 256, half * 256 + 256)
            exponent = jnp.exp(scores[:, cut] * scale)
            prob = exponent * (1.0 / jnp.sum(exponent, axis=-1, keepdims=True))
            gp = grad_probs[:, cut]
            delta = jnp.sum(prob * gp, axis=-1, keepdims=True)
            probs.append(prob.astype(BF16))
            grads.append((scale * prob * (gp - delta)).astype(BF16))
        prob_low = jnp.concatenate(probs, axis=1)
        grad_scores = jnp.concatenate(grads, axis=1)
        att_ref[:, at : at + PW] = dot(prob_low, values).astype(BF16)
        grad_q = dot(grad_scores, keys)
        gq_ref[:, at : at + PW] = pair_unit_back(q_unit, q_inverse, grad_q, first).astype(BF16)
        grad_k = dot(grad_scores.T, q_low)
        grad_v = dot(prob_low.T, g2)
        grad_k = jnp.where(first_low, grad_k[:256], grad_k[256:]).astype(BF16)
        grad_v = jnp.where(first_low, grad_v[:256], grad_v[256:]).astype(BF16)
        part_own_ref[:, at : at + PW] = grad_k[:128]
        part_near_ref[:, at : at + PW] = grad_k[128:]
        part_own_ref[:, hidden + at : hidden + at + PW] = grad_v[:128]
        part_near_ref[:, hidden + at : hidden + at + PW] = grad_v[128:]


def attention_output_kernel(layout, *refs):
    ins, (wout_ref, b_ref), outs = refs[:7], refs[7:9], refs[9:13]
    out_ref, wout_buf, b_buf, sems = refs[13:]
    get_w = stream(wout_ref, wout_buf, sems.at[0], WHOLE)
    get_b = stream(b_ref, b_buf, sems.at[1], WHOLE)
    attention_kernel(layout, *ins, *outs)
    get_w(0)
    get_b(0)
    output_kernel(outs[0], wout_buf, b_buf, out_ref)


def settle_kernel(*refs):
    half = len(refs) // 2
    for source, target in zip(refs[:half], refs[half:]):
        target[...] = source[...]


def output_kernel(att_ref, wout_ref, b_ref, out_ref):
    att = att_ref[...]
    for c in range(0, out_ref.shape[1], 256):
        cut = slice(c, c + 256)
        out_ref[:, cut] = (b_ref[:, cut].astype(F32) - dot(att, wout_ref[:, cut])).astype(BF16)


def key_kernel(layout, owner_ref, own_ref, cross_ref, inner_ref, pk_ref, out_ref, cross_out_ref, inner_out_ref):
    hidden = pk_ref.shape[1]
    first = first_half((128, 128))
    odd = is_odd()
    tile = this_tile(layout)
    last = TILES - 1
    use_prev = (tile > 0) & lists(owner_ref, jnp.maximum(tile - 1, 0), tile)
    use_next = (tile < last) & lists(owner_ref, jnp.minimum(tile + 1, last), tile)
    use_cross = (odd & use_next) | (~odd & use_prev)
    use_inner = (odd & use_prev) | (~odd & use_next)
    for at in range(0, 2 * hidden, 128):
        cut = slice(at, at + 128)
        total = own_ref[:, cut].astype(F32)
        total = total + jnp.where(use_cross, cross_ref[:, cut].astype(F32), 0.0)
        total = total + jnp.where(use_inner, inner_ref[:, cut].astype(F32), 0.0)
        if at < hidden:
            unit, inverse = pair_unit(pk_ref[:, cut].astype(F32), first)
            total = pair_unit_back(unit, inverse, total, first)
        total = total.astype(BF16)
        out_ref[:, cut] = total
        cross_out_ref[:, cut] = jnp.where(odd, total[ROW:], total[:ROW])
        inner_out_ref[:, cut] = jnp.where(odd, total[:ROW], total[ROW:])


def local_kernel(own_ref, gq_ref, w_ref, kern_ref, part_ref, acc_ref, ext_ref):
    hidden = gq_ref.shape[1]
    gq = gq_ref[...]
    for at in range(0, 2 * hidden, 128):
        cut = slice(at, at + 128)
        ext_ref[ROW : ROW + 128, :] = own_ref[:, cut].astype(F32)
        part_ref[:, cut] = pool_lanes(ext_ref, load_taps(kern_ref, cut), True, (1, 2))
        acc_ref[:, cut] = dot_nt(gq, w_ref[cut, :hidden])


def final_kernel(
    cross_ref, inner_ref, part_ref, acc_ref, w_ref, kern_ref, a_ref, ga_ref,
    out_ref, ext_ref, gp_ref, sum_ref,
):
    odd = is_odd()
    channels = part_ref.shape[1]
    hidden = channels // 2
    width = a_ref.shape[1]
    for at in range(0, channels, 128):
        cut = slice(at, at + 128)
        cross, inner = cross_ref[:, cut], inner_ref[:, cut]
        ext_ref[0:ROW, :] = jnp.where(odd, inner, cross).astype(F32)
        ext_ref[ROW + 128 :, :] = jnp.where(odd, cross, inner).astype(F32)
        pooled = pool_lanes(ext_ref, load_taps(kern_ref, cut), True, (0, 3))
        gp_ref[:, cut] = (part_ref[:, cut] + pooled).astype(BF16)
    grad_raw = gp_ref[...]
    for c in range(0, width, 256):
        cut = slice(c, c + 256)
        sum_ref[:, cut] = acc_ref[:, cut] + dot_nt(grad_raw, w_ref[cut, hidden:])
    normalized, inverse = normalize_rows(a_ref[...].astype(F32))
    grad = sum_ref[...]
    grad_mean = jnp.mean(grad, axis=-1, keepdims=True)
    cross_mean = jnp.mean(grad * normalized, axis=-1, keepdims=True)
    back = inverse * (grad - grad_mean - normalized * cross_mean)
    out_ref[...] = (ga_ref[...].astype(F32) + back).astype(BF16)


def grad_kernel(gb_ref, wout_ref, out_ref):
    gb = gb_ref[...]
    for c in range(0, out_ref.shape[1], 256):
        out_ref[:, c : c + 256] = dot_nt(gb, wout_ref[c : c + 256, :]).astype(BF16)


def call(kernel, name, outs, specs, flops, scratch=(), kind=BF16, limit=6):
    def run(*args):
        moved = sum(x.size * x.dtype.itemsize for x in args)
        args = [
            pltpu.with_memory_space_constraint(x, HBM) if space == HBM else x
            for x, space in zip(args, specs)
        ]
        return pl.pallas_call(
            kernel,
            name=name,
            out_shape=[jax.ShapeDtypeStruct(s, kind) for s in outs],
            in_specs=[pl.BlockSpec(memory_space=s) for s in specs],
            out_specs=[pl.BlockSpec(memory_space=VMEM) for _ in outs],
            scratch_shapes=list(scratch),
            compiler_params=pltpu.CompilerParams(vmem_limit_bytes=limit * 1024 * 1024),
            cost_estimate=pl.CostEstimate(flops=flops, bytes_accessed=moved, transcendentals=0),
        )(*args)

    return run


SECTIONS = 16
TILES = 16


def start_layout(section, x):
    return 0


def first_layout(section, x):
    return 0


def second_layout(section, x):
    return ((section & 7) + 1) >> 3


def place(layout, section, tile):
    return section * TILES + (tile ^ (2 * layout(section, tile // 4)))


AXES = ("section", "space")


def move(value, source, target, by):
    pairs = [
        (place(source, s, t), place(target, (s + by) % SECTIONS, t))
        for s in range(SECTIONS)
        for t in range(TILES)
    ]
    return lax.ppermute(value, AXES, pairs)


def swap_cross(value, source, target):
    pairs = []
    for s in range(SECTIONS):
        for t in range(1, TILES - 1, 2):
            pairs.append((place(source, s, t), place(target, s, t + 1)))
            pairs.append((place(source, s, t + 1), place(target, s, t)))
    return lax.ppermute(value, AXES, pairs)


def swap_inner(value, source, target):
    pairs = [(place(source, s, t), place(target, s, t ^ 1)) for s in range(SECTIONS) for t in range(TILES)]
    return lax.ppermute(value, AXES, pairs)


def exchange(cross, inner, source, target=None):
    target = target or source
    inner = swap_inner(inner, source, target)
    return swap_cross(cross, source, target), inner


def together(*values):
    return lax.optimization_barrier(values)


def edges(value):
    odd = lax.rem(lax.axis_index("space"), 2)
    cross = lax.dynamic_slice_in_dim(value, odd * ROW, ROW, 0)
    inner = lax.dynamic_slice_in_dim(value, (1 - odd) * ROW, ROW, 0)
    return cross, inner


def forward_project(a, w_qkv, halo):
    cross, inner = halo
    block, width = a.shape
    (proj,) = call(
        project_kernel, "project", [(block, w_qkv.shape[1])], [VMEM] * 2, 2 * block * width * w_qkv.shape[1]
    )(a, w_qkv)
    return proj, cross, inner


def first_project(a, w_qkv):
    block, width = a.shape
    columns = w_qkv.shape[1]
    return call(
        first_project_kernel, "firstproject", [(block, columns)], [HBM] * 2, 2 * block * width * columns,
        [VMEM(a.shape, BF16), VMEM(w_qkv.shape, BF16), VMEM((block, columns), F32), DMA((1,)), DMA((width // 256,))],
        limit=14,
    )(a, w_qkv)[0]


def forward_pool(proj, cross, inner, w_qkv, kern):
    block = proj.shape[0]
    hidden = proj.shape[1] // 3
    return call(
        pool_kernel, "pool", [(block, 2 * hidden), (block, hidden)], [VMEM] * 5,
        2 * block * w_qkv.shape[0] * 2 * hidden, [VMEM((256, 128), F32)],
    )(cross, inner, w_qkv, proj, kern)


def grad_attended(gb, w_out):
    block, width = gb.shape
    hidden = w_out.shape[0]
    return call(
        grad_kernel, "gradatt", [(block, hidden)], [VMEM] * 2, 2 * block * width * hidden
    )(gb, w_out)[0]


def attend(layout, owner, tau, proj, kv, cross, inner, grad):
    block, hidden = grad.shape
    return call(
        functools.partial(attention_kernel, layout), "attention",
        [(block, hidden), (block, hidden), (block, 2 * hidden), (block, 2 * hidden)],
        [SMEM] * 2 + [VMEM] * 5, 2 * block * 512 * hidden * 8,
    )(owner, tau, proj, kv, cross, inner, grad)


def attend_rebuild(layout, owner, tau, proj, kv, cross, inner, grad, w_out, b):
    block, hidden = grad.shape
    return call(
        functools.partial(attention_output_kernel, layout), "attendout",
        [(block, hidden), (block, hidden), (block, 2 * hidden), (block, 2 * hidden), b.shape],
        [SMEM] * 2 + [VMEM] * 5 + [HBM] * 2, 2 * block * 512 * hidden * 8,
        [VMEM(w_out.shape, BF16), VMEM(b.shape, BF16), DMA((2, 1))],
        limit=9,
    )(owner, tau, proj, kv, cross, inner, grad, w_out, b)


def settle(*values):
    return call(settle_kernel, "settle", [v.shape for v in values], [VMEM] * len(values), 1)(*values)


def rebuild(att, w_out, b):
    block, width = b.shape
    return call(
        output_kernel, "output", [(block, width)], [VMEM] * 3, 2 * block * width * w_out.shape[0]
    )(att, w_out, b)[0]


def key_sums(layout, owner, own, cross, inner, pk):
    block, channels = own.shape
    return call(
        functools.partial(key_kernel, layout), "keys",
        [(block, channels), (ROW, channels), (ROW, channels)],
        [SMEM] + [VMEM] * 4, block * channels * 40,
    )(owner, own, cross, inner, pk)


def finish_local(gpool, gq, w_qkv, kern):
    block, channels = gpool.shape
    width = w_qkv.shape[0]
    return call(
        local_kernel, "local", [(block, channels), (block, width)], [VMEM] * 4,
        2 * block * width * gq.shape[1], [VMEM((256, 128), F32)], F32,
    )(gpool, gq, w_qkv, kern)


def finish(cross, inner, part, acc, w_qkv, kern, a, ga):
    block, width = a.shape
    channels = part.shape[1]
    return call(
        final_kernel, "final", [(block, width)], [VMEM] * 8, 2 * block * width * channels,
        [
            VMEM((256, 128), F32),
            VMEM((block, channels), BF16),
            VMEM((block, width), F32),
        ],
    )(cross, inner, part, acc, w_qkv, kern, a, ga)[0]


def body(top_a, top_b, grad_a, grad_b, w_qkv, w_out, kernel, tau, owner):
    a, b, ga, gb = top_a[0], top_b[0], grad_a[0], grad_b[0]
    w_qkv, w_out, tau = w_qkv[0], w_out[0], tau[0]
    kern = jnp.transpose(kernel, (1, 0, 2))
    one, two, start = first_layout, second_layout, start_layout

    halo = exchange(*edges(a), start, one)
    b2 = move(a, one, two, -1)
    ga2 = move(gb, one, two, -1)
    proj1 = first_project(a, w_qkv)
    cross, inner = halo
    kv1, pk1 = forward_pool(proj1, cross, inner, w_qkv, kern)
    cross, inner = exchange(kv1, kv1, one)
    grad1 = grad_attended(gb, w_out)
    cross, inner, b2, ga2, grad1 = together(cross, inner, b2, ga2, grad1)
    _, gq1, own1, near1, rebuilt1 = attend_rebuild(
        one, owner, tau, proj1, kv1, cross, inner, grad1, w_out, b
    )
    cross, inner = exchange(near1, near1, one)
    a2 = move(rebuilt1, one, two, -1)
    gpool1, cross, inner = key_sums(one, owner, own1, cross, inner, pk1)
    cross, inner = exchange(cross, inner, one)
    part1, acc1 = finish_local(gpool1, gq1, w_qkv, kern)
    new_grad1 = finish(cross, inner, part1, acc1, w_qkv, kern, a, ga)

    proj2, cross, inner = forward_project(a2, w_qkv, exchange(*edges(a2), two))
    kv2, pk2 = forward_pool(proj2, cross, inner, w_qkv, kern)
    kv2, new_grad1 = together(kv2, new_grad1)
    gb2 = move(new_grad1, one, two, -1)
    cross, inner = exchange(kv2, kv2, two)
    grad2 = grad_attended(gb2, w_out)
    passed_a = move(gb2, two, start, -1)
    att2, gq2, own2, near2 = attend(two, owner, tau, proj2, kv2, cross, inner, grad2)
    cross, inner = exchange(near2, near2, two)
    att2, passed_a = together(att2, passed_a)
    rebuilt2 = rebuild(att2, w_out, b2)
    cross, inner, rebuilt2, late = together(cross, inner, rebuilt2, a2)
    rebuilt_b = move(late, two, start, -1)
    gpool2, cross, inner = key_sums(two, owner, own2, cross, inner, pk2)
    cross, inner = exchange(cross, inner, two)
    part2, acc2 = finish_local(gpool2, gq2, w_qkv, kern)
    cross, inner, rebuilt2, rebuilt_b = together(cross, inner, rebuilt2, rebuilt_b)
    rebuilt_a = move(rebuilt2, two, start, -1)
    new_grad2 = finish(cross, inner, part2, acc2, w_qkv, kern, a2, ga2)
    passed_b = move(new_grad2, two, start, -1)
    rebuilt_a, rebuilt_b, passed_a = settle(rebuilt_a, rebuilt_b, passed_a)
    return rebuilt_a[None], rebuilt_b[None], passed_a[None], passed_b[None]


def solution(mesh):
    state = P("section", "space", None)
    weights = P("section", None, None)
    return jax.shard_map(
        body,
        mesh=mesh,
        in_specs=(state,) * 4 + (weights,) * 3 + (P("section", None), P()),
        out_specs=(state,) * 4,
        check_vma=False,
    )
```

time: 172 us -> 147 us (0.85)
  the two profiles are of different devices: /device:TPU:6 before, /device:TPU:11 now
where the time goes in v2:
time: 147 us
  starting transfers between devices  64.7 us (44%)
  waiting for transfers between devices  37.5 us (26%)
  Pallas kernels  36 us (24%)
  local copies, waits for them, and re-layouts  7.44 us (5%)
    pallas_call x16, Pallas kernels, run(): pl.pallas_call(kernel, name=name, out_shape=[jax.ShapeDtypeStruct(s, kind...  36 us
    ppermute x8, starting transfers between devices, move(): return lax.ppermute(value, AXES, pairs)  30.3 us
    ppermute x8, starting transfers between devices, swap_cross(): return lax.ppermute(value, AXES, pairs)  28.1 us
    ppermute x8, waiting for transfers between devices, move(): return lax.ppermute(value, AXES, pairs)  26 us
    ppermute x8, waiting for transfers between devices, swap_cross(): return lax.ppermute(value, AXES, pairs)  11.4 us
    ppermute x8, starting transfers between devices, swap_inner(): return lax.ppermute(value, AXES, pairs)  6.29 us
    unnamed x32, local copies, waits for them, and re-layouts  6.21 us
  transfers between devices with their start and end apart: 24, of which 8 were waited for; matrix products, arithmetic and copies ran while one was open for 0% of the time, Pallas kernels for 16%

profile of v2, /device:TPU:11, one launch (start us, length us, event | category | flops | bytes accessed | tf_op | source)
XLA Modules:
  0.0 146.7 jit_solution(10805372283546693165)
XLA Ops:
  0.7 0.0 copy-start
  0.7 1.2 dynamic-slice_bitcast_fusion
  1.9 0.8 collective-permute-start.1
  2.6 3.2 %collective-permute-start = (bf16[64,1536]{1,0:T(8,128)(2,1)S(1)}, bf16[64,1536]{1,0:T(8,128)(2,1)S(1)}, u32[]{:S(2)}, u32[]{:S(2)}) collective-permute-start(bf16[64,1536]{1,0:T(8,128)(2,1)S(1)} %get-tuple-element.91), channel_id=1, source_target_pairs={{1,2},{2,1},{3,4},{4,3},{5,6},{6,5},{7,8},{8,7},{9,10},{10,9},{11,... | collective-permute-start | bytes 589832 | tf_op jit(solution)/shard_map/ppermute | solution.py:373
  5.8 6.6 %collective-permute-start.5 = (bf16[128,1536]{1,0:T(8,128)(2,1)}, bf16[128,1536]{1,0:T(8,128)(2,1)S(1)}, u32[]{:S(2)}, u32[]{:S(2)}) collective-permute-start(bf16[128,1536]{1,0:T(8,128)(2,1)} %bitcast.40), channel_id=1, source_target_pairs={{0,242},{1,243},{2,240},{3,241},{4,246},{5,247},{6,244},{7,245},{8... | collective-permute-start | bytes 1179656 | tf_op jit(solution)/shard_map/ppermute | solution.py:364
  12.4 0.7 collective-permute-start.4
  13.1 4.7 %firstproject.1.proj_ref.refs_2_ = bf16[128,2304]{1,0:T(8,128)(2,1)S(1)} custom-call(bf16[128,1536]{1,0:T(8,128)(2,1)} %bitcast.37, bf16[1536,2304]{1,0:T(8,128)(2,1)} %bitcast.16), custom_call_target="tpu_custom_call" | custom-call | flops 905969664 | bytes 7471104 | tf_op jit(solution)/shard_map/firstproject/pallas_call | solution.py:321
  17.8 0.0 copy-start.11
  17.8 0.0 collective-permute-done.1.inner_ref
  17.9 0.0 slice-start
  17.9 3.0 %pool.2 = (bf16[128,1536]{1,0:T(8,128)(2,1)}, bf16[128,768]{1,0:T(8,128)(2,1)S(1)}) custom-call(bf16[64,1536]{1,0:T(8,128)(2,1)S(1)} %collective-permute-done.cross_ref, bf16[64,1536]{1,0:T(8,128)(2,1)S(1)} %collective-permute-done.1.inner_ref, bf16[1536,2304]{1,0:T(8,128)(2,1)S(1)} %bitcast.17, bf16[128,2304]{1,0:T(8,128)(2,1)S(1)} %firstproject.1.proj_ref.refs_2_, ...), custom_call_target="tpu_custom_call" | custom-call | flops 603979776 | bytes 8226816 | tf_op jit(solution)/shard_map/pool/pallas_call | solution.py:321
  20.9 0.7 copy-done.9
  21.6 0.9 collective-permute-start.3
  22.5 4.0 %collective-permute-start.2 = (bf16[128,1536]{1,0:T(8,128)(2,1)}, bf16[128,1536]{1,0:T(8,128)(2,1)}, u32[]{:S(2)}, u32[]{:S(2)}) collective-permute-start(bf16[128,1536]{1,0:T(8,128)(2,1)} %get-tuple-element.46.refs_3_), channel_id=1, source_target_pairs={{1,2},{2,1},{3,4},{4,3},{5,6},{6,5},{7,8},{8,7},{9,10},{10,9},{11,... | collective-permute-start | bytes 1179656 | tf_op jit(solution)/shard_map/ppermute | solution.py:373
  26.5 0.1 copy.16.refs_0_.owner_ref
  26.6 1.7 %copy-done.1 = bf16[1,768,1536]{2,1,0:T(8,128)(2,1)S(1)} copy-done((bf16[1,768,1536]{2,1,0:T(8,128)(2,1)S(1)}, bf16[1,768,1536]{2,1,0:T(8,128)(2,1)}, u32[]{:S(2)}) %copy-start.1) | copy-done | bytes 2359320
  28.3 1.0 copy-done.8
  29.3 0.9 gradatt.2.refs_6_
  30.1 0.0 collective-permute-done.4.b_ref
  30.2 0.0 collective-permute-done.3.refs_5_
  30.2 2.7 %collective-permute-done.2.refs_4_ = bf16[128,1536]{1,0:T(8,128)(2,1)} collective-permute-done((bf16[128,1536]{1,0:T(8,128)(2,1)}, bf16[128,1536]{1,0:T(8,128)(2,1)}, u32[]{:S(2)}, u32[]{:S(2)}) %collective-permute-start.2) | collective-permute-done | bytes 393248 | tf_op jit(solution)/shard_map/ppermute | solution.py:373
  32.9 1.1 copy-done.5
  33.9 6.7 %attendout.1 = (bf16[128,768]{1,0:T(8,128)(2,1)}, bf16[128,768]{1,0:T(8,128)(2,1)S(1)}, bf16[128,1536]{1,0:T(8,128)(2,1)S(1)}, bf16[128,1536]{1,0:T(8,128)(2,1)S(1)}, bf16[128,1536]{1,0:T(8,128)(2,1)S(1)}) custom-call(s32[16,2]{1,0:T(8,128)S(1)} %copy.16.refs_0_.owner_ref, f32[12]{0:T(128)S(1)} %bitcast.42, bf16[128,2304]{1,0:T(8,128)(2,1)S(1)} %copy-done.5, ...), custom_call_target="tpu_custom_call" | custom-call | flops 805306368 | bytes 4718768 | tf_op jit(solution)/shard_map/attendout/pallas_call | solution.py:321
  40.6 4.0 %collective-permute-start.6 = (bf16[128,1536]{1,0:T(8,128)(2,1)S(1)}, bf16[128,1536]{1,0:T(8,128)(2,1)S(1)}, u32[]{:S(2)}, u32[]{:S(2)}) collective-permute-start(bf16[128,1536]{1,0:T(8,128)(2,1)S(1)} %get-tuple-element.50), channel_id=1, source_target_pairs={{0,242},{1,243},{2,240},{3,241},{4,246},{5,247},{6,244},{7,245},{8... | collective-permute-start | bytes 1179656 | tf_op jit(solution)/shard_map/ppermute | solution.py:364
  44.6 4.3 %collective-permute-start.9 = (bf16[128,1536]{1,0:T(8,128)(2,1)S(1)}, bf16[128,1536]{1,0:T(8,128)(2,1)S(1)}, u32[]{:S(2)}, u32[]{:S(2)}) collective-permute-start(bf16[128,1536]{1,0:T(8,128)(2,1)S(1)} %get-tuple-element.53), channel_id=1, source_target_pairs={{1,2},{2,1},{3,4},{4,3},{5,6},{6,5},{7,8},{8,7},{9,10},{10,9},{11,... | collective-permute-start | bytes 1179656 | tf_op jit(solution)/shard_map/ppermute | solution.py:373
  48.9 4.1 %collective-permute-done.6.a_ref = bf16[128,1536]{1,0:T(8,128)(2,1)S(1)} collective-permute-done((bf16[128,1536]{1,0:T(8,128)(2,1)S(1)}, bf16[128,1536]{1,0:T(8,128)(2,1)S(1)}, u32[]{:S(2)}, u32[]{:S(2)}) %collective-permute-start.6) | collective-permute-done | bytes 393248 | tf_op jit(solution)/shard_map/ppermute | solution.py:364
  53.0 0.3 collective-permute-start.8
  53.3 4.0 %collective-permute-start.7 = (bf16[64,1536]{1,0:T(8,128)(2,1)S(1)}, bf16[64,1536]{1,0:T(8,128)(2,1)S(1)}, u32[]{:S(2)}, u32[]{:S(2)}) collective-permute-start(bf16[64,1536]{1,0:T(8,128)(2,1)S(1)} %get-tuple-element.89), channel_id=1, source_target_pairs={{1,2},{2,1},{3,4},{4,3},{5,6},{6,5},{7,8},{8,7},{9,10},{10,9},{11,... | collective-permute-start | bytes 589832 | tf_op jit(solution)/shard_map/ppermute | solution.py:373
  57.4 0.0 copy-start.10
  57.4 0.9 copy-done.10
  58.3 1.6 %keys.2 = (bf16[128,1536]{1,0:T(8,128)(2,1)S(1)}, bf16[64,1536]{1,0:T(8,128)(2,1)S(1)}, bf16[64,1536]{1,0:T(8,128)(2,1)S(1)}) custom-call(s32[16,2]{1,0:T(8,128)S(1)} %copy.16.refs_0_.owner_ref, bf16[128,1536]{1,0:T(8,128)(2,1)S(1)} %get-tuple-element.52.own_ref, bf16[128,1536]{1,0:T(8,128)(2,1)S(1)} %collective-permute-done.9.cross_ref, ...), custom_call_target="tpu_custom_call" | custom-call | flops 7864320 | bytes 1376384 | tf_op jit(solution)/shard_map/keys/pallas_call | solution.py:321
  59.9 2.4 %collective-permute-start.11 = (bf16[64,1536]{1,0:T(8,128)(2,1)S(1)}, bf16[64,1536]{1,0:T(8,128)(2,1)S(1)}, u32[]{:S(2)}, u32[]{:S(2)}) collective-permute-start(bf16[64,1536]{1,0:T(8,128)(2,1)S(1)} %get-tuple-element.55), channel_id=1, source_target_pairs={{1,2},{2,1},{3,4},{4,3},{5,6},{6,5},{7,8},{8,7},{9,10},{10,9},{11,... | collective-permute-start | bytes 589832 | tf_op jit(solution)/shard_map/ppermute | solution.py:373
  62.4 2.4 %collective-permute-start.12 = (bf16[64,1536]{1,0:T(8,128)(2,1)S(1)}, bf16[64,1536]{1,0:T(8,128)(2,1)S(1)}, u32[]{:S(2)}, u32[]{:S(2)}) collective-permute-start(bf16[64,1536]{1,0:T(8,128)(2,1)S(1)} %get-tuple-element.56), channel_id=1, source_target_pairs={{0,1},{1,0},{2,3},{3,2},{4,5},{5,4},{6,7},{7,6},{8,9},{9,8},{10,11... | collective-permute-start | bytes 589832 | tf_op jit(solution)/shard_map/ppermute | solution.py:378
  64.7 1.0 local.2
  65.7 0.0 copy-start.6
  65.8 0.0 copy-start.7
  65.8 1.3 project.1.proj_ref
  67.1 2.3 %pool.3 = (bf16[128,1536]{1,0:T(8,128)(2,1)S(1)}, bf16[128,768]{1,0:T(8,128)(2,1)S(1)}) custom-call(bf16[64,1536]{1,0:T(8,128)(2,1)S(1)} %collective-permute-done.7.cross_ref, bf16[64,1536]{1,0:T(8,128)(2,1)S(1)} %collective-permute-done.8.inner_ref, bf16[1536,2304]{1,0:T(8,128)(2,1)S(1)} %bitcast.22, bf16[128,2304]{1,0:T(8,128)(2,1)S(1)} %project.1.proj_ref, ...), custom_call_target="tpu_custom_call" | custom-call | flops 603979776 | bytes 8226816 | tf_op jit(solution)/shard_map/pool/pallas_call | solution.py:321
  69.4 0.0 copy-start.2
  69.5 2.2 %final.2 = bf16[128,1536]{1,0:T(8,128)(2,1)S(1)} custom-call(bf16[64,1536]{1,0:T(8,128)(2,1)S(1)} %collective-permute-done.11.cross_ref, bf16[64,1536]{1,0:T(8,128)(2,1)S(1)} %collective-permute-done.12.inner_ref, f32[128,1536]{1,0:T(8,128)S(1)} %get-tuple-element.59.part_ref, f32[128,1536]{1,0:T(8,128)S(1)} %get-tuple-element.60.acc_ref, ...), custom_call_target="tpu_custom_call" | custom-call | flops 603979776 | bytes 9996288 | tf_op jit(solution)/shard_map/final/pallas_call | solution.py:321
  71.6 4.5 %collective-permute-start.15 = (bf16[128,1536]{1,0:T(8,128)(2,1)S(1)}, bf16[128,1536]{1,0:T(8,128)(2,1)S(1)}, u32[]{:S(2)}, u32[]{:S(2)}) collective-permute-start(bf16[128,1536]{1,0:T(8,128)(2,1)S(1)} %final.2), channel_id=1, source_target_pairs={{0,242},{1,243},{2,240},{3,241},{4,246},{5,247},{6,244},{7,245},{8... | collective-permute-start | bytes 1179656 | tf_op jit(solution)/shard_map/ppermute | solution.py:364
  76.1 3.5 %collective-permute-start.13 = (bf16[128,1536]{1,0:T(8,128)(2,1)S(1)}, bf16[128,1536]{1,0:T(8,128)(2,1)S(1)}, u32[]{:S(2)}, u32[]{:S(2)}) collective-permute-start(bf16[128,1536]{1,0:T(8,128)(2,1)S(1)} %get-tuple-element.61.own_ref), channel_id=1, source_target_pairs={{1,2},{2,1},{3,4},{4,3},{5,6},{6,5},{7,8},{8,7},{9,10},{10,9},{11,... | collective-permute-start | bytes 1179656 | tf_op jit(solution)/shard_map/ppermute | solution.py:373
  79.6 4.6 %collective-permute-done.15.gb_ref = bf16[128,1536]{1,0:T(8,128)(2,1)S(1)} collective-permute-done((bf16[128,1536]{1,0:T(8,128)(2,1)S(1)}, bf16[128,1536]{1,0:T(8,128)(2,1)S(1)}, u32[]{:S(2)}, u32[]{:S(2)}) %collective-permute-start.15) | collective-permute-done | bytes 393248 | tf_op jit(solution)/shard_map/ppermute | solution.py:364
  84.2 4.5 %collective-permute-start.18 = (bf16[128,1536]{1,0:T(8,128)(2,1)S(1)}, bf16[128,1536]{1,0:T(8,128)(2,1)S(1)}, u32[]{:S(2)}, u32[]{:S(2)}) collective-permute-start(bf16[128,1536]{1,0:T(8,128)(2,1)S(1)} %collective-permute-done.15.gb_ref), channel_id=1, source_target_pairs={{0,240},{1,241},{2,242},{3,243},{4,244},{5,245},{6,246},{7,247},{8... | collective-permute-start | bytes 1179656 | tf_op jit(solution)/shard_map/ppermute | solution.py:364
  88.7 0.9 gradatt.3.grad_ref
  89.6 4.3 %attention.1 = (bf16[128,768]{1,0:T(8,128)(2,1)S(1)}, bf16[128,768]{1,0:T(8,128)(2,1)S(1)}, bf16[128,1536]{1,0:T(8,128)(2,1)S(1)}, bf16[128,1536]{1,0:T(8,128)(2,1)S(1)}) custom-call(s32[16,2]{1,0:T(8,128)S(1)} %copy.16.refs_0_.owner_ref, f32[12]{0:T(128)S(1)} %bitcast.43, bf16[128,2304]{1,0:T(8,128)(2,1)S(1)} %project.1.proj_ref, ...), custom_call_target="tpu_custom_call" | custom-call | flops 805306368 | bytes 1966256 | tf_op jit(solution)/shard_map/attention/pallas_call | solution.py:321
  93.9 1.9 %collective-permute-start.17 = (bf16[128,1536]{1,0:T(8,128)(2,1)S(1)}, bf16[128,1536]{1,0:T(8,128)(2,1)S(1)}, u32[]{:S(2)}, u32[]{:S(2)}) collective-permute-start(bf16[128,1536]{1,0:T(8,128)(2,1)S(1)} %get-tuple-element.64), channel_id=1, source_target_pairs={{0,1},{1,0},{2,3},{3,2},{4,5},{5,4},{6,7},{7,6},{8,9},{9,8},{10,11... | collective-permute-start | bytes 1179656 | tf_op jit(solution)/shard_map/ppermute | solution.py:378
  95.7 2.5 %collective-permute-start.16 = (bf16[128,1536]{1,0:T(8,128)(2,1)S(1)}, bf16[128,1536]{1,0:T(8,128)(2,1)S(1)}, u32[]{:S(2)}, u32[]{:S(2)}) collective-permute-start(bf16[128,1536]{1,0:T(8,128)(2,1)S(1)} %get-tuple-element.64), channel_id=1, source_target_pairs={{1,2},{2,1},{3,4},{4,3},{5,6},{6,5},{7,8},{8,7},{9,10},{10,9},{11,... | collective-permute-start | bytes 1179656 | tf_op jit(solution)/shard_map/ppermute | solution.py:373
  98.3 1.5 %output.1 = bf16[128,1536]{1,0:T(8,128)(2,1)S(1)} custom-call(bf16[128,768]{1,0:T(8,128)(2,1)S(1)} %get-tuple-element.66.att_ref, bf16[768,1536]{1,0:T(8,128)(2,1)S(1)} %bitcast.29, bf16[128,1536]{1,0:T(8,128)(2,1)} %collective-permute-done.4.b_ref), custom_call_target="tpu_custom_call" | custom-call | flops 301989888 | bytes 2949120 | tf_op jit(solution)/shard_map/output/pallas_call | solution.py:321
  99.8 6.0 %collective-permute-done.16.cross_ref = bf16[128,1536]{1,0:T(8,128)(2,1)S(1)} collective-permute-done((bf16[128,1536]{1,0:T(8,128)(2,1)S(1)}, bf16[128,1536]{1,0:T(8,128)(2,1)S(1)}, u32[]{:S(2)}, u32[]{:S(2)}) %collective-permute-start.16) | collective-permute-done | bytes 393248 | tf_op jit(solution)/shard_map/ppermute | solution.py:373
  105.8 4.2 %collective-permute-start.21 = (bf16[128,1536]{1,0:T(8,128)(2,1)S(1)}, bf16[128,1536]{1,0:T(8,128)(2,1)S(1)}, u32[]{:S(2)}, u32[]{:S(2)}) collective-permute-start(bf16[128,1536]{1,0:T(8,128)(2,1)S(1)} %collective-permute-done.6.a_ref), channel_id=1, source_target_pairs={{0,240},{1,241},{2,242},{3,243},{4,244},{5,245},{6,246},{7,247},{8... | collective-permute-start | bytes 1179656 | tf_op jit(solution)/shard_map/ppermute | solution.py:364
  110.1 1.6 %keys.3 = (bf16[128,1536]{1,0:T(8,128)(2,1)S(1)}, bf16[64,1536]{1,0:T(8,128)(2,1)S(1)}, bf16[64,1536]{1,0:T(8,128)(2,1)S(1)}) custom-call(s32[16,2]{1,0:T(8,128)S(1)} %copy.16.refs_0_.owner_ref, bf16[128,1536]{1,0:T(8,128)(2,1)S(1)} %get-tuple-element.63.own_ref, bf16[128,1536]{1,0:T(8,128)(2,1)S(1)} %collective-permute-done.16.cross_ref, ...), custom_call_target="tpu_custom_call" | custom-call | flops 7864320 | bytes 1376384 | tf_op jit(solution)/shard_map/keys/pallas_call | solution.py:321
  111.7 4.1 %collective-permute-start.19 = (bf16[64,1536]{1,0:T(8,128)(2,1)S(1)}, bf16[64,1536]{1,0:T(8,128)(2,1)S(1)}, u32[]{:S(2)}, u32[]{:S(2)}) collective-permute-start(bf16[64,1536]{1,0:T(8,128)(2,1)S(1)} %get-tuple-element.71), channel_id=1, source_target_pairs={{1,2},{2,1},{3,4},{4,3},{5,6},{6,5},{7,8},{8,7},{9,10},{10,9},{11,... | collective-permute-start | bytes 589832 | tf_op jit(solution)/shard_map/ppermute | solution.py:373
  115.8 0.1 collective-permute-start.20
  115.9 1.0 local.3
  116.8 2.7 %collective-permute-done.19.cross_ref = bf16[64,1536]{1,0:T(8,128)(2,1)S(1)} collective-permute-done((bf16[64,1536]{1,0:T(8,128)(2,1)S(1)}, bf16[64,1536]{1,0:T(8,128)(2,1)S(1)}, u32[]{:S(2)}, u32[]{:S(2)}) %collective-permute-start.19) | collective-permute-done | bytes 196640 | tf_op jit(solution)/shard_map/ppermute | solution.py:373
  119.5 0.4 collective-permute-done.21.refs_1_
  119.9 2.2 %final.3 = bf16[128,1536]{1,0:T(8,128)(2,1)S(1)} custom-call(bf16[64,1536]{1,0:T(8,128)(2,1)S(1)} %collective-permute-done.19.cross_ref, bf16[64,1536]{1,0:T(8,128)(2,1)S(1)} %collective-permute-done.20.inner_ref, f32[128,1536]{1,0:T(8,128)S(1)} %get-tuple-element.85.part_ref, f32[128,1536]{1,0:T(8,128)S(1)} %get-tuple-element.86.acc_ref, ...), custom_call_target="tpu_custom_call" | custom-call | flops 603979776 | bytes 9996288 | tf_op jit(solution)/shard_map/final/pallas_call | solution.py:321
  122.1 5.7 %collective-permute-start.23 = (bf16[128,1536]{1,0:T(8,128)(2,1)S(1)}, bf16[128,1536]{1,0:T(8,128)(2,1)S(1)}, u32[]{:S(2)}, u32[]{:S(2)}) collective-permute-start(bf16[128,1536]{1,0:T(8,128)(2,1)S(1)} %final.3), channel_id=1, source_target_pairs={{0,240},{1,241},{2,242},{3,243},{4,244},{5,245},{6,246},{7,247},{8... | collective-permute-start | bytes 1179656 | tf_op jit(solution)/shard_map/ppermute | solution.py:364
  127.8 0.1 collective-permute-start.22
  127.9 8.6 %collective-permute-done.23 = bf16[128,1536]{1,0:T(8,128)(2,1)S(1)} collective-permute-done((bf16[128,1536]{1,0:T(8,128)(2,1)S(1)}, bf16[128,1536]{1,0:T(8,128)(2,1)S(1)}, u32[]{:S(2)}, u32[]{:S(2)}) %collective-permute-start.23) | collective-permute-done | bytes 393248 | tf_op jit(solution)/shard_map/ppermute | solution.py:364
  136.4 8.4 %collective-permute-done.22.refs_0_ = bf16[128,1536]{1,0:T(8,128)(2,1)S(1)} collective-permute-done((bf16[128,1536]{1,0:T(8,128)(2,1)S(1)}, bf16[128,1536]{1,0:T(8,128)(2,1)S(1)}, u32[]{:S(2)}, u32[]{:S(2)}) %collective-permute-start.22) | collective-permute-done | bytes 393248 | tf_op jit(solution)/shard_map/ppermute | solution.py:364
  144.9 1.1 settle.1
  145.9 0.7 copy.18
  (35 shorter events, 0.1 us)
Async XLA Ops:
  0.6 17.2 %copy-start.3 = (f32[1,27,1536]{2,0,1:T(1,128)S(1)}, f32[1,27,1536]{2,0,1:T(1,128)}, u32[]{:S(2)}) copy-start(f32[1,27,1536]{2,0,1:T(1,128)} %param.15) | copy-start | bytes 497668
  0.7 17.2 %copy-start = (bf16[1,1536,2304]{2,1,0:T(8,128)(2,1)S(1)}, bf16[1,1536,2304]{2,1,0:T(8,128)(2,1)}, u32[]{:S(2)}) copy-start(bf16[1,1536,2304]{2,1,0:T(8,128)(2,1)} %param.13) | copy-start | bytes 21233668
  1.9 16.0 %collective-permute-start.1 = (bf16[64,1536]{1,0:T(8,128)(2,1)S(1)}, bf16[64,1536]{1,0:T(8,128)(2,1)S(1)}, u32[]{:S(2)}, u32[]{:S(2)}) collective-permute-start(bf16[64,1536]{1,0:T(8,128)(2,1)S(1)} %get-tuple-element.90), channel_id=1, source_target_pairs={{0,1},{1,0},{2,3},{3,2},{4,5},{5,4},{6,7},{7,6},{8,9},{9,8},{10,11... | collective-permute-start | bytes 589832 | tf_op jit(solution)/shard_map/ppermute | solution.py:378
  2.6 15.2 %collective-permute-start = (bf16[64,1536]{1,0:T(8,128)(2,1)S(1)}, bf16[64,1536]{1,0:T(8,128)(2,1)S(1)}, u32[]{:S(2)}, u32[]{:S(2)}) collective-permute-start(bf16[64,1536]{1,0:T(8,128)(2,1)S(1)} %get-tuple-element.91), channel_id=1, source_target_pairs={{1,2},{2,1},{3,4},{4,3},{5,6},{6,5},{7,8},{8,7},{9,10},{10,9},{11,... | collective-permute-start | bytes 589832 | tf_op jit(solution)/shard_map/ppermute | solution.py:373
  5.8 24.3 %collective-permute-start.5 = (bf16[128,1536]{1,0:T(8,128)(2,1)}, bf16[128,1536]{1,0:T(8,128)(2,1)S(1)}, u32[]{:S(2)}, u32[]{:S(2)}) collective-permute-start(bf16[128,1536]{1,0:T(8,128)(2,1)} %bitcast.40), channel_id=1, source_target_pairs={{0,242},{1,243},{2,240},{3,241},{4,246},{5,247},{6,244},{7,245},{8... | collective-permute-start | bytes 1179656 | tf_op jit(solution)/shard_map/ppermute | solution.py:364
  12.4 17.8 %collective-permute-start.4 = (bf16[128,1536]{1,0:T(8,128)(2,1)}, bf16[128,1536]{1,0:T(8,128)(2,1)}, u32[]{:S(2)}, u32[]{:S(2)}) collective-permute-start(bf16[128,1536]{1,0:T(8,128)(2,1)} %bitcast.36), channel_id=1, source_target_pairs={{0,242},{1,243},{2,240},{3,241},{4,246},{5,247},{6,244},{7,245},{8... | collective-permute-start | bytes 1179656 | tf_op jit(solution)/shard_map/ppermute | solution.py:364
  13.1 13.4 %copy-start.12 = (s32[16,2]{0,1:T(2,128)S(1)}, s32[16,2]{0,1:T(2,128)}, u32[]{:S(2)}) copy-start(s32[16,2]{0,1:T(2,128)} %param.17) | copy-start | bytes 388
  17.8 3.1 %copy-start.4 = (bf16[128,2304]{1,0:T(8,128)(2,1)}, bf16[128,2304]{1,0:T(8,128)(2,1)S(1)}, u32[]{:S(2)}) copy-start(bf16[128,2304]{1,0:T(8,128)(2,1)S(1)} %firstproject.1.proj_ref.refs_2_) | copy-start | bytes 1769476
  17.8 15.1 %copy-start.11 = (f32[1,12]{1,0:T(1,128)S(1)}, f32[1,12]{1,0:T(1,128)}, u32[]{:S(2)}) copy-start(f32[1,12]{1,0:T(1,128)} %param.16) | copy-start | bytes 148
  17.9 46.9 %slice-start = ((s8[7077888]{0:T(1024)(128)(4,1)}), s8[2883584]{0:T(1024)(128)(4,1)S(1)}, s32[]{:S(2)}) async-start(s8[7077888]{0:T(1024)(128)(4,1)} %bitcast.18), calls=%async_computation | async-start | bytes 5767168
  20.9 0.7 copy-start.9
  21.6 8.6 %collective-permute-start.3 = (bf16[128,1536]{1,0:T(8,128)(2,1)}, bf16[128,1536]{1,0:T(8,128)(2,1)}, u32[]{:S(2)}, u32[]{:S(2)}) collective-permute-start(bf16[128,1536]{1,0:T(8,128)(2,1)} %get-tuple-element.46.refs_3_), channel_id=1, source_target_pairs={{0,1},{1,0},{2,3},{3,2},{4,5},{5,4},{6,7},{7,6},{8,9},{9,8},{10,11... | collective-permute-start | bytes 1179656 | tf_op jit(solution)/shard_map/ppermute | solution.py:378
  22.5 10.4 %collective-permute-start.2 = (bf16[128,1536]{1,0:T(8,128)(2,1)}, bf16[128,1536]{1,0:T(8,128)(2,1)}, u32[]{:S(2)}, u32[]{:S(2)}) collective-permute-start(bf16[128,1536]{1,0:T(8,128)(2,1)} %get-tuple-element.46.refs_3_), channel_id=1, source_target_pairs={{1,2},{2,1},{3,4},{4,3},{5,6},{6,5},{7,8},{8,7},{9,10},{10,9},{11,... | collective-permute-start | bytes 1179656 | tf_op jit(solution)/shard_map/ppermute | solution.py:373
  26.6 1.7 %copy-start.1 = (bf16[1,768,1536]{2,1,0:T(8,128)(2,1)S(1)}, bf16[1,768,1536]{2,1,0:T(8,128)(2,1)}, u32[]{:S(2)}) copy-start(bf16[1,768,1536]{2,1,0:T(8,128)(2,1)} %param.14) | copy-start | bytes 7077892
  28.3 1.0 copy-start.8
  29.3 35.5 %slice-start.1 = ((s8[7077888]{0:T(1024)(128)(4,1)}), s8[4194304]{0:T(1024)(128)(4,1)S(1)}, s32[]{:S(2)}) async-start(s8[7077888]{0:T(1024)(128)(4,1)} %bitcast.18), calls=%async_computation.1 | async-start | bytes 8388608
  32.9 1.1 copy-start.5
  40.6 12.4 %collective-permute-start.6 = (bf16[128,1536]{1,0:T(8,128)(2,1)S(1)}, bf16[128,1536]{1,0:T(8,128)(2,1)S(1)}, u32[]{:S(2)}, u32[]{:S(2)}) collective-permute-start(bf16[128,1536]{1,0:T(8,128)(2,1)S(1)} %get-tuple-element.50), channel_id=1, source_target_pairs={{0,242},{1,243},{2,240},{3,241},{4,246},{5,247},{6,244},{7,245},{8... | collective-permute-start | bytes 1179656 | tf_op jit(solution)/shard_map/ppermute | solution.py:364
  44.6 12.7 %collective-permute-start.10 = (bf16[128,1536]{1,0:T(8,128)(2,1)S(1)}, bf16[128,1536]{1,0:T(8,128)(2,1)S(1)}, u32[]{:S(2)}, u32[]{:S(2)}) collective-permute-start(bf16[128,1536]{1,0:T(8,128)(2,1)S(1)} %get-tuple-element.53), channel_id=1, source_target_pairs={{0,1},{1,0},{2,3},{3,2},{4,5},{5,4},{6,7},{7,6},{8,9},{9,8},{10,11... | collective-permute-start | bytes 1179656 | tf_op jit(solution)/shard_map/ppermute | solution.py:378
  44.6 12.7 %collective-permute-start.9 = (bf16[128,1536]{1,0:T(8,128)(2,1)S(1)}, bf16[128,1536]{1,0:T(8,128)(2,1)S(1)}, u32[]{:S(2)}, u32[]{:S(2)}) collective-permute-start(bf16[128,1536]{1,0:T(8,128)(2,1)S(1)} %get-tuple-element.53), channel_id=1, source_target_pairs={{1,2},{2,1},{3,4},{4,3},{5,6},{6,5},{7,8},{8,7},{9,10},{10,9},{11,... | collective-permute-start | bytes 1179656 | tf_op jit(solution)/shard_map/ppermute | solution.py:373
  53.0 14.1 %collective-permute-start.8 = (bf16[64,1536]{1,0:T(8,128)(2,1)S(1)}, bf16[64,1536]{1,0:T(8,128)(2,1)S(1)}, u32[]{:S(2)}, u32[]{:S(2)}) collective-permute-start(bf16[64,1536]{1,0:T(8,128)(2,1)S(1)} %get-tuple-element.88), channel_id=1, source_target_pairs={{0,1},{1,0},{2,3},{3,2},{4,5},{5,4},{6,7},{7,6},{8,9},{9,8},{10,11... | collective-permute-start | bytes 589832 | tf_op jit(solution)/shard_map/ppermute | solution.py:378
  53.3 13.8 %collective-permute-start.7 = (bf16[64,1536]{1,0:T(8,128)(2,1)S(1)}, bf16[64,1536]{1,0:T(8,128)(2,1)S(1)}, u32[]{:S(2)}, u32[]{:S(2)}) collective-permute-start(bf16[64,1536]{1,0:T(8,128)(2,1)S(1)} %get-tuple-element.89), channel_id=1, source_target_pairs={{1,2},{2,1},{3,4},{4,3},{5,6},{6,5},{7,8},{8,7},{9,10},{10,9},{11,... | collective-permute-start | bytes 589832 | tf_op jit(solution)/shard_map/ppermute | solution.py:373
  57.4 0.9 copy-start.10
  59.9 9.5 %collective-permute-start.11 = (bf16[64,1536]{1,0:T(8,128)(2,1)S(1)}, bf16[64,1536]{1,0:T(8,128)(2,1)S(1)}, u32[]{:S(2)}, u32[]{:S(2)}) collective-permute-start(bf16[64,1536]{1,0:T(8,128)(2,1)S(1)} %get-tuple-element.55), channel_id=1, source_target_pairs={{1,2},{2,1},{3,4},{4,3},{5,6},{6,5},{7,8},{8,7},{9,10},{10,9},{11,... | collective-permute-start | bytes 589832 | tf_op jit(solution)/shard_map/ppermute | solution.py:373
  62.4 7.1 %collective-permute-start.12 = (bf16[64,1536]{1,0:T(8,128)(2,1)S(1)}, bf16[64,1536]{1,0:T(8,128)(2,1)S(1)}, u32[]{:S(2)}, u32[]{:S(2)}) collective-permute-start(bf16[64,1536]{1,0:T(8,128)(2,1)S(1)} %get-tuple-element.56), channel_id=1, source_target_pairs={{0,1},{1,0},{2,3},{3,2},{4,5},{5,4},{6,7},{7,6},{8,9},{9,8},{10,11... | collective-permute-start | bytes 589832 | tf_op jit(solution)/shard_map/ppermute | solution.py:378
  65.7 3.7 %copy-start.6 = (bf16[1,128,1536]{2,1,0:T(8,128)(2,1)S(1)}, bf16[1,128,1536]{2,1,0:T(8,128)(2,1)}, u32[]{:S(2)}) copy-start(bf16[1,128,1536]{2,1,0:T(8,128)(2,1)} %param.9) | copy-start | bytes 1179652
  65.8 3.7 %copy-start.7 = (bf16[1,128,1536]{2,1,0:T(8,128)(2,1)S(1)}, bf16[1,128,1536]{2,1,0:T(8,128)(2,1)}, u32[]{:S(2)}) copy-start(bf16[1,128,1536]{2,1,0:T(8,128)(2,1)} %param.11) | copy-start | bytes 1179652
  69.4 19.3 %copy-start.2 = (bf16[1,768,1536]{2,1,0:T(8,128)(2,1)S(1)}, bf16[1,768,1536]{2,1,0:T(8,128)(2,1)}, u32[]{:S(2)}) copy-start(bf16[1,768,1536]{2,1,0:T(8,128)(2,1)} %param.14) | copy-start | bytes 7077892
  71.6 12.6 %collective-permute-start.15 = (bf16[128,1536]{1,0:T(8,128)(2,1)S(1)}, bf16[128,1536]{1,0:T(8,128)(2,1)S(1)}, u32[]{:S(2)}, u32[]{:S(2)}) collective-permute-start(bf16[128,1536]{1,0:T(8,128)(2,1)S(1)} %final.2), channel_id=1, source_target_pairs={{0,242},{1,243},{2,240},{3,241},{4,246},{5,247},{6,244},{7,245},{8... | collective-permute-start | bytes 1179656 | tf_op jit(solution)/shard_map/ppermute | solution.py:364
  76.1 13.5 %collective-permute-start.14 = (bf16[128,1536]{1,0:T(8,128)(2,1)S(1)}, bf16[128,1536]{1,0:T(8,128)(2,1)S(1)}, u32[]{:S(2)}, u32[]{:S(2)}) collective-permute-start(bf16[128,1536]{1,0:T(8,128)(2,1)S(1)} %get-tuple-element.61.own_ref), channel_id=1, source_target_pairs={{0,1},{1,0},{2,3},{3,2},{4,5},{5,4},{6,7},{7,6},{8,9},{9,8},{10,11... | collective-permute-start | bytes 1179656 | tf_op jit(solution)/shard_map/ppermute | solution.py:378
  76.1 13.5 %collective-permute-start.13 = (bf16[128,1536]{1,0:T(8,128)(2,1)S(1)}, bf16[128,1536]{1,0:T(8,128)(2,1)S(1)}, u32[]{:S(2)}, u32[]{:S(2)}) collective-permute-start(bf16[128,1536]{1,0:T(8,128)(2,1)S(1)} %get-tuple-element.61.own_ref), channel_id=1, source_target_pairs={{1,2},{2,1},{3,4},{4,3},{5,6},{6,5},{7,8},{8,7},{9,10},{10,9},{11,... | collective-permute-start | bytes 1179656 | tf_op jit(solution)/shard_map/ppermute | solution.py:373
  84.2 14.1 %collective-permute-start.18 = (bf16[128,1536]{1,0:T(8,128)(2,1)S(1)}, bf16[128,1536]{1,0:T(8,128)(2,1)S(1)}, u32[]{:S(2)}, u32[]{:S(2)}) collective-permute-start(bf16[128,1536]{1,0:T(8,128)(2,1)S(1)} %collective-permute-done.15.gb_ref), channel_id=1, source_target_pairs={{0,240},{1,241},{2,242},{3,243},{4,244},{5,245},{6,246},{7,247},{8... | collective-permute-start | bytes 1179656 | tf_op jit(solution)/shard_map/ppermute | solution.py:364
  93.9 5.9 %collective-permute-start.17 = (bf16[128,1536]{1,0:T(8,128)(2,1)S(1)}, bf16[128,1536]{1,0:T(8,128)(2,1)S(1)}, u32[]{:S(2)}, u32[]{:S(2)}) collective-permute-start(bf16[128,1536]{1,0:T(8,128)(2,1)S(1)} %get-tuple-element.64), channel_id=1, source_target_pairs={{0,1},{1,0},{2,3},{3,2},{4,5},{5,4},{6,7},{7,6},{8,9},{9,8},{10,11... | collective-permute-start | bytes 1179656 | tf_op jit(solution)/shard_map/ppermute | solution.py:378
  95.7 10.1 %collective-permute-start.16 = (bf16[128,1536]{1,0:T(8,128)(2,1)S(1)}, bf16[128,1536]{1,0:T(8,128)(2,1)S(1)}, u32[]{:S(2)}, u32[]{:S(2)}) collective-permute-start(bf16[128,1536]{1,0:T(8,128)(2,1)S(1)} %get-tuple-element.64), channel_id=1, source_target_pairs={{1,2},{2,1},{3,4},{4,3},{5,6},{6,5},{7,8},{8,7},{9,10},{10,9},{11,... | collective-permute-start | bytes 1179656 | tf_op jit(solution)/shard_map/ppermute | solution.py:373
  105.8 14.1 %collective-permute-start.21 = (bf16[128,1536]{1,0:T(8,128)(2,1)S(1)}, bf16[128,1536]{1,0:T(8,128)(2,1)S(1)}, u32[]{:S(2)}, u32[]{:S(2)}) collective-permute-start(bf16[128,1536]{1,0:T(8,128)(2,1)S(1)} %collective-permute-done.6.a_ref), channel_id=1, source_target_pairs={{0,240},{1,241},{2,242},{3,243},{4,244},{5,245},{6,246},{7,247},{8... | collective-permute-start | bytes 1179656 | tf_op jit(solution)/shard_map/ppermute | solution.py:364
  111.7 7.9 %collective-permute-start.19 = (bf16[64,1536]{1,0:T(8,128)(2,1)S(1)}, bf16[64,1536]{1,0:T(8,128)(2,1)S(1)}, u32[]{:S(2)}, u32[]{:S(2)}) collective-permute-start(bf16[64,1536]{1,0:T(8,128)(2,1)S(1)} %get-tuple-element.71), channel_id=1, source_target_pairs={{1,2},{2,1},{3,4},{4,3},{5,6},{6,5},{7,8},{8,7},{9,10},{10,9},{11,... | collective-permute-start | bytes 589832 | tf_op jit(solution)/shard_map/ppermute | solution.py:373
  115.8 3.8 %collective-permute-start.20 = (bf16[64,1536]{1,0:T(8,128)(2,1)S(1)}, bf16[64,1536]{1,0:T(8,128)(2,1)S(1)}, u32[]{:S(2)}, u32[]{:S(2)}) collective-permute-start(bf16[64,1536]{1,0:T(8,128)(2,1)S(1)} %get-tuple-element.72), channel_id=1, source_target_pairs={{0,1},{1,0},{2,3},{3,2},{4,5},{5,4},{6,7},{7,6},{8,9},{9,8},{10,11... | collective-permute-start | bytes 589832 | tf_op jit(solution)/shard_map/ppermute | solution.py:378
  122.1 14.3 %collective-permute-start.23 = (bf16[128,1536]{1,0:T(8,128)(2,1)S(1)}, bf16[128,1536]{1,0:T(8,128)(2,1)S(1)}, u32[]{:S(2)}, u32[]{:S(2)}) collective-permute-start(bf16[128,1536]{1,0:T(8,128)(2,1)S(1)} %final.3), channel_id=1, source_target_pairs={{0,240},{1,241},{2,242},{3,243},{4,244},{5,245},{6,246},{7,247},{8... | collective-permute-start | bytes 1179656 | tf_op jit(solution)/shard_map/ppermute | solution.py:364
  127.8 17.1 %collective-permute-start.22 = (bf16[128,1536]{1,0:T(8,128)(2,1)S(1)}, bf16[128,1536]{1,0:T(8,128)(2,1)S(1)}, u32[]{:S(2)}, u32[]{:S(2)}) collective-permute-start(bf16[128,1536]{1,0:T(8,128)(2,1)S(1)} %output.1), channel_id=1, source_target_pairs={{0,240},{1,241},{2,242},{3,243},{4,244},{5,245},{6,246},{7,247},{8... | collective-permute-start | bytes 1179656 | tf_op jit(solution)/shard_map/ppermute | solution.py:364

commit v3 on v2

--- a/solution.py
+++ b/solution.py
@@ -117,14 +117,21 @@
 WHOLE = [(slice(None), slice(None))]
 
 
-def project_kernel(a_ref, w_ref, out_ref):
+def put_projected(q_ref, raw_ref, c, value):
+    hidden = q_ref.shape[1]
+    if c < hidden:
+        q_ref[:, c : c + 256] = value.astype(BF16)
+    else:
+        raw_ref[:, c - hidden : c - hidden + 256] = value.astype(BF16)
+
+
+def project_kernel(a_ref, w_ref, q_ref, raw_ref):
     low = normalize_rows(a_ref[...].astype(F32))[0].astype(BF16)
     for c in range(0, w_ref.shape[1], 256):
-        cut = slice(c, c + 256)
-        out_ref[:, cut] = dot(low, w_ref[:, cut]).astype(BF16)
-
-
-def first_project_kernel(a_ref, w_ref, out_ref, a_buf, w_buf, acc_ref, sems, w_sems):
+        put_projected(q_ref, raw_ref, c, dot(low, w_ref[:, c : c + 256]))
+
+
+def first_project_kernel(a_ref, w_ref, q_ref, raw_ref, a_buf, w_buf, acc_ref, sems, w_sems):
     get_a = stream(a_ref, a_buf, sems, WHOLE)
     cuts = [(slice(r, r + 256), slice(None)) for r in range(0, w_ref.shape[0], 256)]
     get = stream(w_ref, w_buf, w_sems, cuts)
@@ -139,10 +146,10 @@
             if k + 1 < len(cuts):
                 acc_ref[:, cut] = total
             else:
-                out_ref[:, cut] = total.astype(BF16)
-
-
-def pool_kernel(cross_ref, inner_ref, w_ref, proj_ref, kern_ref, kv_ref, pk_ref, ext_ref):
+                put_projected(q_ref, raw_ref, c, total)
+
+
+def pool_kernel(cross_ref, inner_ref, w_ref, raw_ref, kern_ref, kv_ref, pk_ref, ext_ref):
     hidden = pk_ref.shape[1]
     odd = is_odd()
     cross, inner = cross_ref[...], inner_ref[...]
@@ -156,7 +163,7 @@
         for j in (0, 128):
             at = c + j
             ext_ref[0:ROW, :] = outer[:ROW, j : j + 128]
-            ext_ref[ROW : ROW + 128, :] = proj_ref[:, hidden + at : hidden + at + 128].astype(F32)
+            ext_ref[ROW : ROW + 128, :] = raw_ref[:, at : at + 128].astype(F32)
             ext_ref[ROW + 128 :, :] = outer[ROW:, j : j + 128]
             pooled = pool_lanes(ext_ref, load_taps(kern_ref, slice(at, at + 128)), False, (0, 1, 2, 3)).astype(BF16)
             if at < hidden:
@@ -193,25 +200,25 @@
         q_low = q_unit.astype(BF16)
         keys = masked(both(at))
         values = masked(both(hidden + at))
-        scores = dot_nt(q_low, keys)
-        grad_probs = dot_nt(g2, values)
+        scores = dot_nt(keys, q_low)
+        grad_probs = dot_nt(values, g2)
         probs, grads = [], []
         for half in range(2):
             scale = tau_ref[2 * p + half]
             cut = slice(half * 256, half * 256 + 256)
-            exponent = jnp.exp(scores[:, cut] * scale)
-            prob = exponent * (1.0 / jnp.sum(exponent, axis=-1, keepdims=True))
-            gp = grad_probs[:, cut]
-            delta = jnp.sum(prob * gp, axis=-1, keepdims=True)
+            exponent = jnp.exp(scores[cut] * scale)
+            prob = exponent * (1.0 / jnp.sum(exponent, axis=0, keepdims=True))
+            gp = grad_probs[cut]
+            delta = jnp.sum(prob * gp, axis=0, keepdims=True)
             probs.append(prob.astype(BF16))
             grads.append((scale * prob * (gp - delta)).astype(BF16))
-        prob_low = jnp.concatenate(probs, axis=1)
-        grad_scores = jnp.concatenate(grads, axis=1)
-        att_ref[:, at : at + PW] = dot(prob_low, values).astype(BF16)
-        grad_q = dot(grad_scores, keys)
+        prob_low = jnp.concatenate(probs, axis=0)
+        grad_scores = jnp.concatenate(grads, axis=0)
+        att_ref[:, at : at + PW] = dot(values.T, prob_low).T.astype(BF16)
+        grad_q = dot(keys.T, grad_scores).T
         gq_ref[:, at : at + PW] = pair_unit_back(q_unit, q_inverse, grad_q, first).astype(BF16)
-        grad_k = dot(grad_scores.T, q_low)
-        grad_v = dot(prob_low.T, g2)
+        grad_k = dot(grad_scores, q_low)
+        grad_v = dot(prob_low, g2)
         grad_k = jnp.where(first_low, grad_k[:256], grad_k[256:]).astype(BF16)
         grad_v = jnp.where(first_low, grad_v[:256], grad_v[256:]).astype(BF16)
         part_own_ref[:, at : at + PW] = grad_k[:128]
@@ -395,32 +402,32 @@
     return cross, inner
 
 
-def forward_project(a, w_qkv, halo):
-    cross, inner = halo
+def forward_project(a, w_qkv):
     block, width = a.shape
-    (proj,) = call(
-        project_kernel, "project", [(block, w_qkv.shape[1])], [VMEM] * 2, 2 * block * width * w_qkv.shape[1]
+    columns = w_qkv.shape[1]
+    return call(
+        project_kernel, "project", [(block, columns // 3), (block, columns // 3 * 2)], [VMEM] * 2,
+        2 * block * width * columns,
     )(a, w_qkv)
-    return proj, cross, inner
 
 
 def first_project(a, w_qkv):
     block, width = a.shape
     columns = w_qkv.shape[1]
     return call(
-        first_project_kernel, "firstproject", [(block, columns)], [HBM] * 2, 2 * block * width * columns,
+        first_project_kernel, "firstproject", [(block, columns // 3), (block, columns // 3 * 2)], [HBM] * 2, 2 * block * width * columns,
         [VMEM(a.shape, BF16), VMEM(w_qkv.shape, BF16), VMEM((block, columns), F32), DMA((1,)), DMA((width // 256,))],
         limit=14,
-    )(a, w_qkv)[0]
-
-
-def forward_pool(proj, cross, inner, w_qkv, kern):
-    block = proj.shape[0]
-    hidden = proj.shape[1] // 3
+    )(a, w_qkv)
+
+
+def forward_pool(raw, cross, inner, w_qkv, kern):
+    block, channels = raw.shape
+    hidden = channels // 2
     return call(
         pool_kernel, "pool", [(block, 2 * hidden), (block, hidden)], [VMEM] * 5,
         2 * block * w_qkv.shape[0] * 2 * hidden, [VMEM((256, 128), F32)],
-    )(cross, inner, w_qkv, proj, kern)
+    )(cross, inner, w_qkv, raw, kern)
 
 
 def grad_attended(gb, w_out):
@@ -500,17 +507,19 @@
     one, two, start = first_layout, second_layout, start_layout
 
     halo = exchange(*edges(a), start, one)
-    b2 = move(a, one, two, -1)
-    ga2 = move(gb, one, two, -1)
-    proj1 = first_project(a, w_qkv)
+    q1, raw1 = first_project(a, w_qkv)
     cross, inner = halo
-    kv1, pk1 = forward_pool(proj1, cross, inner, w_qkv, kern)
+    kv1, pk1 = forward_pool(raw1, cross, inner, w_qkv, kern)
+    kv1, a_pass, gb_pass = together(kv1, a, gb)
     cross, inner = exchange(kv1, kv1, one)
+    b2 = move(a_pass, one, two, -1)
+    ga2 = move(gb_pass, one, two, -1)
     grad1 = grad_attended(gb, w_out)
-    cross, inner, b2, ga2, grad1 = together(cross, inner, b2, ga2, grad1)
+    cross, inner, grad1 = together(cross, inner, grad1)
     _, gq1, own1, near1, rebuilt1 = attend_rebuild(
-        one, owner, tau, proj1, kv1, cross, inner, grad1, w_out, b
+        one, owner, tau, q1, kv1, cross, inner, grad1, w_out, b
     )
+    near1, b2, ga2 = together(near1, b2, ga2)
     cross, inner = exchange(near1, near1, one)
     a2 = move(rebuilt1, one, two, -1)
     gpool1, cross, inner = key_sums(one, owner, own1, cross, inner, pk1)
@@ -518,14 +527,15 @@
     part1, acc1 = finish_local(gpool1, gq1, w_qkv, kern)
     new_grad1 = finish(cross, inner, part1, acc1, w_qkv, kern, a, ga)
 
-    proj2, cross, inner = forward_project(a2, w_qkv, exchange(*edges(a2), two))
-    kv2, pk2 = forward_pool(proj2, cross, inner, w_qkv, kern)
+    cross, inner = exchange(*edges(a2), two)
+    q2, raw2 = forward_project(a2, w_qkv)
+    kv2, pk2 = forward_pool(raw2, cross, inner, w_qkv, kern)
     kv2, new_grad1 = together(kv2, new_grad1)
     gb2 = move(new_grad1, one, two, -1)
     cross, inner = exchange(kv2, kv2, two)
     grad2 = grad_attended(gb2, w_out)
     passed_a = move(gb2, two, start, -1)
-    att2, gq2, own2, near2 = attend(two, owner, tau, proj2, kv2, cross, inner, grad2)
+    att2, gq2, own2, near2 = attend(two, owner, tau, q2, kv2, cross, inner, grad2)
     cross, inner = exchange(near2, near2, two)
     att2, passed_a = together(att2, passed_a)
     rebuilt2 = rebuild(att2, w_out, b2)

time: 147 us -> 148 us (level); the launches traced: 147 us -> 146 us
  starting transfers between devices: 64.7 us -> 74.2 us
  waiting for transfers between devices: 37.5 us -> 29.3 us
  Pallas kernels: 36 us -> 32.7 us
    ppermute x8, starting transfers between devices: 30.3 us -> 35.2 us  [move(): return lax.ppermute(value, AXES, pairs)]
    ppermute x8, waiting for transfers between devices: 26 us -> 21.3 us  [move(): return lax.ppermute(value, AXES, pairs)]
    ppermute x8, waiting for transfers between devices: 11.4 us -> 8.06 us  [swap_cross(): return lax.ppermute(value, AXES, pairs)]
    pallas_call x16, Pallas kernels: 36 us -> 32.7 us  [run(): pl.pallas_call(kernel, name=name, out_shape=[jax.ShapeDtypeStruct(s, kind...]
    ppermute x8, starting transfers between devices: 28.1 us -> 30.8 us  [swap_cross(): return lax.ppermute(value, AXES, pairs)]
    ppermute x8, starting transfers between devices: 6.29 us -> 8.2 us  [swap_inner(): return lax.ppermute(value, AXES, pairs)]
  transfers between devices with their start and end apart: 24 -> 24, of which waited for: 8 -> 7; matrix products, arithmetic and copies ran while one was open for 0% -> 0% of each run, Pallas kernels for 16% -> 17%
where the time goes in v3:
time: 148 us; the launch traced here: 146 us
  starting transfers between devices  74.2 us (50%)
  Pallas kernels  32.7 us (22%)
  waiting for transfers between devices  29.3 us (20%)
  local copies, waits for them, and re-layouts  8.31 us (6%)
    ppermute x8, starting transfers between devices, move(): return lax.ppermute(value, AXES, pairs)  35.2 us
    pallas_call x16, Pallas kernels, run(): pl.pallas_call(kernel, name=name, out_shape=[jax.ShapeDtypeStruct(s, kind...  32.7 us
    ppermute x8, starting transfers between devices, swap_cross(): return lax.ppermute(value, AXES, pairs)  30.8 us
    ppermute x8, waiting for transfers between devices, move(): return lax.ppermute(value, AXES, pairs)  21.3 us
    ppermute x8, starting transfers between devices, swap_inner(): return lax.ppermute(value, AXES, pairs)  8.2 us
    ppermute x8, waiting for transfers between devices, swap_cross(): return lax.ppermute(value, AXES, pairs)  8.06 us
    unnamed x32, local copies, waits for them, and re-layouts  7.08 us
  transfers between devices with their start and end apart: 24, of which 7 were waited for; matrix products, arithmetic and copies ran while one was open for 0% of the time, Pallas kernels for 17%

profile of v3, /device:TPU:11, one launch (start us, length us, event | category | flops | bytes accessed | tf_op | source)
XLA Modules:
  0.0 145.6 jit_solution(237283794097365073)
XLA Ops:
  0.7 0.0 copy-start
  0.7 1.2 dynamic-slice_bitcast_fusion
  1.9 0.8 collective-permute-start.1
  2.6 3.2 %collective-permute-start = (bf16[64,1536]{1,0:T(8,128)(2,1)S(1)}, bf16[64,1536]{1,0:T(8,128)(2,1)S(1)}, u32[]{:S(2)}, u32[]{:S(2)}) collective-permute-start(bf16[64,1536]{1,0:T(8,128)(2,1)S(1)} %get-tuple-element.107), channel_id=1, source_target_pairs={{1,2},{2,1},{3,4},{4,3},{5,6},{6,5},{7,8},{8,7},{9,10},{10,9},{11,... | collective-permute-start | bytes 589832 | tf_op jit(solution)/shard_map/ppermute | solution.py:380
  5.8 0.0 copy-start.12
  5.8 0.0 copy-start.4
  5.8 4.9 %firstproject.1 = (bf16[128,768]{1,0:T(8,128)(2,1)S(1)}, bf16[128,1536]{1,0:T(8,128)(2,1)S(1)}) custom-call(bf16[128,1536]{1,0:T(8,128)(2,1)} %bitcast.36, bf16[1536,2304]{1,0:T(8,128)(2,1)} %bitcast.16), custom_call_target="tpu_custom_call" | custom-call | flops 905969664 | bytes 7471104 | tf_op jit(solution)/shard_map/firstproject/pallas_call | solution.py:328
  10.7 0.0 copy-start.7
  10.7 0.7 copy-done.7
  11.4 0.0 slice-start
  11.4 3.0 %pool.2 = (bf16[128,1536]{1,0:T(8,128)(2,1)}, bf16[128,768]{1,0:T(8,128)(2,1)S(1)}) custom-call(bf16[64,1536]{1,0:T(8,128)(2,1)S(1)} %collective-permute-done.cross_ref, bf16[64,1536]{1,0:T(8,128)(2,1)S(1)} %collective-permute-done.1.inner_ref, bf16[1536,2304]{1,0:T(8,128)(2,1)S(1)} %bitcast.17, bf16[128,1536]{1,0:T(8,128)(2,1)S(1)} %get-tuple-element.55.raw_ref, ...), custom_call_target="tpu_custom_call" | custom-call | flops 603979776 | bytes 8030208 | tf_op jit(solution)/shard_map/pool/pallas_call | solution.py:328
  14.4 0.7 copy-done.9
  15.1 0.6 collective-permute-start.3
  15.7 3.2 %collective-permute-start.2 = (bf16[128,1536]{1,0:T(8,128)(2,1)}, bf16[128,1536]{1,0:T(8,128)(2,1)}, u32[]{:S(2)}, u32[]{:S(2)}) collective-permute-start(bf16[128,1536]{1,0:T(8,128)(2,1)} %get-tuple-element.57.refs_3_), channel_id=1, source_target_pairs={{1,2},{2,1},{3,4},{4,3},{5,6},{6,5},{7,8},{8,7},{9,10},{10,9},{11,... | collective-permute-start | bytes 1179656 | tf_op jit(solution)/shard_map/ppermute | solution.py:380
  19.0 0.1 copy.16.refs_0_.owner_ref
  19.1 6.4 %collective-permute-start.7 = (bf16[128,1536]{1,0:T(8,128)(2,1)S(1)}, bf16[128,1536]{1,0:T(8,128)(2,1)S(1)}, u32[]{:S(2)}, u32[]{:S(2)}) collective-permute-start(bf16[128,1536]{1,0:T(8,128)(2,1)S(1)} %bitcast.37), channel_id=1, source_target_pairs={{0,242},{1,243},{2,240},{3,241},{4,246},{5,247},{6,244},{7,245},{8... | collective-permute-start | bytes 1179656 | tf_op jit(solution)/shard_map/ppermute | solution.py:371
  25.4 0.7 collective-permute-start.8
  26.1 1.7 %copy-done.1 = bf16[1,768,1536]{2,1,0:T(8,128)(2,1)S(1)} copy-done((bf16[1,768,1536]{2,1,0:T(8,128)(2,1)S(1)}, bf16[1,768,1536]{2,1,0:T(8,128)(2,1)}, u32[]{:S(2)}) %copy-start.1) | copy-done | bytes 2359320
  27.8 1.0 copy-done.6
  28.8 0.9 gradatt.2.refs_6_
  29.7 0.0 copy-start.8
  29.7 1.3 copy-done.8
  31.0 4.9 %attendout.1 = (bf16[128,768]{1,0:T(8,128)(2,1)}, bf16[128,768]{1,0:T(8,128)(2,1)S(1)}, bf16[128,1536]{1,0:T(8,128)(2,1)S(1)}, bf16[128,1536]{1,0:T(8,128)(2,1)S(1)}, bf16[128,1536]{1,0:T(8,128)(2,1)S(1)}) custom-call(s32[16,2]{1,0:T(8,128)S(1)} %copy.16.refs_0_.owner_ref, f32[12]{0:T(128)S(1)} %bitcast.42, bf16[128,768]{1,0:T(8,128)(2,1)S(1)} %copy-done.8, ...), custom_call_target="tpu_custom_call" | custom-call | flops 805306368 | bytes 4325552 | tf_op jit(solution)/shard_map/attendout/pallas_call | solution.py:328
  35.9 5.9 %collective-permute-start.4 = (bf16[128,1536]{1,0:T(8,128)(2,1)S(1)}, bf16[128,1536]{1,0:T(8,128)(2,1)S(1)}, u32[]{:S(2)}, u32[]{:S(2)}) collective-permute-start(bf16[128,1536]{1,0:T(8,128)(2,1)S(1)} %get-tuple-element.61), channel_id=1, source_target_pairs={{0,242},{1,243},{2,240},{3,241},{4,246},{5,247},{6,244},{7,245},{8... | collective-permute-start | bytes 1179656 | tf_op jit(solution)/shard_map/ppermute | solution.py:371
  41.9 0.3 collective-permute-done.8.ga_ref
  42.2 1.4 collective-permute-start.10
  43.6 4.2 %collective-permute-start.9 = (bf16[128,1536]{1,0:T(8,128)(2,1)S(1)}, bf16[128,1536]{1,0:T(8,128)(2,1)S(1)}, u32[]{:S(2)}, u32[]{:S(2)}) collective-permute-start(bf16[128,1536]{1,0:T(8,128)(2,1)S(1)} %get-tuple-element.69), channel_id=1, source_target_pairs={{1,2},{2,1},{3,4},{4,3},{5,6},{6,5},{7,8},{8,7},{9,10},{10,9},{11,... | collective-permute-start | bytes 1179656 | tf_op jit(solution)/shard_map/ppermute | solution.py:380
  47.8 3.1 %collective-permute-done.4.a_ref = bf16[128,1536]{1,0:T(8,128)(2,1)S(1)} collective-permute-done((bf16[128,1536]{1,0:T(8,128)(2,1)S(1)}, bf16[128,1536]{1,0:T(8,128)(2,1)S(1)}, u32[]{:S(2)}, u32[]{:S(2)}) %collective-permute-start.4) | collective-permute-done | bytes 393248 | tf_op jit(solution)/shard_map/ppermute | solution.py:371
  50.9 0.8 collective-permute-start.6
  51.7 4.7 %collective-permute-start.5 = (bf16[64,1536]{1,0:T(8,128)(2,1)S(1)}, bf16[64,1536]{1,0:T(8,128)(2,1)S(1)}, u32[]{:S(2)}, u32[]{:S(2)}) collective-permute-start(bf16[64,1536]{1,0:T(8,128)(2,1)S(1)} %get-tuple-element.105), channel_id=1, source_target_pairs={{1,2},{2,1},{3,4},{4,3},{5,6},{6,5},{7,8},{8,7},{9,10},{10,9},{11,... | collective-permute-start | bytes 589832 | tf_op jit(solution)/shard_map/ppermute | solution.py:380
  56.4 0.0 copy-start.10
  56.4 0.9 copy-done.10
  57.4 1.6 %keys.2 = (bf16[128,1536]{1,0:T(8,128)(2,1)S(1)}, bf16[64,1536]{1,0:T(8,128)(2,1)S(1)}, bf16[64,1536]{1,0:T(8,128)(2,1)S(1)}) custom-call(s32[16,2]{1,0:T(8,128)S(1)} %copy.16.refs_0_.owner_ref, bf16[128,1536]{1,0:T(8,128)(2,1)S(1)} %get-tuple-element.65.own_ref, bf16[128,1536]{1,0:T(8,128)(2,1)S(1)} %collective-permute-done.9.cross_ref, ...), custom_call_target="tpu_custom_call" | custom-call | flops 7864320 | bytes 1376384 | tf_op jit(solution)/shard_map/keys/pallas_call | solution.py:328
  59.0 2.0 %collective-permute-start.11 = (bf16[64,1536]{1,0:T(8,128)(2,1)S(1)}, bf16[64,1536]{1,0:T(8,128)(2,1)S(1)}, u32[]{:S(2)}, u32[]{:S(2)}) collective-permute-start(bf16[64,1536]{1,0:T(8,128)(2,1)S(1)} %get-tuple-element.71), channel_id=1, source_target_pairs={{1,2},{2,1},{3,4},{4,3},{5,6},{6,5},{7,8},{8,7},{9,10},{10,9},{11,... | collective-permute-start | bytes 589832 | tf_op jit(solution)/shard_map/ppermute | solution.py:380
  60.9 1.9 %collective-permute-start.12 = (bf16[64,1536]{1,0:T(8,128)(2,1)S(1)}, bf16[64,1536]{1,0:T(8,128)(2,1)S(1)}, u32[]{:S(2)}, u32[]{:S(2)}) collective-permute-start(bf16[64,1536]{1,0:T(8,128)(2,1)S(1)} %get-tuple-element.72), channel_id=1, source_target_pairs={{0,1},{1,0},{2,3},{3,2},{4,5},{5,4},{6,7},{7,6},{8,9},{9,8},{10,11... | collective-permute-start | bytes 589832 | tf_op jit(solution)/shard_map/ppermute | solution.py:385
  62.8 1.0 local.2
  63.8 0.0 copy-start.5
  63.8 1.3 project.1
  65.1 2.3 %pool.3 = (bf16[128,1536]{1,0:T(8,128)(2,1)S(1)}, bf16[128,768]{1,0:T(8,128)(2,1)S(1)}) custom-call(bf16[64,1536]{1,0:T(8,128)(2,1)S(1)} %collective-permute-done.5.cross_ref, bf16[64,1536]{1,0:T(8,128)(2,1)S(1)} %collective-permute-done.6.inner_ref, bf16[1536,2304]{1,0:T(8,128)(2,1)S(1)} %bitcast.22, bf16[128,1536]{1,0:T(8,128)(2,1)S(1)} %get-tuple-element.63.raw_ref, ...), custom_call_target="tpu_custom_call" | custom-call | flops 603979776 | bytes 8030208 | tf_op jit(solution)/shard_map/pool/pallas_call | solution.py:328
  67.5 2.2 %final.2 = bf16[128,1536]{1,0:T(8,128)(2,1)S(1)} custom-call(bf16[64,1536]{1,0:T(8,128)(2,1)S(1)} %collective-permute-done.11.cross_ref, bf16[64,1536]{1,0:T(8,128)(2,1)S(1)} %collective-permute-done.12.inner_ref, f32[128,1536]{1,0:T(8,128)S(1)} %get-tuple-element.75.part_ref, f32[128,1536]{1,0:T(8,128)S(1)} %get-tuple-element.76.acc_ref, ...), custom_call_target="tpu_custom_call" | custom-call | flops 603979776 | bytes 9996288 | tf_op jit(solution)/shard_map/final/pallas_call | solution.py:328
  69.7 5.2 %collective-permute-start.15 = (bf16[128,1536]{1,0:T(8,128)(2,1)S(1)}, bf16[128,1536]{1,0:T(8,128)(2,1)S(1)}, u32[]{:S(2)}, u32[]{:S(2)}) collective-permute-start(bf16[128,1536]{1,0:T(8,128)(2,1)S(1)} %final.2), channel_id=1, source_target_pairs={{0,242},{1,243},{2,240},{3,241},{4,246},{5,247},{6,244},{7,245},{8... | collective-permute-start | bytes 1179656 | tf_op jit(solution)/shard_map/ppermute | solution.py:371
  74.9 0.1 collective-permute-start.14
  75.0 4.5 %collective-permute-start.13 = (bf16[128,1536]{1,0:T(8,128)(2,1)S(1)}, bf16[128,1536]{1,0:T(8,128)(2,1)S(1)}, u32[]{:S(2)}, u32[]{:S(2)}) collective-permute-start(bf16[128,1536]{1,0:T(8,128)(2,1)S(1)} %get-tuple-element.77.own_ref), channel_id=1, source_target_pairs={{1,2},{2,1},{3,4},{4,3},{5,6},{6,5},{7,8},{8,7},{9,10},{10,9},{11,... | collective-permute-start | bytes 1179656 | tf_op jit(solution)/shard_map/ppermute | solution.py:380
  79.5 4.0 %collective-permute-done.15.gb_ref = bf16[128,1536]{1,0:T(8,128)(2,1)S(1)} collective-permute-done((bf16[128,1536]{1,0:T(8,128)(2,1)S(1)}, bf16[128,1536]{1,0:T(8,128)(2,1)S(1)}, u32[]{:S(2)}, u32[]{:S(2)}) %collective-permute-start.15) | collective-permute-done | bytes 393248 | tf_op jit(solution)/shard_map/ppermute | solution.py:371
  83.5 3.6 %collective-permute-start.18 = (bf16[128,1536]{1,0:T(8,128)(2,1)S(1)}, bf16[128,1536]{1,0:T(8,128)(2,1)S(1)}, u32[]{:S(2)}, u32[]{:S(2)}) collective-permute-start(bf16[128,1536]{1,0:T(8,128)(2,1)S(1)} %collective-permute-done.15.gb_ref), channel_id=1, source_target_pairs={{0,240},{1,241},{2,242},{3,243},{4,244},{5,245},{6,246},{7,247},{8... | collective-permute-start | bytes 1179656 | tf_op jit(solution)/shard_map/ppermute | solution.py:371
  87.1 0.9 gradatt.3.grad_ref
  88.0 3.5 %attention.1 = (bf16[128,768]{1,0:T(8,128)(2,1)S(1)}, bf16[128,768]{1,0:T(8,128)(2,1)S(1)}, bf16[128,1536]{1,0:T(8,128)(2,1)S(1)}, bf16[128,1536]{1,0:T(8,128)(2,1)S(1)}) custom-call(s32[16,2]{1,0:T(8,128)S(1)} %copy.16.refs_0_.owner_ref, f32[12]{0:T(128)S(1)} %bitcast.43, bf16[128,768]{1,0:T(8,128)(2,1)S(1)} %get-tuple-element.62.proj_ref, ...), custom_call_target="tpu_custom_call" | custom-call | flops 805306368 | bytes 1573040 | tf_op jit(solution)/shard_map/attention/pallas_call | solution.py:328
  91.5 2.5 %collective-permute-start.17 = (bf16[128,1536]{1,0:T(8,128)(2,1)S(1)}, bf16[128,1536]{1,0:T(8,128)(2,1)S(1)}, u32[]{:S(2)}, u32[]{:S(2)}) collective-permute-start(bf16[128,1536]{1,0:T(8,128)(2,1)S(1)} %get-tuple-element.80), channel_id=1, source_target_pairs={{0,1},{1,0},{2,3},{3,2},{4,5},{5,4},{6,7},{7,6},{8,9},{9,8},{10,11... | collective-permute-start | bytes 1179656 | tf_op jit(solution)/shard_map/ppermute | solution.py:385
  94.0 3.8 %collective-permute-start.16 = (bf16[128,1536]{1,0:T(8,128)(2,1)S(1)}, bf16[128,1536]{1,0:T(8,128)(2,1)S(1)}, u32[]{:S(2)}, u32[]{:S(2)}) collective-permute-start(bf16[128,1536]{1,0:T(8,128)(2,1)S(1)} %get-tuple-element.80), channel_id=1, source_target_pairs={{1,2},{2,1},{3,4},{4,3},{5,6},{6,5},{7,8},{8,7},{9,10},{10,9},{11,... | collective-permute-start | bytes 1179656 | tf_op jit(solution)/shard_map/ppermute | solution.py:380
  97.8 0.5 output.1
  98.3 5.8 %collective-permute-done.16.cross_ref = bf16[128,1536]{1,0:T(8,128)(2,1)S(1)} collective-permute-done((bf16[128,1536]{1,0:T(8,128)(2,1)S(1)}, bf16[128,1536]{1,0:T(8,128)(2,1)S(1)}, u32[]{:S(2)}, u32[]{:S(2)}) %collective-permute-start.16) | collective-permute-done | bytes 393248 | tf_op jit(solution)/shard_map/ppermute | solution.py:380
  104.1 8.3 %collective-permute-start.21 = (bf16[128,1536]{1,0:T(8,128)(2,1)S(1)}, bf16[128,1536]{1,0:T(8,128)(2,1)S(1)}, u32[]{:S(2)}, u32[]{:S(2)}) collective-permute-start(bf16[128,1536]{1,0:T(8,128)(2,1)S(1)} %collective-permute-done.4.a_ref), channel_id=1, source_target_pairs={{0,240},{1,241},{2,242},{3,243},{4,244},{5,245},{6,246},{7,247},{8... | collective-permute-start | bytes 1179656 | tf_op jit(solution)/shard_map/ppermute | solution.py:371
  112.4 1.6 %keys.3 = (bf16[128,1536]{1,0:T(8,128)(2,1)S(1)}, bf16[64,1536]{1,0:T(8,128)(2,1)S(1)}, bf16[64,1536]{1,0:T(8,128)(2,1)S(1)}) custom-call(s32[16,2]{1,0:T(8,128)S(1)} %copy.16.refs_0_.owner_ref, bf16[128,1536]{1,0:T(8,128)(2,1)S(1)} %get-tuple-element.79.own_ref, bf16[128,1536]{1,0:T(8,128)(2,1)S(1)} %collective-permute-done.16.cross_ref, ...), custom_call_target="tpu_custom_call" | custom-call | flops 7864320 | bytes 1376384 | tf_op jit(solution)/shard_map/keys/pallas_call | solution.py:328
  114.0 5.4 %collective-permute-start.19 = (bf16[64,1536]{1,0:T(8,128)(2,1)S(1)}, bf16[64,1536]{1,0:T(8,128)(2,1)S(1)}, u32[]{:S(2)}, u32[]{:S(2)}) collective-permute-start(bf16[64,1536]{1,0:T(8,128)(2,1)S(1)} %get-tuple-element.87), channel_id=1, source_target_pairs={{1,2},{2,1},{3,4},{4,3},{5,6},{6,5},{7,8},{8,7},{9,10},{10,9},{11,... | collective-permute-start | bytes 589832 | tf_op jit(solution)/shard_map/ppermute | solution.py:380
  119.4 0.1 collective-permute-start.20
  119.5 1.0 local.3
  120.5 2.3 %collective-permute-done.19.cross_ref = bf16[64,1536]{1,0:T(8,128)(2,1)S(1)} collective-permute-done((bf16[64,1536]{1,0:T(8,128)(2,1)S(1)}, bf16[64,1536]{1,0:T(8,128)(2,1)S(1)}, u32[]{:S(2)}, u32[]{:S(2)}) %collective-permute-start.19) | collective-permute-done | bytes 196640 | tf_op jit(solution)/shard_map/ppermute | solution.py:380
  122.7 2.2 %final.3 = bf16[128,1536]{1,0:T(8,128)(2,1)S(1)} custom-call(bf16[64,1536]{1,0:T(8,128)(2,1)S(1)} %collective-permute-done.19.cross_ref, bf16[64,1536]{1,0:T(8,128)(2,1)S(1)} %collective-permute-done.20.inner_ref, f32[128,1536]{1,0:T(8,128)S(1)} %get-tuple-element.101.part_ref, f32[128,1536]{1,0:T(8,128)S(1)} %get-tuple-element.102.acc_ref, ...), custom_call_target="tpu_custom_call" | custom-call | flops 603979776 | bytes 9996288 | tf_op jit(solution)/shard_map/final/pallas_call | solution.py:328
  124.9 4.9 %collective-permute-start.23 = (bf16[128,1536]{1,0:T(8,128)(2,1)S(1)}, bf16[128,1536]{1,0:T(8,128)(2,1)S(1)}, u32[]{:S(2)}, u32[]{:S(2)}) collective-permute-start(bf16[128,1536]{1,0:T(8,128)(2,1)S(1)} %final.3), channel_id=1, source_target_pairs={{0,240},{1,241},{2,242},{3,243},{4,244},{5,245},{6,246},{7,247},{8... | collective-permute-start | bytes 1179656 | tf_op jit(solution)/shard_map/ppermute | solution.py:371
  129.9 0.1 collective-permute-start.22
  130.0 8.9 %collective-permute-done.23 = bf16[128,1536]{1,0:T(8,128)(2,1)S(1)} collective-permute-done((bf16[128,1536]{1,0:T(8,128)(2,1)S(1)}, bf16[128,1536]{1,0:T(8,128)(2,1)S(1)}, u32[]{:S(2)}, u32[]{:S(2)}) %collective-permute-start.23) | collective-permute-done | bytes 393248 | tf_op jit(solution)/shard_map/ppermute | solution.py:371
  138.9 4.9 %collective-permute-done.22.refs_0_ = bf16[128,1536]{1,0:T(8,128)(2,1)S(1)} collective-permute-done((bf16[128,1536]{1,0:T(8,128)(2,1)S(1)}, bf16[128,1536]{1,0:T(8,128)(2,1)S(1)}, u32[]{:S(2)}, u32[]{:S(2)}) %collective-permute-start.22) | collective-permute-done | bytes 393248 | tf_op jit(solution)/shard_map/ppermute | solution.py:371
  143.8 1.1 settle.1
  144.9 0.7 copy.18
  (35 shorter events, 0.1 us)
Async XLA Ops:
  0.6 10.8 %copy-start.3 = (f32[1,27,1536]{2,0,1:T(1,128)S(1)}, f32[1,27,1536]{2,0,1:T(1,128)}, u32[]{:S(2)}) copy-start(f32[1,27,1536]{2,0,1:T(1,128)} %param.15) | copy-start | bytes 497668
  0.7 10.7 %copy-start = (bf16[1,1536,2304]{2,1,0:T(8,128)(2,1)S(1)}, bf16[1,1536,2304]{2,1,0:T(8,128)(2,1)}, u32[]{:S(2)}) copy-start(bf16[1,1536,2304]{2,1,0:T(8,128)(2,1)} %param.13) | copy-start | bytes 21233668
  1.9 9.5 %collective-permute-start.1 = (bf16[64,1536]{1,0:T(8,128)(2,1)S(1)}, bf16[64,1536]{1,0:T(8,128)(2,1)S(1)}, u32[]{:S(2)}, u32[]{:S(2)}) collective-permute-start(bf16[64,1536]{1,0:T(8,128)(2,1)S(1)} %get-tuple-element.106), channel_id=1, source_target_pairs={{0,1},{1,0},{2,3},{3,2},{4,5},{5,4},{6,7},{7,6},{8,9},{9,8},{10,11... | collective-permute-start | bytes 589832 | tf_op jit(solution)/shard_map/ppermute | solution.py:385
  2.6 8.7 %collective-permute-start = (bf16[64,1536]{1,0:T(8,128)(2,1)S(1)}, bf16[64,1536]{1,0:T(8,128)(2,1)S(1)}, u32[]{:S(2)}, u32[]{:S(2)}) collective-permute-start(bf16[64,1536]{1,0:T(8,128)(2,1)S(1)} %get-tuple-element.107), channel_id=1, source_target_pairs={{1,2},{2,1},{3,4},{4,3},{5,6},{6,5},{7,8},{8,7},{9,10},{10,9},{11,... | collective-permute-start | bytes 589832 | tf_op jit(solution)/shard_map/ppermute | solution.py:380
  5.8 13.2 %copy-start.12 = (s32[16,2]{0,1:T(2,128)S(1)}, s32[16,2]{0,1:T(2,128)}, u32[]{:S(2)}) copy-start(s32[16,2]{0,1:T(2,128)} %param.17) | copy-start | bytes 388
  5.8 13.2 %copy-start.4 = (bf16[1,128,1536]{2,1,0:T(8,128)(2,1)S(1)}, bf16[1,128,1536]{2,1,0:T(8,128)(2,1)}, u32[]{:S(2)}) copy-start(bf16[1,128,1536]{2,1,0:T(8,128)(2,1)} %param.9) | copy-start | bytes 1179652
  10.7 0.7 copy-start.7
  11.4 18.3 %copy-start.11 = (f32[1,12]{1,0:T(1,128)S(1)}, f32[1,12]{1,0:T(1,128)}, u32[]{:S(2)}) copy-start(f32[1,12]{1,0:T(1,128)} %param.16) | copy-start | bytes 148
  11.4 51.4 %slice-start = ((s8[7077888]{0:T(1024)(128)(4,1)}), s8[2883584]{0:T(1024)(128)(4,1)S(1)}, s32[]{:S(2)}) async-start(s8[7077888]{0:T(1024)(128)(4,1)} %bitcast.18), calls=%async_computation | async-start | bytes 5767168
  14.4 0.7 copy-start.9
  15.1 14.6 %collective-permute-start.3 = (bf16[128,1536]{1,0:T(8,128)(2,1)}, bf16[128,1536]{1,0:T(8,128)(2,1)}, u32[]{:S(2)}, u32[]{:S(2)}) collective-permute-start(bf16[128,1536]{1,0:T(8,128)(2,1)} %get-tuple-element.57.refs_3_), channel_id=1, source_target_pairs={{0,1},{1,0},{2,3},{3,2},{4,5},{5,4},{6,7},{7,6},{8,9},{9,8},{10,11... | collective-permute-start | bytes 1179656 | tf_op jit(solution)/shard_map/ppermute | solution.py:385
  15.7 14.0 %collective-permute-start.2 = (bf16[128,1536]{1,0:T(8,128)(2,1)}, bf16[128,1536]{1,0:T(8,128)(2,1)}, u32[]{:S(2)}, u32[]{:S(2)}) collective-permute-start(bf16[128,1536]{1,0:T(8,128)(2,1)} %get-tuple-element.57.refs_3_), channel_id=1, source_target_pairs={{1,2},{2,1},{3,4},{4,3},{5,6},{6,5},{7,8},{8,7},{9,10},{10,9},{11,... | collective-permute-start | bytes 1179656 | tf_op jit(solution)/shard_map/ppermute | solution.py:380
  19.1 22.8 %collective-permute-start.7 = (bf16[128,1536]{1,0:T(8,128)(2,1)S(1)}, bf16[128,1536]{1,0:T(8,128)(2,1)S(1)}, u32[]{:S(2)}, u32[]{:S(2)}) collective-permute-start(bf16[128,1536]{1,0:T(8,128)(2,1)S(1)} %bitcast.37), channel_id=1, source_target_pairs={{0,242},{1,243},{2,240},{3,241},{4,246},{5,247},{6,244},{7,245},{8... | collective-permute-start | bytes 1179656 | tf_op jit(solution)/shard_map/ppermute | solution.py:371
  25.4 16.8 %collective-permute-start.8 = (bf16[128,1536]{1,0:T(8,128)(2,1)}, bf16[128,1536]{1,0:T(8,128)(2,1)S(1)}, u32[]{:S(2)}, u32[]{:S(2)}) collective-permute-start(bf16[128,1536]{1,0:T(8,128)(2,1)} %bitcast.40), channel_id=1, source_target_pairs={{0,242},{1,243},{2,240},{3,241},{4,246},{5,247},{6,244},{7,245},{8... | collective-permute-start | bytes 1179656 | tf_op jit(solution)/shard_map/ppermute | solution.py:371
  26.1 1.7 %copy-start.1 = (bf16[1,768,1536]{2,1,0:T(8,128)(2,1)S(1)}, bf16[1,768,1536]{2,1,0:T(8,128)(2,1)}, u32[]{:S(2)}) copy-start(bf16[1,768,1536]{2,1,0:T(8,128)(2,1)} %param.14) | copy-start | bytes 7077892
  27.8 1.0 copy-start.6
  28.8 34.0 %slice-start.1 = ((s8[7077888]{0:T(1024)(128)(4,1)}), s8[4194304]{0:T(1024)(128)(4,1)S(1)}, s32[]{:S(2)}) async-start(s8[7077888]{0:T(1024)(128)(4,1)} %bitcast.18), calls=%async_computation.1 | async-start | bytes 8388608
  29.7 1.3 copy-start.8
  35.9 14.9 %collective-permute-start.4 = (bf16[128,1536]{1,0:T(8,128)(2,1)S(1)}, bf16[128,1536]{1,0:T(8,128)(2,1)S(1)}, u32[]{:S(2)}, u32[]{:S(2)}) collective-permute-start(bf16[128,1536]{1,0:T(8,128)(2,1)S(1)} %get-tuple-element.61), channel_id=1, source_target_pairs={{0,242},{1,243},{2,240},{3,241},{4,246},{5,247},{6,244},{7,245},{8... | collective-permute-start | bytes 1179656 | tf_op jit(solution)/shard_map/ppermute | solution.py:371
  42.2 14.2 %collective-permute-start.10 = (bf16[128,1536]{1,0:T(8,128)(2,1)S(1)}, bf16[128,1536]{1,0:T(8,128)(2,1)S(1)}, u32[]{:S(2)}, u32[]{:S(2)}) collective-permute-start(bf16[128,1536]{1,0:T(8,128)(2,1)S(1)} %get-tuple-element.69), channel_id=1, source_target_pairs={{0,1},{1,0},{2,3},{3,2},{4,5},{5,4},{6,7},{7,6},{8,9},{9,8},{10,11... | collective-permute-start | bytes 1179656 | tf_op jit(solution)/shard_map/ppermute | solution.py:385
  43.6 12.8 %collective-permute-start.9 = (bf16[128,1536]{1,0:T(8,128)(2,1)S(1)}, bf16[128,1536]{1,0:T(8,128)(2,1)S(1)}, u32[]{:S(2)}, u32[]{:S(2)}) collective-permute-start(bf16[128,1536]{1,0:T(8,128)(2,1)S(1)} %get-tuple-element.69), channel_id=1, source_target_pairs={{1,2},{2,1},{3,4},{4,3},{5,6},{6,5},{7,8},{8,7},{9,10},{10,9},{11,... | collective-permute-start | bytes 1179656 | tf_op jit(solution)/shard_map/ppermute | solution.py:380
  50.9 14.2 %collective-permute-start.6 = (bf16[64,1536]{1,0:T(8,128)(2,1)S(1)}, bf16[64,1536]{1,0:T(8,128)(2,1)S(1)}, u32[]{:S(2)}, u32[]{:S(2)}) collective-permute-start(bf16[64,1536]{1,0:T(8,128)(2,1)S(1)} %get-tuple-element.104), channel_id=1, source_target_pairs={{0,1},{1,0},{2,3},{3,2},{4,5},{5,4},{6,7},{7,6},{8,9},{9,8},{10,11... | collective-permute-start | bytes 589832 | tf_op jit(solution)/shard_map/ppermute | solution.py:385
  51.7 13.4 %collective-permute-start.5 = (bf16[64,1536]{1,0:T(8,128)(2,1)S(1)}, bf16[64,1536]{1,0:T(8,128)(2,1)S(1)}, u32[]{:S(2)}, u32[]{:S(2)}) collective-permute-start(bf16[64,1536]{1,0:T(8,128)(2,1)S(1)} %get-tuple-element.105), channel_id=1, source_target_pairs={{1,2},{2,1},{3,4},{4,3},{5,6},{6,5},{7,8},{8,7},{9,10},{10,9},{11,... | collective-permute-start | bytes 589832 | tf_op jit(solution)/shard_map/ppermute | solution.py:380
  56.4 0.9 copy-start.10
  59.0 8.5 %collective-permute-start.11 = (bf16[64,1536]{1,0:T(8,128)(2,1)S(1)}, bf16[64,1536]{1,0:T(8,128)(2,1)S(1)}, u32[]{:S(2)}, u32[]{:S(2)}) collective-permute-start(bf16[64,1536]{1,0:T(8,128)(2,1)S(1)} %get-tuple-element.71), channel_id=1, source_target_pairs={{1,2},{2,1},{3,4},{4,3},{5,6},{6,5},{7,8},{8,7},{9,10},{10,9},{11,... | collective-permute-start | bytes 589832 | tf_op jit(solution)/shard_map/ppermute | solution.py:380
  60.9 6.5 %collective-permute-start.12 = (bf16[64,1536]{1,0:T(8,128)(2,1)S(1)}, bf16[64,1536]{1,0:T(8,128)(2,1)S(1)}, u32[]{:S(2)}, u32[]{:S(2)}) collective-permute-start(bf16[64,1536]{1,0:T(8,128)(2,1)S(1)} %get-tuple-element.72), channel_id=1, source_target_pairs={{0,1},{1,0},{2,3},{3,2},{4,5},{5,4},{6,7},{7,6},{8,9},{9,8},{10,11... | collective-permute-start | bytes 589832 | tf_op jit(solution)/shard_map/ppermute | solution.py:385
  63.8 3.7 %copy-start.5 = (bf16[1,128,1536]{2,1,0:T(8,128)(2,1)S(1)}, bf16[1,128,1536]{2,1,0:T(8,128)(2,1)}, u32[]{:S(2)}) copy-start(bf16[1,128,1536]{2,1,0:T(8,128)(2,1)} %param.11) | copy-start | bytes 1179652
  67.4 19.7 %copy-start.2 = (bf16[1,768,1536]{2,1,0:T(8,128)(2,1)S(1)}, bf16[1,768,1536]{2,1,0:T(8,128)(2,1)}, u32[]{:S(2)}) copy-start(bf16[1,768,1536]{2,1,0:T(8,128)(2,1)} %param.14) | copy-start | bytes 7077892
  69.7 13.9 %collective-permute-start.15 = (bf16[128,1536]{1,0:T(8,128)(2,1)S(1)}, bf16[128,1536]{1,0:T(8,128)(2,1)S(1)}, u32[]{:S(2)}, u32[]{:S(2)}) collective-permute-start(bf16[128,1536]{1,0:T(8,128)(2,1)S(1)} %final.2), channel_id=1, source_target_pairs={{0,242},{1,243},{2,240},{3,241},{4,246},{5,247},{6,244},{7,245},{8... | collective-permute-start | bytes 1179656 | tf_op jit(solution)/shard_map/ppermute | solution.py:371
  74.9 13.1 %collective-permute-start.14 = (bf16[128,1536]{1,0:T(8,128)(2,1)S(1)}, bf16[128,1536]{1,0:T(8,128)(2,1)S(1)}, u32[]{:S(2)}, u32[]{:S(2)}) collective-permute-start(bf16[128,1536]{1,0:T(8,128)(2,1)S(1)} %get-tuple-element.77.own_ref), channel_id=1, source_target_pairs={{0,1},{1,0},{2,3},{3,2},{4,5},{5,4},{6,7},{7,6},{8,9},{9,8},{10,11... | collective-permute-start | bytes 1179656 | tf_op jit(solution)/shard_map/ppermute | solution.py:385
  75.0 13.0 %collective-permute-start.13 = (bf16[128,1536]{1,0:T(8,128)(2,1)S(1)}, bf16[128,1536]{1,0:T(8,128)(2,1)S(1)}, u32[]{:S(2)}, u32[]{:S(2)}) collective-permute-start(bf16[128,1536]{1,0:T(8,128)(2,1)S(1)} %get-tuple-element.77.own_ref), channel_id=1, source_target_pairs={{1,2},{2,1},{3,4},{4,3},{5,6},{6,5},{7,8},{8,7},{9,10},{10,9},{11,... | collective-permute-start | bytes 1179656 | tf_op jit(solution)/shard_map/ppermute | solution.py:380
  83.5 14.3 %collective-permute-start.18 = (bf16[128,1536]{1,0:T(8,128)(2,1)S(1)}, bf16[128,1536]{1,0:T(8,128)(2,1)S(1)}, u32[]{:S(2)}, u32[]{:S(2)}) collective-permute-start(bf16[128,1536]{1,0:T(8,128)(2,1)S(1)} %collective-permute-done.15.gb_ref), channel_id=1, source_target_pairs={{0,240},{1,241},{2,242},{3,243},{4,244},{5,245},{6,246},{7,247},{8... | collective-permute-start | bytes 1179656 | tf_op jit(solution)/shard_map/ppermute | solution.py:371
  91.5 6.8 %collective-permute-start.17 = (bf16[128,1536]{1,0:T(8,128)(2,1)S(1)}, bf16[128,1536]{1,0:T(8,128)(2,1)S(1)}, u32[]{:S(2)}, u32[]{:S(2)}) collective-permute-start(bf16[128,1536]{1,0:T(8,128)(2,1)S(1)} %get-tuple-element.80), channel_id=1, source_target_pairs={{0,1},{1,0},{2,3},{3,2},{4,5},{5,4},{6,7},{7,6},{8,9},{9,8},{10,11... | collective-permute-start | bytes 1179656 | tf_op jit(solution)/shard_map/ppermute | solution.py:385
  94.0 10.1 %collective-permute-start.16 = (bf16[128,1536]{1,0:T(8,128)(2,1)S(1)}, bf16[128,1536]{1,0:T(8,128)(2,1)S(1)}, u32[]{:S(2)}, u32[]{:S(2)}) collective-permute-start(bf16[128,1536]{1,0:T(8,128)(2,1)S(1)} %get-tuple-element.80), channel_id=1, source_target_pairs={{1,2},{2,1},{3,4},{4,3},{5,6},{6,5},{7,8},{8,7},{9,10},{10,9},{11,... | collective-permute-start | bytes 1179656 | tf_op jit(solution)/shard_map/ppermute | solution.py:380
  104.1 18.6 %collective-permute-start.21 = (bf16[128,1536]{1,0:T(8,128)(2,1)S(1)}, bf16[128,1536]{1,0:T(8,128)(2,1)S(1)}, u32[]{:S(2)}, u32[]{:S(2)}) collective-permute-start(bf16[128,1536]{1,0:T(8,128)(2,1)S(1)} %collective-permute-done.4.a_ref), channel_id=1, source_target_pairs={{0,240},{1,241},{2,242},{3,243},{4,244},{5,245},{6,246},{7,247},{8... | collective-permute-start | bytes 1179656 | tf_op jit(solution)/shard_map/ppermute | solution.py:371
  114.0 8.7 %collective-permute-start.19 = (bf16[64,1536]{1,0:T(8,128)(2,1)S(1)}, bf16[64,1536]{1,0:T(8,128)(2,1)S(1)}, u32[]{:S(2)}, u32[]{:S(2)}) collective-permute-start(bf16[64,1536]{1,0:T(8,128)(2,1)S(1)} %get-tuple-element.87), channel_id=1, source_target_pairs={{1,2},{2,1},{3,4},{4,3},{5,6},{6,5},{7,8},{8,7},{9,10},{10,9},{11,... | collective-permute-start | bytes 589832 | tf_op jit(solution)/shard_map/ppermute | solution.py:380
  119.4 3.3 %collective-permute-start.20 = (bf16[64,1536]{1,0:T(8,128)(2,1)S(1)}, bf16[64,1536]{1,0:T(8,128)(2,1)S(1)}, u32[]{:S(2)}, u32[]{:S(2)}) collective-permute-start(bf16[64,1536]{1,0:T(8,128)(2,1)S(1)} %get-tuple-element.88), channel_id=1, source_target_pairs={{0,1},{1,0},{2,3},{3,2},{4,5},{5,4},{6,7},{7,6},{8,9},{9,8},{10,11... | collective-permute-start | bytes 589832 | tf_op jit(solution)/shard_map/ppermute | solution.py:385
  124.9 13.9 %collective-permute-start.23 = (bf16[128,1536]{1,0:T(8,128)(2,1)S(1)}, bf16[128,1536]{1,0:T(8,128)(2,1)S(1)}, u32[]{:S(2)}, u32[]{:S(2)}) collective-permute-start(bf16[128,1536]{1,0:T(8,128)(2,1)S(1)} %final.3), channel_id=1, source_target_pairs={{0,240},{1,241},{2,242},{3,243},{4,244},{5,245},{6,246},{7,247},{8... | collective-permute-start | bytes 1179656 | tf_op jit(solution)/shard_map/ppermute | solution.py:371
  129.9 13.9 %collective-permute-start.22 = (bf16[128,1536]{1,0:T(8,128)(2,1)S(1)}, bf16[128,1536]{1,0:T(8,128)(2,1)S(1)}, u32[]{:S(2)}, u32[]{:S(2)}) collective-permute-start(bf16[128,1536]{1,0:T(8,128)(2,1)S(1)} %output.1), channel_id=1, source_target_pairs={{0,240},{1,241},{2,242},{3,243},{4,244},{5,245},{6,246},{7,247},{8... | collective-permute-start | bytes 1179656 | tf_op jit(solution)/shard_map/ppermute | solution.py:371

commit v4 on v2

--- a/solution.py
+++ b/solution.py
@@ -193,25 +193,25 @@
         q_low = q_unit.astype(BF16)
         keys = masked(both(at))
         values = masked(both(hidden + at))
-        scores = dot_nt(q_low, keys)
-        grad_probs = dot_nt(g2, values)
+        scores = dot_nt(keys, q_low)
+        grad_probs = dot_nt(values, g2)
         probs, grads = [], []
         for half in range(2):
             scale = tau_ref[2 * p + half]
             cut = slice(half * 256, half * 256 + 256)
-            exponent = jnp.exp(scores[:, cut] * scale)
-            prob = exponent * (1.0 / jnp.sum(exponent, axis=-1, keepdims=True))
-            gp = grad_probs[:, cut]
-            delta = jnp.sum(prob * gp, axis=-1, keepdims=True)
+            exponent = jnp.exp(scores[cut] * scale)
+            prob = exponent * (1.0 / jnp.sum(exponent, axis=0, keepdims=True))
+            gp = grad_probs[cut]
+            delta = jnp.sum(prob * gp, axis=0, keepdims=True)
             probs.append(prob.astype(BF16))
             grads.append((scale * prob * (gp - delta)).astype(BF16))
-        prob_low = jnp.concatenate(probs, axis=1)
-        grad_scores = jnp.concatenate(grads, axis=1)
-        att_ref[:, at : at + PW] = dot(prob_low, values).astype(BF16)
-        grad_q = dot(grad_scores, keys)
+        prob_low = jnp.concatenate(probs, axis=0)
+        grad_scores = jnp.concatenate(grads, axis=0)
+        att_ref[:, at : at + PW] = dot(values.T, prob_low).T.astype(BF16)
+        grad_q = dot(keys.T, grad_scores).T
         gq_ref[:, at : at + PW] = pair_unit_back(q_unit, q_inverse, grad_q, first).astype(BF16)
-        grad_k = dot(grad_scores.T, q_low)
-        grad_v = dot(prob_low.T, g2)
+        grad_k = dot(grad_scores, q_low)
+        grad_v = dot(prob_low, g2)
         grad_k = jnp.where(first_low, grad_k[:256], grad_k[256:]).astype(BF16)
         grad_v = jnp.where(first_low, grad_v[:256], grad_v[256:]).astype(BF16)
         part_own_ref[:, at : at + PW] = grad_k[:128]

time: 147 us -> 145 us (0.986)
  Pallas kernels: 36 us -> 33.5 us
    pallas_call x16, Pallas kernels: 36 us -> 33.5 us  [run(): pl.pallas_call(kernel, name=name, out_shape=[jax.ShapeDtypeStruct(s, kind...]
  transfers between devices with their start and end apart: 24 -> 24, of which waited for: 8 -> 7; matrix products, arithmetic and copies ran while one was open for 0% -> 0% of each run, Pallas kernels for 16% -> 16%
where the time goes in v4:
time: 145 us; the launch traced here: 144 us
  starting transfers between devices  65.6 us (45%)
  waiting for transfers between devices  36.8 us (25%)
  Pallas kernels  33.5 us (23%)
  local copies, waits for them, and re-layouts  7.44 us (5%)
    pallas_call x16, Pallas kernels, run(): pl.pallas_call(kernel, name=name, out_shape=[jax.ShapeDtypeStruct(s, kind...  33.5 us
    ppermute x8, starting transfers between devices, move(): return lax.ppermute(value, AXES, pairs)  30.8 us
    ppermute x8, starting transfers between devices, swap_cross(): return lax.ppermute(value, AXES, pairs)  28.4 us
    ppermute x8, waiting for transfers between devices, move(): return lax.ppermute(value, AXES, pairs)  25.4 us
    ppermute x8, waiting for transfers between devices, swap_cross(): return lax.ppermute(value, AXES, pairs)  11.3 us
    ppermute x8, starting transfers between devices, swap_inner(): return lax.ppermute(value, AXES, pairs)  6.41 us
    unnamed x32, local copies, waits for them, and re-layouts  6.21 us
  transfers between devices with their start and end apart: 24, of which 7 were waited for; matrix products, arithmetic and copies ran while one was open for 0% of the time, Pallas kernels for 16%

profile of v4, /device:TPU:11, one launch (start us, length us, event | category | flops | bytes accessed | tf_op | source)
XLA Modules:
  0.0 144.3 jit_solution(15479846571512165746)
XLA Ops:
  0.7 0.0 copy-start
  0.7 1.2 dynamic-slice_bitcast_fusion
  1.9 0.8 collective-permute-start.1
  2.6 3.2 %collective-permute-start = (bf16[64,1536]{1,0:T(8,128)(2,1)S(1)}, bf16[64,1536]{1,0:T(8,128)(2,1)S(1)}, u32[]{:S(2)}, u32[]{:S(2)}) collective-permute-start(bf16[64,1536]{1,0:T(8,128)(2,1)S(1)} %get-tuple-element.91), channel_id=1, source_target_pairs={{1,2},{2,1},{3,4},{4,3},{5,6},{6,5},{7,8},{8,7},{9,10},{10,9},{11,... | collective-permute-start | bytes 589832 | tf_op jit(solution)/shard_map/ppermute | solution.py:373
  5.8 6.6 %collective-permute-start.5 = (bf16[128,1536]{1,0:T(8,128)(2,1)}, bf16[128,1536]{1,0:T(8,128)(2,1)S(1)}, u32[]{:S(2)}, u32[]{:S(2)}) collective-permute-start(bf16[128,1536]{1,0:T(8,128)(2,1)} %bitcast.40), channel_id=1, source_target_pairs={{0,242},{1,243},{2,240},{3,241},{4,246},{5,247},{6,244},{7,245},{8... | collective-permute-start | bytes 1179656 | tf_op jit(solution)/shard_map/ppermute | solution.py:364
  12.4 0.7 collective-permute-start.4
  13.1 4.7 %firstproject.1.proj_ref.refs_2_ = bf16[128,2304]{1,0:T(8,128)(2,1)S(1)} custom-call(bf16[128,1536]{1,0:T(8,128)(2,1)} %bitcast.37, bf16[1536,2304]{1,0:T(8,128)(2,1)} %bitcast.16), custom_call_target="tpu_custom_call" | custom-call | flops 905969664 | bytes 7471104 | tf_op jit(solution)/shard_map/firstproject/pallas_call | solution.py:321
  17.8 0.0 copy-start.11
  17.8 0.0 collective-permute-done.cross_ref
  17.9 0.0 slice-start
  17.9 3.0 %pool.2 = (bf16[128,1536]{1,0:T(8,128)(2,1)}, bf16[128,768]{1,0:T(8,128)(2,1)S(1)}) custom-call(bf16[64,1536]{1,0:T(8,128)(2,1)S(1)} %collective-permute-done.cross_ref, bf16[64,1536]{1,0:T(8,128)(2,1)S(1)} %collective-permute-done.1.inner_ref, bf16[1536,2304]{1,0:T(8,128)(2,1)S(1)} %bitcast.17, bf16[128,2304]{1,0:T(8,128)(2,1)S(1)} %firstproject.1.proj_ref.refs_2_, ...), custom_call_target="tpu_custom_call" | custom-call | flops 603979776 | bytes 8226816 | tf_op jit(solution)/shard_map/pool/pallas_call | solution.py:321
  20.9 0.7 copy-done.9
  21.6 0.9 collective-permute-start.3
  22.5 4.0 %collective-permute-start.2 = (bf16[128,1536]{1,0:T(8,128)(2,1)}, bf16[128,1536]{1,0:T(8,128)(2,1)}, u32[]{:S(2)}, u32[]{:S(2)}) collective-permute-start(bf16[128,1536]{1,0:T(8,128)(2,1)} %get-tuple-element.46.refs_3_), channel_id=1, source_target_pairs={{1,2},{2,1},{3,4},{4,3},{5,6},{6,5},{7,8},{8,7},{9,10},{10,9},{11,... | collective-permute-start | bytes 1179656 | tf_op jit(solution)/shard_map/ppermute | solution.py:373
  26.5 0.1 copy.16.refs_0_.owner_ref
  26.6 1.7 %copy-done.1 = bf16[1,768,1536]{2,1,0:T(8,128)(2,1)S(1)} copy-done((bf16[1,768,1536]{2,1,0:T(8,128)(2,1)S(1)}, bf16[1,768,1536]{2,1,0:T(8,128)(2,1)}, u32[]{:S(2)}) %copy-start.1) | copy-done | bytes 2359320
  28.3 1.0 copy-done.8
  29.3 0.9 gradatt.2.refs_6_
  30.1 0.0 collective-permute-done.5.ga_ref
  30.2 2.7 %collective-permute-done.2.refs_4_ = bf16[128,1536]{1,0:T(8,128)(2,1)} collective-permute-done((bf16[128,1536]{1,0:T(8,128)(2,1)}, bf16[128,1536]{1,0:T(8,128)(2,1)}, u32[]{:S(2)}, u32[]{:S(2)}) %collective-permute-start.2) | collective-permute-done | bytes 393248 | tf_op jit(solution)/shard_map/ppermute | solution.py:373
  32.9 1.1 copy-done.5
  33.9 4.9 %attendout.1 = (bf16[128,768]{1,0:T(8,128)(2,1)}, bf16[128,768]{1,0:T(8,128)(2,1)S(1)}, bf16[128,1536]{1,0:T(8,128)(2,1)S(1)}, bf16[128,1536]{1,0:T(8,128)(2,1)S(1)}, bf16[128,1536]{1,0:T(8,128)(2,1)S(1)}) custom-call(s32[16,2]{1,0:T(8,128)S(1)} %copy.16.refs_0_.owner_ref, f32[12]{0:T(128)S(1)} %bitcast.42, bf16[128,2304]{1,0:T(8,128)(2,1)S(1)} %copy-done.5, ...), custom_call_target="tpu_custom_call" | custom-call | flops 805306368 | bytes 4718768 | tf_op jit(solution)/shard_map/attendout/pallas_call | solution.py:321
  38.8 4.0 %collective-permute-start.6 = (bf16[128,1536]{1,0:T(8,128)(2,1)S(1)}, bf16[128,1536]{1,0:T(8,128)(2,1)S(1)}, u32[]{:S(2)}, u32[]{:S(2)}) collective-permute-start(bf16[128,1536]{1,0:T(8,128)(2,1)S(1)} %get-tuple-element.50), channel_id=1, source_target_pairs={{0,242},{1,243},{2,240},{3,241},{4,246},{5,247},{6,244},{7,245},{8... | collective-permute-start | bytes 1179656 | tf_op jit(solution)/shard_map/ppermute | solution.py:364
  42.8 4.3 %collective-permute-start.9 = (bf16[128,1536]{1,0:T(8,128)(2,1)S(1)}, bf16[128,1536]{1,0:T(8,128)(2,1)S(1)}, u32[]{:S(2)}, u32[]{:S(2)}) collective-permute-start(bf16[128,1536]{1,0:T(8,128)(2,1)S(1)} %get-tuple-element.53), channel_id=1, source_target_pairs={{1,2},{2,1},{3,4},{4,3},{5,6},{6,5},{7,8},{8,7},{9,10},{10,9},{11,... | collective-permute-start | bytes 1179656 | tf_op jit(solution)/shard_map/ppermute | solution.py:373
  47.2 4.1 %collective-permute-done.6.a_ref = bf16[128,1536]{1,0:T(8,128)(2,1)S(1)} collective-permute-done((bf16[128,1536]{1,0:T(8,128)(2,1)S(1)}, bf16[128,1536]{1,0:T(8,128)(2,1)S(1)}, u32[]{:S(2)}, u32[]{:S(2)}) %collective-permute-start.6) | collective-permute-done | bytes 393248 | tf_op jit(solution)/shard_map/ppermute | solution.py:364
  51.3 0.1 collective-permute-start.8
  51.4 4.2 %collective-permute-start.7 = (bf16[64,1536]{1,0:T(8,128)(2,1)S(1)}, bf16[64,1536]{1,0:T(8,128)(2,1)S(1)}, u32[]{:S(2)}, u32[]{:S(2)}) collective-permute-start(bf16[64,1536]{1,0:T(8,128)(2,1)S(1)} %get-tuple-element.89), channel_id=1, source_target_pairs={{1,2},{2,1},{3,4},{4,3},{5,6},{6,5},{7,8},{8,7},{9,10},{10,9},{11,... | collective-permute-start | bytes 589832 | tf_op jit(solution)/shard_map/ppermute | solution.py:373
  55.6 0.0 collective-permute-done.10.inner_ref
  55.6 0.0 copy-start.10
  55.6 0.9 copy-done.10
  56.5 1.6 %keys.2 = (bf16[128,1536]{1,0:T(8,128)(2,1)S(1)}, bf16[64,1536]{1,0:T(8,128)(2,1)S(1)}, bf16[64,1536]{1,0:T(8,128)(2,1)S(1)}) custom-call(s32[16,2]{1,0:T(8,128)S(1)} %copy.16.refs_0_.owner_ref, bf16[128,1536]{1,0:T(8,128)(2,1)S(1)} %get-tuple-element.52.own_ref, bf16[128,1536]{1,0:T(8,128)(2,1)S(1)} %collective-permute-done.9.cross_ref, ...), custom_call_target="tpu_custom_call" | custom-call | flops 7864320 | bytes 1376384 | tf_op jit(solution)/shard_map/keys/pallas_call | solution.py:321
  58.1 2.5 %collective-permute-start.11 = (bf16[64,1536]{1,0:T(8,128)(2,1)S(1)}, bf16[64,1536]{1,0:T(8,128)(2,1)S(1)}, u32[]{:S(2)}, u32[]{:S(2)}) collective-permute-start(bf16[64,1536]{1,0:T(8,128)(2,1)S(1)} %get-tuple-element.55), channel_id=1, source_target_pairs={{1,2},{2,1},{3,4},{4,3},{5,6},{6,5},{7,8},{8,7},{9,10},{10,9},{11,... | collective-permute-start | bytes 589832 | tf_op jit(solution)/shard_map/ppermute | solution.py:373
  60.6 2.7 %collective-permute-start.12 = (bf16[64,1536]{1,0:T(8,128)(2,1)S(1)}, bf16[64,1536]{1,0:T(8,128)(2,1)S(1)}, u32[]{:S(2)}, u32[]{:S(2)}) collective-permute-start(bf16[64,1536]{1,0:T(8,128)(2,1)S(1)} %get-tuple-element.56), channel_id=1, source_target_pairs={{0,1},{1,0},{2,3},{3,2},{4,5},{5,4},{6,7},{7,6},{8,9},{9,8},{10,11... | collective-permute-start | bytes 589832 | tf_op jit(solution)/shard_map/ppermute | solution.py:378
  63.3 1.0 local.2
  64.3 0.0 copy-start.6
  64.3 0.0 copy-start.7
  64.3 1.3 project.1.proj_ref
  65.7 2.3 %pool.3 = (bf16[128,1536]{1,0:T(8,128)(2,1)S(1)}, bf16[128,768]{1,0:T(8,128)(2,1)S(1)}) custom-call(bf16[64,1536]{1,0:T(8,128)(2,1)S(1)} %collective-permute-done.7.cross_ref, bf16[64,1536]{1,0:T(8,128)(2,1)S(1)} %collective-permute-done.8.inner_ref, bf16[1536,2304]{1,0:T(8,128)(2,1)S(1)} %bitcast.22, bf16[128,2304]{1,0:T(8,128)(2,1)S(1)} %project.1.proj_ref, ...), custom_call_target="tpu_custom_call" | custom-call | flops 603979776 | bytes 8226816 | tf_op jit(solution)/shard_map/pool/pallas_call | solution.py:321
  67.9 0.0 copy-start.2
  68.0 2.2 %final.2 = bf16[128,1536]{1,0:T(8,128)(2,1)S(1)} custom-call(bf16[64,1536]{1,0:T(8,128)(2,1)S(1)} %collective-permute-done.11.cross_ref, bf16[64,1536]{1,0:T(8,128)(2,1)S(1)} %collective-permute-done.12.inner_ref, f32[128,1536]{1,0:T(8,128)S(1)} %get-tuple-element.59.part_ref, f32[128,1536]{1,0:T(8,128)S(1)} %get-tuple-element.60.acc_ref, ...), custom_call_target="tpu_custom_call" | custom-call | flops 603979776 | bytes 9996288 | tf_op jit(solution)/shard_map/final/pallas_call | solution.py:321
  70.2 4.2 %collective-permute-start.15 = (bf16[128,1536]{1,0:T(8,128)(2,1)S(1)}, bf16[128,1536]{1,0:T(8,128)(2,1)S(1)}, u32[]{:S(2)}, u32[]{:S(2)}) collective-permute-start(bf16[128,1536]{1,0:T(8,128)(2,1)S(1)} %final.2), channel_id=1, source_target_pairs={{0,242},{1,243},{2,240},{3,241},{4,246},{5,247},{6,244},{7,245},{8... | collective-permute-start | bytes 1179656 | tf_op jit(solution)/shard_map/ppermute | solution.py:364
  74.4 3.5 %collective-permute-start.13 = (bf16[128,1536]{1,0:T(8,128)(2,1)S(1)}, bf16[128,1536]{1,0:T(8,128)(2,1)S(1)}, u32[]{:S(2)}, u32[]{:S(2)}) collective-permute-start(bf16[128,1536]{1,0:T(8,128)(2,1)S(1)} %get-tuple-element.61.own_ref), channel_id=1, source_target_pairs={{1,2},{2,1},{3,4},{4,3},{5,6},{6,5},{7,8},{8,7},{9,10},{10,9},{11,... | collective-permute-start | bytes 1179656 | tf_op jit(solution)/shard_map/ppermute | solution.py:373
  77.8 4.6 %collective-permute-done.15.gb_ref = bf16[128,1536]{1,0:T(8,128)(2,1)S(1)} collective-permute-done((bf16[128,1536]{1,0:T(8,128)(2,1)S(1)}, bf16[128,1536]{1,0:T(8,128)(2,1)S(1)}, u32[]{:S(2)}, u32[]{:S(2)}) %collective-permute-start.15) | collective-permute-done | bytes 393248 | tf_op jit(solution)/shard_map/ppermute | solution.py:364
  82.4 4.5 %collective-permute-start.18 = (bf16[128,1536]{1,0:T(8,128)(2,1)S(1)}, bf16[128,1536]{1,0:T(8,128)(2,1)S(1)}, u32[]{:S(2)}, u32[]{:S(2)}) collective-permute-start(bf16[128,1536]{1,0:T(8,128)(2,1)S(1)} %collective-permute-done.15.gb_ref), channel_id=1, source_target_pairs={{0,240},{1,241},{2,242},{3,243},{4,244},{5,245},{6,246},{7,247},{8... | collective-permute-start | bytes 1179656 | tf_op jit(solution)/shard_map/ppermute | solution.py:364
  86.9 0.9 gradatt.3.grad_ref
  87.8 3.5 %attention.1 = (bf16[128,768]{1,0:T(8,128)(2,1)S(1)}, bf16[128,768]{1,0:T(8,128)(2,1)S(1)}, bf16[128,1536]{1,0:T(8,128)(2,1)S(1)}, bf16[128,1536]{1,0:T(8,128)(2,1)S(1)}) custom-call(s32[16,2]{1,0:T(8,128)S(1)} %copy.16.refs_0_.owner_ref, f32[12]{0:T(128)S(1)} %bitcast.43, bf16[128,2304]{1,0:T(8,128)(2,1)S(1)} %project.1.proj_ref, ...), custom_call_target="tpu_custom_call" | custom-call | flops 805306368 | bytes 1966256 | tf_op jit(solution)/shard_map/attention/pallas_call | solution.py:321
  91.3 1.9 %collective-permute-start.17 = (bf16[128,1536]{1,0:T(8,128)(2,1)S(1)}, bf16[128,1536]{1,0:T(8,128)(2,1)S(1)}, u32[]{:S(2)}, u32[]{:S(2)}) collective-permute-start(bf16[128,1536]{1,0:T(8,128)(2,1)S(1)} %get-tuple-element.64), channel_id=1, source_target_pairs={{0,1},{1,0},{2,3},{3,2},{4,5},{5,4},{6,7},{7,6},{8,9},{9,8},{10,11... | collective-permute-start | bytes 1179656 | tf_op jit(solution)/shard_map/ppermute | solution.py:378
  93.2 2.6 %collective-permute-start.16 = (bf16[128,1536]{1,0:T(8,128)(2,1)S(1)}, bf16[128,1536]{1,0:T(8,128)(2,1)S(1)}, u32[]{:S(2)}, u32[]{:S(2)}) collective-permute-start(bf16[128,1536]{1,0:T(8,128)(2,1)S(1)} %get-tuple-element.64), channel_id=1, source_target_pairs={{1,2},{2,1},{3,4},{4,3},{5,6},{6,5},{7,8},{8,7},{9,10},{10,9},{11,... | collective-permute-start | bytes 1179656 | tf_op jit(solution)/shard_map/ppermute | solution.py:373
  95.8 1.5 %output.1 = bf16[128,1536]{1,0:T(8,128)(2,1)S(1)} custom-call(bf16[128,768]{1,0:T(8,128)(2,1)S(1)} %get-tuple-element.66.att_ref, bf16[768,1536]{1,0:T(8,128)(2,1)S(1)} %bitcast.29, bf16[128,1536]{1,0:T(8,128)(2,1)} %collective-permute-done.4.b_ref), custom_call_target="tpu_custom_call" | custom-call | flops 301989888 | bytes 2949120 | tf_op jit(solution)/shard_map/output/pallas_call | solution.py:321
  97.3 6.0 %collective-permute-done.16.cross_ref = bf16[128,1536]{1,0:T(8,128)(2,1)S(1)} collective-permute-done((bf16[128,1536]{1,0:T(8,128)(2,1)S(1)}, bf16[128,1536]{1,0:T(8,128)(2,1)S(1)}, u32[]{:S(2)}, u32[]{:S(2)}) %collective-permute-start.16) | collective-permute-done | bytes 393248 | tf_op jit(solution)/shard_map/ppermute | solution.py:373
  103.3 5.0 %collective-permute-start.21 = (bf16[128,1536]{1,0:T(8,128)(2,1)S(1)}, bf16[128,1536]{1,0:T(8,128)(2,1)S(1)}, u32[]{:S(2)}, u32[]{:S(2)}) collective-permute-start(bf16[128,1536]{1,0:T(8,128)(2,1)S(1)} %collective-permute-done.6.a_ref), channel_id=1, source_target_pairs={{0,240},{1,241},{2,242},{3,243},{4,244},{5,245},{6,246},{7,247},{8... | collective-permute-start | bytes 1179656 | tf_op jit(solution)/shard_map/ppermute | solution.py:364
  108.3 1.6 %keys.3 = (bf16[128,1536]{1,0:T(8,128)(2,1)S(1)}, bf16[64,1536]{1,0:T(8,128)(2,1)S(1)}, bf16[64,1536]{1,0:T(8,128)(2,1)S(1)}) custom-call(s32[16,2]{1,0:T(8,128)S(1)} %copy.16.refs_0_.owner_ref, bf16[128,1536]{1,0:T(8,128)(2,1)S(1)} %get-tuple-element.63.own_ref, bf16[128,1536]{1,0:T(8,128)(2,1)S(1)} %collective-permute-done.16.cross_ref, ...), custom_call_target="tpu_custom_call" | custom-call | flops 7864320 | bytes 1376384 | tf_op jit(solution)/shard_map/keys/pallas_call | solution.py:321
  109.9 4.2 %collective-permute-start.19 = (bf16[64,1536]{1,0:T(8,128)(2,1)S(1)}, bf16[64,1536]{1,0:T(8,128)(2,1)S(1)}, u32[]{:S(2)}, u32[]{:S(2)}) collective-permute-start(bf16[64,1536]{1,0:T(8,128)(2,1)S(1)} %get-tuple-element.71), channel_id=1, source_target_pairs={{1,2},{2,1},{3,4},{4,3},{5,6},{6,5},{7,8},{8,7},{9,10},{10,9},{11,... | collective-permute-start | bytes 589832 | tf_op jit(solution)/shard_map/ppermute | solution.py:373
  114.1 0.1 collective-permute-start.20
  114.2 1.0 local.3
  115.1 2.6 %collective-permute-done.19.cross_ref = bf16[64,1536]{1,0:T(8,128)(2,1)S(1)} collective-permute-done((bf16[64,1536]{1,0:T(8,128)(2,1)S(1)}, bf16[64,1536]{1,0:T(8,128)(2,1)S(1)}, u32[]{:S(2)}, u32[]{:S(2)}) %collective-permute-start.19) | collective-permute-done | bytes 196640 | tf_op jit(solution)/shard_map/ppermute | solution.py:373
  117.8 0.0 collective-permute-done.21.refs_1_
  117.8 2.2 %final.3 = bf16[128,1536]{1,0:T(8,128)(2,1)S(1)} custom-call(bf16[64,1536]{1,0:T(8,128)(2,1)S(1)} %collective-permute-done.19.cross_ref, bf16[64,1536]{1,0:T(8,128)(2,1)S(1)} %collective-permute-done.20.inner_ref, f32[128,1536]{1,0:T(8,128)S(1)} %get-tuple-element.85.part_ref, f32[128,1536]{1,0:T(8,128)S(1)} %get-tuple-element.86.acc_ref, ...), custom_call_target="tpu_custom_call" | custom-call | flops 603979776 | bytes 9996288 | tf_op jit(solution)/shard_map/final/pallas_call | solution.py:321
  120.0 5.7 %collective-permute-start.23 = (bf16[128,1536]{1,0:T(8,128)(2,1)S(1)}, bf16[128,1536]{1,0:T(8,128)(2,1)S(1)}, u32[]{:S(2)}, u32[]{:S(2)}) collective-permute-start(bf16[128,1536]{1,0:T(8,128)(2,1)S(1)} %final.3), channel_id=1, source_target_pairs={{0,240},{1,241},{2,242},{3,243},{4,244},{5,245},{6,246},{7,247},{8... | collective-permute-start | bytes 1179656 | tf_op jit(solution)/shard_map/ppermute | solution.py:364
  125.7 0.1 collective-permute-start.22
  125.8 8.8 %collective-permute-done.23 = bf16[128,1536]{1,0:T(8,128)(2,1)S(1)} collective-permute-done((bf16[128,1536]{1,0:T(8,128)(2,1)S(1)}, bf16[128,1536]{1,0:T(8,128)(2,1)S(1)}, u32[]{:S(2)}, u32[]{:S(2)}) %collective-permute-start.23) | collective-permute-done | bytes 393248 | tf_op jit(solution)/shard_map/ppermute | solution.py:364
  134.6 8.0 %collective-permute-done.22.refs_0_ = bf16[128,1536]{1,0:T(8,128)(2,1)S(1)} collective-permute-done((bf16[128,1536]{1,0:T(8,128)(2,1)S(1)}, bf16[128,1536]{1,0:T(8,128)(2,1)S(1)}, u32[]{:S(2)}, u32[]{:S(2)}) %collective-permute-start.22) | collective-permute-done | bytes 393248 | tf_op jit(solution)/shard_map/ppermute | solution.py:364
  142.5 1.1 settle.1
  143.6 0.7 copy.18
  (35 shorter events, 0.1 us)
Async XLA Ops:
  0.6 17.2 %copy-start.3 = (f32[1,27,1536]{2,0,1:T(1,128)S(1)}, f32[1,27,1536]{2,0,1:T(1,128)}, u32[]{:S(2)}) copy-start(f32[1,27,1536]{2,0,1:T(1,128)} %param.15) | copy-start | bytes 497668
  0.7 17.2 %copy-start = (bf16[1,1536,2304]{2,1,0:T(8,128)(2,1)S(1)}, bf16[1,1536,2304]{2,1,0:T(8,128)(2,1)}, u32[]{:S(2)}) copy-start(bf16[1,1536,2304]{2,1,0:T(8,128)(2,1)} %param.13) | copy-start | bytes 21233668
  1.9 16.0 %collective-permute-start.1 = (bf16[64,1536]{1,0:T(8,128)(2,1)S(1)}, bf16[64,1536]{1,0:T(8,128)(2,1)S(1)}, u32[]{:S(2)}, u32[]{:S(2)}) collective-permute-start(bf16[64,1536]{1,0:T(8,128)(2,1)S(1)} %get-tuple-element.90), channel_id=1, source_target_pairs={{0,1},{1,0},{2,3},{3,2},{4,5},{5,4},{6,7},{7,6},{8,9},{9,8},{10,11... | collective-permute-start | bytes 589832 | tf_op jit(solution)/shard_map/ppermute | solution.py:378
  2.6 15.2 %collective-permute-start = (bf16[64,1536]{1,0:T(8,128)(2,1)S(1)}, bf16[64,1536]{1,0:T(8,128)(2,1)S(1)}, u32[]{:S(2)}, u32[]{:S(2)}) collective-permute-start(bf16[64,1536]{1,0:T(8,128)(2,1)S(1)} %get-tuple-element.91), channel_id=1, source_target_pairs={{1,2},{2,1},{3,4},{4,3},{5,6},{6,5},{7,8},{8,7},{9,10},{10,9},{11,... | collective-permute-start | bytes 589832 | tf_op jit(solution)/shard_map/ppermute | solution.py:373
  5.8 24.3 %collective-permute-start.5 = (bf16[128,1536]{1,0:T(8,128)(2,1)}, bf16[128,1536]{1,0:T(8,128)(2,1)S(1)}, u32[]{:S(2)}, u32[]{:S(2)}) collective-permute-start(bf16[128,1536]{1,0:T(8,128)(2,1)} %bitcast.40), channel_id=1, source_target_pairs={{0,242},{1,243},{2,240},{3,241},{4,246},{5,247},{6,244},{7,245},{8... | collective-permute-start | bytes 1179656 | tf_op jit(solution)/shard_map/ppermute | solution.py:364
  12.4 17.8 %collective-permute-start.4 = (bf16[128,1536]{1,0:T(8,128)(2,1)}, bf16[128,1536]{1,0:T(8,128)(2,1)}, u32[]{:S(2)}, u32[]{:S(2)}) collective-permute-start(bf16[128,1536]{1,0:T(8,128)(2,1)} %bitcast.36), channel_id=1, source_target_pairs={{0,242},{1,243},{2,240},{3,241},{4,246},{5,247},{6,244},{7,245},{8... | collective-permute-start | bytes 1179656 | tf_op jit(solution)/shard_map/ppermute | solution.py:364
  13.1 13.4 %copy-start.12 = (s32[16,2]{0,1:T(2,128)S(1)}, s32[16,2]{0,1:T(2,128)}, u32[]{:S(2)}) copy-start(s32[16,2]{0,1:T(2,128)} %param.17) | copy-start | bytes 388
  17.8 3.1 %copy-start.4 = (bf16[128,2304]{1,0:T(8,128)(2,1)}, bf16[128,2304]{1,0:T(8,128)(2,1)S(1)}, u32[]{:S(2)}) copy-start(bf16[128,2304]{1,0:T(8,128)(2,1)S(1)} %firstproject.1.proj_ref.refs_2_) | copy-start | bytes 1769476
  17.8 15.1 %copy-start.11 = (f32[1,12]{1,0:T(1,128)S(1)}, f32[1,12]{1,0:T(1,128)}, u32[]{:S(2)}) copy-start(f32[1,12]{1,0:T(1,128)} %param.16) | copy-start | bytes 148
  17.9 45.4 %slice-start = ((s8[7077888]{0:T(1024)(128)(4,1)}), s8[2883584]{0:T(1024)(128)(4,1)S(1)}, s32[]{:S(2)}) async-start(s8[7077888]{0:T(1024)(128)(4,1)} %bitcast.18), calls=%async_computation | async-start | bytes 5767168
  20.9 0.7 copy-start.9
  21.6 8.6 %collective-permute-start.3 = (bf16[128,1536]{1,0:T(8,128)(2,1)}, bf16[128,1536]{1,0:T(8,128)(2,1)}, u32[]{:S(2)}, u32[]{:S(2)}) collective-permute-start(bf16[128,1536]{1,0:T(8,128)(2,1)} %get-tuple-element.46.refs_3_), channel_id=1, source_target_pairs={{0,1},{1,0},{2,3},{3,2},{4,5},{5,4},{6,7},{7,6},{8,9},{9,8},{10,11... | collective-permute-start | bytes 1179656 | tf_op jit(solution)/shard_map/ppermute | solution.py:378
  22.5 10.4 %collective-permute-start.2 = (bf16[128,1536]{1,0:T(8,128)(2,1)}, bf16[128,1536]{1,0:T(8,128)(2,1)}, u32[]{:S(2)}, u32[]{:S(2)}) collective-permute-start(bf16[128,1536]{1,0:T(8,128)(2,1)} %get-tuple-element.46.refs_3_), channel_id=1, source_target_pairs={{1,2},{2,1},{3,4},{4,3},{5,6},{6,5},{7,8},{8,7},{9,10},{10,9},{11,... | collective-permute-start | bytes 1179656 | tf_op jit(solution)/shard_map/ppermute | solution.py:373
  26.6 1.7 %copy-start.1 = (bf16[1,768,1536]{2,1,0:T(8,128)(2,1)S(1)}, bf16[1,768,1536]{2,1,0:T(8,128)(2,1)}, u32[]{:S(2)}) copy-start(bf16[1,768,1536]{2,1,0:T(8,128)(2,1)} %param.14) | copy-start | bytes 7077892
  28.3 1.0 copy-start.8
  29.3 34.0 %slice-start.1 = ((s8[7077888]{0:T(1024)(128)(4,1)}), s8[4194304]{0:T(1024)(128)(4,1)S(1)}, s32[]{:S(2)}) async-start(s8[7077888]{0:T(1024)(128)(4,1)} %bitcast.18), calls=%async_computation.1 | async-start | bytes 8388608
  32.9 1.1 copy-start.5
  38.8 12.4 %collective-permute-start.6 = (bf16[128,1536]{1,0:T(8,128)(2,1)S(1)}, bf16[128,1536]{1,0:T(8,128)(2,1)S(1)}, u32[]{:S(2)}, u32[]{:S(2)}) collective-permute-start(bf16[128,1536]{1,0:T(8,128)(2,1)S(1)} %get-tuple-element.50), channel_id=1, source_target_pairs={{0,242},{1,243},{2,240},{3,241},{4,246},{5,247},{6,244},{7,245},{8... | collective-permute-start | bytes 1179656 | tf_op jit(solution)/shard_map/ppermute | solution.py:364
  42.8 12.7 %collective-permute-start.10 = (bf16[128,1536]{1,0:T(8,128)(2,1)S(1)}, bf16[128,1536]{1,0:T(8,128)(2,1)S(1)}, u32[]{:S(2)}, u32[]{:S(2)}) collective-permute-start(bf16[128,1536]{1,0:T(8,128)(2,1)S(1)} %get-tuple-element.53), channel_id=1, source_target_pairs={{0,1},{1,0},{2,3},{3,2},{4,5},{5,4},{6,7},{7,6},{8,9},{9,8},{10,11... | collective-permute-start | bytes 1179656 | tf_op jit(solution)/shard_map/ppermute | solution.py:378
  42.8 12.7 %collective-permute-start.9 = (bf16[128,1536]{1,0:T(8,128)(2,1)S(1)}, bf16[128,1536]{1,0:T(8,128)(2,1)S(1)}, u32[]{:S(2)}, u32[]{:S(2)}) collective-permute-start(bf16[128,1536]{1,0:T(8,128)(2,1)S(1)} %get-tuple-element.53), channel_id=1, source_target_pairs={{1,2},{2,1},{3,4},{4,3},{5,6},{6,5},{7,8},{8,7},{9,10},{10,9},{11,... | collective-permute-start | bytes 1179656 | tf_op jit(solution)/shard_map/ppermute | solution.py:373
  51.3 14.4 %collective-permute-start.8 = (bf16[64,1536]{1,0:T(8,128)(2,1)S(1)}, bf16[64,1536]{1,0:T(8,128)(2,1)S(1)}, u32[]{:S(2)}, u32[]{:S(2)}) collective-permute-start(bf16[64,1536]{1,0:T(8,128)(2,1)S(1)} %get-tuple-element.88), channel_id=1, source_target_pairs={{0,1},{1,0},{2,3},{3,2},{4,5},{5,4},{6,7},{7,6},{8,9},{9,8},{10,11... | collective-permute-start | bytes 589832 | tf_op jit(solution)/shard_map/ppermute | solution.py:378
  51.4 14.3 %collective-permute-start.7 = (bf16[64,1536]{1,0:T(8,128)(2,1)S(1)}, bf16[64,1536]{1,0:T(8,128)(2,1)S(1)}, u32[]{:S(2)}, u32[]{:S(2)}) collective-permute-start(bf16[64,1536]{1,0:T(8,128)(2,1)S(1)} %get-tuple-element.89), channel_id=1, source_target_pairs={{1,2},{2,1},{3,4},{4,3},{5,6},{6,5},{7,8},{8,7},{9,10},{10,9},{11,... | collective-permute-start | bytes 589832 | tf_op jit(solution)/shard_map/ppermute | solution.py:373
  55.6 0.9 copy-start.10
  58.1 9.8 %collective-permute-start.11 = (bf16[64,1536]{1,0:T(8,128)(2,1)S(1)}, bf16[64,1536]{1,0:T(8,128)(2,1)S(1)}, u32[]{:S(2)}, u32[]{:S(2)}) collective-permute-start(bf16[64,1536]{1,0:T(8,128)(2,1)S(1)} %get-tuple-element.55), channel_id=1, source_target_pairs={{1,2},{2,1},{3,4},{4,3},{5,6},{6,5},{7,8},{8,7},{9,10},{10,9},{11,... | collective-permute-start | bytes 589832 | tf_op jit(solution)/shard_map/ppermute | solution.py:373
  60.6 7.4 %collective-permute-start.12 = (bf16[64,1536]{1,0:T(8,128)(2,1)S(1)}, bf16[64,1536]{1,0:T(8,128)(2,1)S(1)}, u32[]{:S(2)}, u32[]{:S(2)}) collective-permute-start(bf16[64,1536]{1,0:T(8,128)(2,1)S(1)} %get-tuple-element.56), channel_id=1, source_target_pairs={{0,1},{1,0},{2,3},{3,2},{4,5},{5,4},{6,7},{7,6},{8,9},{9,8},{10,11... | collective-permute-start | bytes 589832 | tf_op jit(solution)/shard_map/ppermute | solution.py:378
  64.3 3.7 %copy-start.6 = (bf16[1,128,1536]{2,1,0:T(8,128)(2,1)S(1)}, bf16[1,128,1536]{2,1,0:T(8,128)(2,1)}, u32[]{:S(2)}) copy-start(bf16[1,128,1536]{2,1,0:T(8,128)(2,1)} %param.9) | copy-start | bytes 1179652
  64.3 3.7 %copy-start.7 = (bf16[1,128,1536]{2,1,0:T(8,128)(2,1)S(1)}, bf16[1,128,1536]{2,1,0:T(8,128)(2,1)}, u32[]{:S(2)}) copy-start(bf16[1,128,1536]{2,1,0:T(8,128)(2,1)} %param.11) | copy-start | bytes 1179652
  67.9 19.0 %copy-start.2 = (bf16[1,768,1536]{2,1,0:T(8,128)(2,1)S(1)}, bf16[1,768,1536]{2,1,0:T(8,128)(2,1)}, u32[]{:S(2)}) copy-start(bf16[1,768,1536]{2,1,0:T(8,128)(2,1)} %param.14) | copy-start | bytes 7077892
  70.2 12.3 %collective-permute-start.15 = (bf16[128,1536]{1,0:T(8,128)(2,1)S(1)}, bf16[128,1536]{1,0:T(8,128)(2,1)S(1)}, u32[]{:S(2)}, u32[]{:S(2)}) collective-permute-start(bf16[128,1536]{1,0:T(8,128)(2,1)S(1)} %final.2), channel_id=1, source_target_pairs={{0,242},{1,243},{2,240},{3,241},{4,246},{5,247},{6,244},{7,245},{8... | collective-permute-start | bytes 1179656 | tf_op jit(solution)/shard_map/ppermute | solution.py:364
  74.4 13.5 %collective-permute-start.14 = (bf16[128,1536]{1,0:T(8,128)(2,1)S(1)}, bf16[128,1536]{1,0:T(8,128)(2,1)S(1)}, u32[]{:S(2)}, u32[]{:S(2)}) collective-permute-start(bf16[128,1536]{1,0:T(8,128)(2,1)S(1)} %get-tuple-element.61.own_ref), channel_id=1, source_target_pairs={{0,1},{1,0},{2,3},{3,2},{4,5},{5,4},{6,7},{7,6},{8,9},{9,8},{10,11... | collective-permute-start | bytes 1179656 | tf_op jit(solution)/shard_map/ppermute | solution.py:378
  74.4 13.5 %collective-permute-start.13 = (bf16[128,1536]{1,0:T(8,128)(2,1)S(1)}, bf16[128,1536]{1,0:T(8,128)(2,1)S(1)}, u32[]{:S(2)}, u32[]{:S(2)}) collective-permute-start(bf16[128,1536]{1,0:T(8,128)(2,1)S(1)} %get-tuple-element.61.own_ref), channel_id=1, source_target_pairs={{1,2},{2,1},{3,4},{4,3},{5,6},{6,5},{7,8},{8,7},{9,10},{10,9},{11,... | collective-permute-start | bytes 1179656 | tf_op jit(solution)/shard_map/ppermute | solution.py:373
  82.4 13.3 %collective-permute-start.18 = (bf16[128,1536]{1,0:T(8,128)(2,1)S(1)}, bf16[128,1536]{1,0:T(8,128)(2,1)S(1)}, u32[]{:S(2)}, u32[]{:S(2)}) collective-permute-start(bf16[128,1536]{1,0:T(8,128)(2,1)S(1)} %collective-permute-done.15.gb_ref), channel_id=1, source_target_pairs={{0,240},{1,241},{2,242},{3,243},{4,244},{5,245},{6,246},{7,247},{8... | collective-permute-start | bytes 1179656 | tf_op jit(solution)/shard_map/ppermute | solution.py:364
  91.3 5.9 %collective-permute-start.17 = (bf16[128,1536]{1,0:T(8,128)(2,1)S(1)}, bf16[128,1536]{1,0:T(8,128)(2,1)S(1)}, u32[]{:S(2)}, u32[]{:S(2)}) collective-permute-start(bf16[128,1536]{1,0:T(8,128)(2,1)S(1)} %get-tuple-element.64), channel_id=1, source_target_pairs={{0,1},{1,0},{2,3},{3,2},{4,5},{5,4},{6,7},{7,6},{8,9},{9,8},{10,11... | collective-permute-start | bytes 1179656 | tf_op jit(solution)/shard_map/ppermute | solution.py:378
  93.2 10.1 %collective-permute-start.16 = (bf16[128,1536]{1,0:T(8,128)(2,1)S(1)}, bf16[128,1536]{1,0:T(8,128)(2,1)S(1)}, u32[]{:S(2)}, u32[]{:S(2)}) collective-permute-start(bf16[128,1536]{1,0:T(8,128)(2,1)S(1)} %get-tuple-element.64), channel_id=1, source_target_pairs={{1,2},{2,1},{3,4},{4,3},{5,6},{6,5},{7,8},{8,7},{9,10},{10,9},{11,... | collective-permute-start | bytes 1179656 | tf_op jit(solution)/shard_map/ppermute | solution.py:373
  103.3 14.5 %collective-permute-start.21 = (bf16[128,1536]{1,0:T(8,128)(2,1)S(1)}, bf16[128,1536]{1,0:T(8,128)(2,1)S(1)}, u32[]{:S(2)}, u32[]{:S(2)}) collective-permute-start(bf16[128,1536]{1,0:T(8,128)(2,1)S(1)} %collective-permute-done.6.a_ref), channel_id=1, source_target_pairs={{0,240},{1,241},{2,242},{3,243},{4,244},{5,245},{6,246},{7,247},{8... | collective-permute-start | bytes 1179656 | tf_op jit(solution)/shard_map/ppermute | solution.py:364
  109.9 7.9 %collective-permute-start.19 = (bf16[64,1536]{1,0:T(8,128)(2,1)S(1)}, bf16[64,1536]{1,0:T(8,128)(2,1)S(1)}, u32[]{:S(2)}, u32[]{:S(2)}) collective-permute-start(bf16[64,1536]{1,0:T(8,128)(2,1)S(1)} %get-tuple-element.71), channel_id=1, source_target_pairs={{1,2},{2,1},{3,4},{4,3},{5,6},{6,5},{7,8},{8,7},{9,10},{10,9},{11,... | collective-permute-start | bytes 589832 | tf_op jit(solution)/shard_map/ppermute | solution.py:373
  114.1 3.7 %collective-permute-start.20 = (bf16[64,1536]{1,0:T(8,128)(2,1)S(1)}, bf16[64,1536]{1,0:T(8,128)(2,1)S(1)}, u32[]{:S(2)}, u32[]{:S(2)}) collective-permute-start(bf16[64,1536]{1,0:T(8,128)(2,1)S(1)} %get-tuple-element.72), channel_id=1, source_target_pairs={{0,1},{1,0},{2,3},{3,2},{4,5},{5,4},{6,7},{7,6},{8,9},{9,8},{10,11... | collective-permute-start | bytes 589832 | tf_op jit(solution)/shard_map/ppermute | solution.py:378
  120.0 14.6 %collective-permute-start.23 = (bf16[128,1536]{1,0:T(8,128)(2,1)S(1)}, bf16[128,1536]{1,0:T(8,128)(2,1)S(1)}, u32[]{:S(2)}, u32[]{:S(2)}) collective-permute-start(bf16[128,1536]{1,0:T(8,128)(2,1)S(1)} %final.3), channel_id=1, source_target_pairs={{0,240},{1,241},{2,242},{3,243},{4,244},{5,245},{6,246},{7,247},{8... | collective-permute-start | bytes 1179656 | tf_op jit(solution)/shard_map/ppermute | solution.py:364
  125.7 16.8 %collective-permute-start.22 = (bf16[128,1536]{1,0:T(8,128)(2,1)S(1)}, bf16[128,1536]{1,0:T(8,128)(2,1)S(1)}, u32[]{:S(2)}, u32[]{:S(2)}) collective-permute-start(bf16[128,1536]{1,0:T(8,128)(2,1)S(1)} %output.1), channel_id=1, source_target_pairs={{0,240},{1,241},{2,242},{3,243},{4,244},{5,245},{6,246},{7,247},{8... | collective-permute-start | bytes 1179656 | tf_op jit(solution)/shard_map/ppermute | solution.py:364

commit v5 on v3

--- a/solution.py
+++ b/solution.py
@@ -507,19 +507,17 @@
     one, two, start = first_layout, second_layout, start_layout
 
     halo = exchange(*edges(a), start, one)
+    b2 = move(a, one, two, -1)
+    ga2 = move(gb, one, two, -1)
     q1, raw1 = first_project(a, w_qkv)
     cross, inner = halo
     kv1, pk1 = forward_pool(raw1, cross, inner, w_qkv, kern)
-    kv1, a_pass, gb_pass = together(kv1, a, gb)
     cross, inner = exchange(kv1, kv1, one)
-    b2 = move(a_pass, one, two, -1)
-    ga2 = move(gb_pass, one, two, -1)
     grad1 = grad_attended(gb, w_out)
-    cross, inner, grad1 = together(cross, inner, grad1)
+    cross, inner, b2, ga2, grad1 = together(cross, inner, b2, ga2, grad1)
     _, gq1, own1, near1, rebuilt1 = attend_rebuild(
         one, owner, tau, q1, kv1, cross, inner, grad1, w_out, b
     )
-    near1, b2, ga2 = together(near1, b2, ga2)
     cross, inner = exchange(near1, near1, one)
     a2 = move(rebuilt1, one, two, -1)
     gpool1, cross, inner = key_sums(one, owner, own1, cross, inner, pk1)

time: 148 us -> 146 us (0.986); the launches traced: 146 us -> 145 us
  starting transfers between devices: 74.2 us -> 64.6 us
  waiting for transfers between devices: 29.3 us -> 38.2 us
    ppermute x8, starting transfers between devices: 35.2 us -> 28 us  [move(): return lax.ppermute(value, AXES, pairs)]
    ppermute x8, waiting for transfers between devices: 21.3 us -> 26.6 us  [move(): return lax.ppermute(value, AXES, pairs)]
    ppermute x8, waiting for transfers between devices: 8.06 us -> 11.6 us  [swap_cross(): return lax.ppermute(value, AXES, pairs)]
    ppermute x8, starting transfers between devices: 30.8 us -> 28.3 us  [swap_cross(): return lax.ppermute(value, AXES, pairs)]
  transfers between devices with their start and end apart: 24 -> 24, of which waited for: 7 -> 8; matrix products, arithmetic and copies ran while one was open for 0% -> 0% of each run, Pallas kernels for 17% -> 16%
where the time goes in v5:
time: 146 us; the launch traced here: 145 us
  starting transfers between devices  64.6 us (44%)
  waiting for transfers between devices  38.2 us (26%)
  Pallas kernels  33.5 us (23%)
  local copies, waits for them, and re-layouts  7.96 us (5%)
    pallas_call x16, Pallas kernels, run(): pl.pallas_call(kernel, name=name, out_shape=[jax.ShapeDtypeStruct(s, kind...  33.5 us
    ppermute x8, starting transfers between devices, swap_cross(): return lax.ppermute(value, AXES, pairs)  28.3 us
    ppermute x8, starting transfers between devices, move(): return lax.ppermute(value, AXES, pairs)  28 us
    ppermute x8, waiting for transfers between devices, move(): return lax.ppermute(value, AXES, pairs)  26.6 us
    ppermute x8, waiting for transfers between devices, swap_cross(): return lax.ppermute(value, AXES, pairs)  11.6 us
    ppermute x8, starting transfers between devices, swap_inner(): return lax.ppermute(value, AXES, pairs)  8.35 us
    unnamed x32, local copies, waits for them, and re-layouts  6.73 us
  transfers between devices with their start and end apart: 24, of which 8 were waited for; matrix products, arithmetic and copies ran while one was open for 0% of the time, Pallas kernels for 16%

profile of v5, /device:TPU:11, one launch (start us, length us, event | category | flops | bytes accessed | tf_op | source)
XLA Modules:
  0.0 145.4 jit_solution(5512095547125948871)
XLA Ops:
  0.7 0.0 copy-start
  0.7 1.2 dynamic-slice_bitcast_fusion
  1.9 0.8 collective-permute-start.1
  2.6 3.2 %collective-permute-start = (bf16[64,1536]{1,0:T(8,128)(2,1)S(1)}, bf16[64,1536]{1,0:T(8,128)(2,1)S(1)}, u32[]{:S(2)}, u32[]{:S(2)}) collective-permute-start(bf16[64,1536]{1,0:T(8,128)(2,1)S(1)} %get-tuple-element.99), channel_id=1, source_target_pairs={{1,2},{2,1},{3,4},{4,3},{5,6},{6,5},{7,8},{8,7},{9,10},{10,9},{11,... | collective-permute-start | bytes 589832 | tf_op jit(solution)/shard_map/ppermute | solution.py:380
  5.8 6.6 %collective-permute-start.5 = (bf16[128,1536]{1,0:T(8,128)(2,1)}, bf16[128,1536]{1,0:T(8,128)(2,1)S(1)}, u32[]{:S(2)}, u32[]{:S(2)}) collective-permute-start(bf16[128,1536]{1,0:T(8,128)(2,1)} %bitcast.40), channel_id=1, source_target_pairs={{0,242},{1,243},{2,240},{3,241},{4,246},{5,247},{6,244},{7,245},{8... | collective-permute-start | bytes 1179656 | tf_op jit(solution)/shard_map/ppermute | solution.py:371
  12.4 0.7 collective-permute-start.4
  13.1 4.7 %firstproject.1 = (bf16[128,768]{1,0:T(8,128)(2,1)S(1)}, bf16[128,1536]{1,0:T(8,128)(2,1)S(1)}) custom-call(bf16[128,1536]{1,0:T(8,128)(2,1)} %bitcast.37, bf16[1536,2304]{1,0:T(8,128)(2,1)} %bitcast.16), custom_call_target="tpu_custom_call" | custom-call | flops 905969664 | bytes 7471104 | tf_op jit(solution)/shard_map/firstproject/pallas_call | solution.py:328
  17.8 0.0 copy-start.7
  17.8 0.7 copy-done.7
  18.5 0.0 collective-permute-done.1.inner_ref
  18.5 0.0 collective-permute-done.cross_ref
  18.5 0.0 slice-start
  18.5 3.0 %pool.2 = (bf16[128,1536]{1,0:T(8,128)(2,1)}, bf16[128,768]{1,0:T(8,128)(2,1)S(1)}) custom-call(bf16[64,1536]{1,0:T(8,128)(2,1)S(1)} %collective-permute-done.cross_ref, bf16[64,1536]{1,0:T(8,128)(2,1)S(1)} %collective-permute-done.1.inner_ref, bf16[1536,2304]{1,0:T(8,128)(2,1)S(1)} %bitcast.17, bf16[128,1536]{1,0:T(8,128)(2,1)S(1)} %get-tuple-element.51.raw_ref, ...), custom_call_target="tpu_custom_call" | custom-call | flops 603979776 | bytes 8030208 | tf_op jit(solution)/shard_map/pool/pallas_call | solution.py:328
  21.6 0.7 copy-done.9
  22.2 0.9 collective-permute-start.3
  23.1 4.0 %collective-permute-start.2 = (bf16[128,1536]{1,0:T(8,128)(2,1)}, bf16[128,1536]{1,0:T(8,128)(2,1)}, u32[]{:S(2)}, u32[]{:S(2)}) collective-permute-start(bf16[128,1536]{1,0:T(8,128)(2,1)} %get-tuple-element.52.refs_3_), channel_id=1, source_target_pairs={{1,2},{2,1},{3,4},{4,3},{5,6},{6,5},{7,8},{8,7},{9,10},{10,9},{11,... | collective-permute-start | bytes 1179656 | tf_op jit(solution)/shard_map/ppermute | solution.py:380
  27.2 0.1 copy.16.refs_0_.owner_ref
  27.3 1.7 %copy-done.1 = bf16[1,768,1536]{2,1,0:T(8,128)(2,1)S(1)} copy-done((bf16[1,768,1536]{2,1,0:T(8,128)(2,1)S(1)}, bf16[1,768,1536]{2,1,0:T(8,128)(2,1)}, u32[]{:S(2)}) %copy-start.1) | copy-done | bytes 2359320
  28.9 1.0 copy-done.6
  29.9 0.9 gradatt.2.refs_6_
  30.8 2.7 %collective-permute-done.2.refs_4_ = bf16[128,1536]{1,0:T(8,128)(2,1)} collective-permute-done((bf16[128,1536]{1,0:T(8,128)(2,1)}, bf16[128,1536]{1,0:T(8,128)(2,1)}, u32[]{:S(2)}, u32[]{:S(2)}) %collective-permute-start.2) | collective-permute-done | bytes 393248 | tf_op jit(solution)/shard_map/ppermute | solution.py:380
  33.5 0.9 copy-done.8
  34.4 4.9 %attendout.1 = (bf16[128,768]{1,0:T(8,128)(2,1)}, bf16[128,768]{1,0:T(8,128)(2,1)S(1)}, bf16[128,1536]{1,0:T(8,128)(2,1)S(1)}, bf16[128,1536]{1,0:T(8,128)(2,1)S(1)}, bf16[128,1536]{1,0:T(8,128)(2,1)S(1)}) custom-call(s32[16,2]{1,0:T(8,128)S(1)} %copy.16.refs_0_.owner_ref, f32[12]{0:T(128)S(1)} %bitcast.42, bf16[128,768]{1,0:T(8,128)(2,1)S(1)} %copy-done.8, ...), custom_call_target="tpu_custom_call" | custom-call | flops 805306368 | bytes 4325552 | tf_op jit(solution)/shard_map/attendout/pallas_call | solution.py:328
  39.3 4.0 %collective-permute-start.6 = (bf16[128,1536]{1,0:T(8,128)(2,1)S(1)}, bf16[128,1536]{1,0:T(8,128)(2,1)S(1)}, u32[]{:S(2)}, u32[]{:S(2)}) collective-permute-start(bf16[128,1536]{1,0:T(8,128)(2,1)S(1)} %get-tuple-element.56), channel_id=1, source_target_pairs={{0,242},{1,243},{2,240},{3,241},{4,246},{5,247},{6,244},{7,245},{8... | collective-permute-start | bytes 1179656 | tf_op jit(solution)/shard_map/ppermute | solution.py:371
  43.4 4.3 %collective-permute-start.9 = (bf16[128,1536]{1,0:T(8,128)(2,1)S(1)}, bf16[128,1536]{1,0:T(8,128)(2,1)S(1)}, u32[]{:S(2)}, u32[]{:S(2)}) collective-permute-start(bf16[128,1536]{1,0:T(8,128)(2,1)S(1)} %get-tuple-element.61), channel_id=1, source_target_pairs={{1,2},{2,1},{3,4},{4,3},{5,6},{6,5},{7,8},{8,7},{9,10},{10,9},{11,... | collective-permute-start | bytes 1179656 | tf_op jit(solution)/shard_map/ppermute | solution.py:380
  47.7 4.1 %collective-permute-done.6.a_ref = bf16[128,1536]{1,0:T(8,128)(2,1)S(1)} collective-permute-done((bf16[128,1536]{1,0:T(8,128)(2,1)S(1)}, bf16[128,1536]{1,0:T(8,128)(2,1)S(1)}, u32[]{:S(2)}, u32[]{:S(2)}) %collective-permute-start.6) | collective-permute-done | bytes 393248 | tf_op jit(solution)/shard_map/ppermute | solution.py:371
  51.8 0.1 collective-permute-start.8
  51.9 4.2 %collective-permute-start.7 = (bf16[64,1536]{1,0:T(8,128)(2,1)S(1)}, bf16[64,1536]{1,0:T(8,128)(2,1)S(1)}, u32[]{:S(2)}, u32[]{:S(2)}) collective-permute-start(bf16[64,1536]{1,0:T(8,128)(2,1)S(1)} %get-tuple-element.97), channel_id=1, source_target_pairs={{1,2},{2,1},{3,4},{4,3},{5,6},{6,5},{7,8},{8,7},{9,10},{10,9},{11,... | collective-permute-start | bytes 589832 | tf_op jit(solution)/shard_map/ppermute | solution.py:380
  56.1 0.0 copy-start.10
  56.1 0.9 copy-done.10
  57.1 1.6 %keys.2 = (bf16[128,1536]{1,0:T(8,128)(2,1)S(1)}, bf16[64,1536]{1,0:T(8,128)(2,1)S(1)}, bf16[64,1536]{1,0:T(8,128)(2,1)S(1)}) custom-call(s32[16,2]{1,0:T(8,128)S(1)} %copy.16.refs_0_.owner_ref, bf16[128,1536]{1,0:T(8,128)(2,1)S(1)} %get-tuple-element.60.own_ref, bf16[128,1536]{1,0:T(8,128)(2,1)S(1)} %collective-permute-done.9.cross_ref, ...), custom_call_target="tpu_custom_call" | custom-call | flops 7864320 | bytes 1376384 | tf_op jit(solution)/shard_map/keys/pallas_call | solution.py:328
  58.7 2.4 %collective-permute-start.11 = (bf16[64,1536]{1,0:T(8,128)(2,1)S(1)}, bf16[64,1536]{1,0:T(8,128)(2,1)S(1)}, u32[]{:S(2)}, u32[]{:S(2)}) collective-permute-start(bf16[64,1536]{1,0:T(8,128)(2,1)S(1)} %get-tuple-element.63), channel_id=1, source_target_pairs={{1,2},{2,1},{3,4},{4,3},{5,6},{6,5},{7,8},{8,7},{9,10},{10,9},{11,... | collective-permute-start | bytes 589832 | tf_op jit(solution)/shard_map/ppermute | solution.py:380
  61.1 4.6 %collective-permute-start.12 = (bf16[64,1536]{1,0:T(8,128)(2,1)S(1)}, bf16[64,1536]{1,0:T(8,128)(2,1)S(1)}, u32[]{:S(2)}, u32[]{:S(2)}) collective-permute-start(bf16[64,1536]{1,0:T(8,128)(2,1)S(1)} %get-tuple-element.64), channel_id=1, source_target_pairs={{0,1},{1,0},{2,3},{3,2},{4,5},{5,4},{6,7},{7,6},{8,9},{9,8},{10,11... | collective-permute-start | bytes 589832 | tf_op jit(solution)/shard_map/ppermute | solution.py:385
  65.7 1.0 local.2
  66.7 0.0 copy-start.4
  66.7 0.0 copy-start.5
  66.8 1.3 project.1
  68.1 2.3 %pool.3 = (bf16[128,1536]{1,0:T(8,128)(2,1)S(1)}, bf16[128,768]{1,0:T(8,128)(2,1)S(1)}) custom-call(bf16[64,1536]{1,0:T(8,128)(2,1)S(1)} %collective-permute-done.7.cross_ref, bf16[64,1536]{1,0:T(8,128)(2,1)S(1)} %collective-permute-done.8.inner_ref, bf16[1536,2304]{1,0:T(8,128)(2,1)S(1)} %bitcast.22, bf16[128,1536]{1,0:T(8,128)(2,1)S(1)} %get-tuple-element.58.raw_ref, ...), custom_call_target="tpu_custom_call" | custom-call | flops 603979776 | bytes 8030208 | tf_op jit(solution)/shard_map/pool/pallas_call | solution.py:328
  70.4 0.0 copy-start.2
  70.4 2.2 %final.2 = bf16[128,1536]{1,0:T(8,128)(2,1)S(1)} custom-call(bf16[64,1536]{1,0:T(8,128)(2,1)S(1)} %collective-permute-done.11.cross_ref, bf16[64,1536]{1,0:T(8,128)(2,1)S(1)} %collective-permute-done.12.inner_ref, f32[128,1536]{1,0:T(8,128)S(1)} %get-tuple-element.67.part_ref, f32[128,1536]{1,0:T(8,128)S(1)} %get-tuple-element.68.acc_ref, ...), custom_call_target="tpu_custom_call" | custom-call | flops 603979776 | bytes 9996288 | tf_op jit(solution)/shard_map/final/pallas_call | solution.py:328
  72.6 2.1 %collective-permute-start.15 = (bf16[128,1536]{1,0:T(8,128)(2,1)S(1)}, bf16[128,1536]{1,0:T(8,128)(2,1)S(1)}, u32[]{:S(2)}, u32[]{:S(2)}) collective-permute-start(bf16[128,1536]{1,0:T(8,128)(2,1)S(1)} %final.2), channel_id=1, source_target_pairs={{0,242},{1,243},{2,240},{3,241},{4,246},{5,247},{6,244},{7,245},{8... | collective-permute-start | bytes 1179656 | tf_op jit(solution)/shard_map/ppermute | solution.py:371
  74.7 3.6 %collective-permute-start.13 = (bf16[128,1536]{1,0:T(8,128)(2,1)S(1)}, bf16[128,1536]{1,0:T(8,128)(2,1)S(1)}, u32[]{:S(2)}, u32[]{:S(2)}) collective-permute-start(bf16[128,1536]{1,0:T(8,128)(2,1)S(1)} %get-tuple-element.69.own_ref), channel_id=1, source_target_pairs={{1,2},{2,1},{3,4},{4,3},{5,6},{6,5},{7,8},{8,7},{9,10},{10,9},{11,... | collective-permute-start | bytes 1179656 | tf_op jit(solution)/shard_map/ppermute | solution.py:380
  78.4 5.0 %collective-permute-done.15.gb_ref = bf16[128,1536]{1,0:T(8,128)(2,1)S(1)} collective-permute-done((bf16[128,1536]{1,0:T(8,128)(2,1)S(1)}, bf16[128,1536]{1,0:T(8,128)(2,1)S(1)}, u32[]{:S(2)}, u32[]{:S(2)}) %collective-permute-start.15) | collective-permute-done | bytes 393248 | tf_op jit(solution)/shard_map/ppermute | solution.py:371
  83.4 4.1 %collective-permute-start.18 = (bf16[128,1536]{1,0:T(8,128)(2,1)S(1)}, bf16[128,1536]{1,0:T(8,128)(2,1)S(1)}, u32[]{:S(2)}, u32[]{:S(2)}) collective-permute-start(bf16[128,1536]{1,0:T(8,128)(2,1)S(1)} %collective-permute-done.15.gb_ref), channel_id=1, source_target_pairs={{0,240},{1,241},{2,242},{3,243},{4,244},{5,245},{6,246},{7,247},{8... | collective-permute-start | bytes 1179656 | tf_op jit(solution)/shard_map/ppermute | solution.py:371
  87.5 0.9 gradatt.3.grad_ref
  88.4 3.5 %attention.1 = (bf16[128,768]{1,0:T(8,128)(2,1)S(1)}, bf16[128,768]{1,0:T(8,128)(2,1)S(1)}, bf16[128,1536]{1,0:T(8,128)(2,1)S(1)}, bf16[128,1536]{1,0:T(8,128)(2,1)S(1)}) custom-call(s32[16,2]{1,0:T(8,128)S(1)} %copy.16.refs_0_.owner_ref, f32[12]{0:T(128)S(1)} %bitcast.43, bf16[128,768]{1,0:T(8,128)(2,1)S(1)} %get-tuple-element.57.proj_ref, ...), custom_call_target="tpu_custom_call" | custom-call | flops 805306368 | bytes 1573040 | tf_op jit(solution)/shard_map/attention/pallas_call | solution.py:328
  91.8 1.9 %collective-permute-start.17 = (bf16[128,1536]{1,0:T(8,128)(2,1)S(1)}, bf16[128,1536]{1,0:T(8,128)(2,1)S(1)}, u32[]{:S(2)}, u32[]{:S(2)}) collective-permute-start(bf16[128,1536]{1,0:T(8,128)(2,1)S(1)} %get-tuple-element.72), channel_id=1, source_target_pairs={{0,1},{1,0},{2,3},{3,2},{4,5},{5,4},{6,7},{7,6},{8,9},{9,8},{10,11... | collective-permute-start | bytes 1179656 | tf_op jit(solution)/shard_map/ppermute | solution.py:385
  93.7 2.5 %collective-permute-start.16 = (bf16[128,1536]{1,0:T(8,128)(2,1)S(1)}, bf16[128,1536]{1,0:T(8,128)(2,1)S(1)}, u32[]{:S(2)}, u32[]{:S(2)}) collective-permute-start(bf16[128,1536]{1,0:T(8,128)(2,1)S(1)} %get-tuple-element.72), channel_id=1, source_target_pairs={{1,2},{2,1},{3,4},{4,3},{5,6},{6,5},{7,8},{8,7},{9,10},{10,9},{11,... | collective-permute-start | bytes 1179656 | tf_op jit(solution)/shard_map/ppermute | solution.py:380
  96.3 1.5 %output.1 = bf16[128,1536]{1,0:T(8,128)(2,1)S(1)} custom-call(bf16[128,768]{1,0:T(8,128)(2,1)S(1)} %get-tuple-element.74.att_ref, bf16[768,1536]{1,0:T(8,128)(2,1)S(1)} %bitcast.29, bf16[128,1536]{1,0:T(8,128)(2,1)} %collective-permute-done.4.b_ref), custom_call_target="tpu_custom_call" | custom-call | flops 301989888 | bytes 2949120 | tf_op jit(solution)/shard_map/output/pallas_call | solution.py:328
  97.8 6.0 %collective-permute-done.16.cross_ref = bf16[128,1536]{1,0:T(8,128)(2,1)S(1)} collective-permute-done((bf16[128,1536]{1,0:T(8,128)(2,1)S(1)}, bf16[128,1536]{1,0:T(8,128)(2,1)S(1)}, u32[]{:S(2)}, u32[]{:S(2)}) %collective-permute-start.16) | collective-permute-done | bytes 393248 | tf_op jit(solution)/shard_map/ppermute | solution.py:380
  103.8 4.8 %collective-permute-start.21 = (bf16[128,1536]{1,0:T(8,128)(2,1)S(1)}, bf16[128,1536]{1,0:T(8,128)(2,1)S(1)}, u32[]{:S(2)}, u32[]{:S(2)}) collective-permute-start(bf16[128,1536]{1,0:T(8,128)(2,1)S(1)} %collective-permute-done.6.a_ref), channel_id=1, source_target_pairs={{0,240},{1,241},{2,242},{3,243},{4,244},{5,245},{6,246},{7,247},{8... | collective-permute-start | bytes 1179656 | tf_op jit(solution)/shard_map/ppermute | solution.py:371
  108.6 1.6 %keys.3 = (bf16[128,1536]{1,0:T(8,128)(2,1)S(1)}, bf16[64,1536]{1,0:T(8,128)(2,1)S(1)}, bf16[64,1536]{1,0:T(8,128)(2,1)S(1)}) custom-call(s32[16,2]{1,0:T(8,128)S(1)} %copy.16.refs_0_.owner_ref, bf16[128,1536]{1,0:T(8,128)(2,1)S(1)} %get-tuple-element.71.own_ref, bf16[128,1536]{1,0:T(8,128)(2,1)S(1)} %collective-permute-done.16.cross_ref, ...), custom_call_target="tpu_custom_call" | custom-call | flops 7864320 | bytes 1376384 | tf_op jit(solution)/shard_map/keys/pallas_call | solution.py:328
  110.2 4.0 %collective-permute-start.19 = (bf16[64,1536]{1,0:T(8,128)(2,1)S(1)}, bf16[64,1536]{1,0:T(8,128)(2,1)S(1)}, u32[]{:S(2)}, u32[]{:S(2)}) collective-permute-start(bf16[64,1536]{1,0:T(8,128)(2,1)S(1)} %get-tuple-element.79), channel_id=1, source_target_pairs={{1,2},{2,1},{3,4},{4,3},{5,6},{6,5},{7,8},{8,7},{9,10},{10,9},{11,... | collective-permute-start | bytes 589832 | tf_op jit(solution)/shard_map/ppermute | solution.py:380
  114.2 0.1 collective-permute-start.20
  114.3 1.0 local.3
  115.3 2.8 %collective-permute-done.19.cross_ref = bf16[64,1536]{1,0:T(8,128)(2,1)S(1)} collective-permute-done((bf16[64,1536]{1,0:T(8,128)(2,1)S(1)}, bf16[64,1536]{1,0:T(8,128)(2,1)S(1)}, u32[]{:S(2)}, u32[]{:S(2)}) %collective-permute-start.19) | collective-permute-done | bytes 196640 | tf_op jit(solution)/shard_map/ppermute | solution.py:380
  118.1 0.3 collective-permute-done.21.refs_1_
  118.4 2.2 %final.3 = bf16[128,1536]{1,0:T(8,128)(2,1)S(1)} custom-call(bf16[64,1536]{1,0:T(8,128)(2,1)S(1)} %collective-permute-done.19.cross_ref, bf16[64,1536]{1,0:T(8,128)(2,1)S(1)} %collective-permute-done.20.inner_ref, f32[128,1536]{1,0:T(8,128)S(1)} %get-tuple-element.93.part_ref, f32[128,1536]{1,0:T(8,128)S(1)} %get-tuple-element.94.acc_ref, ...), custom_call_target="tpu_custom_call" | custom-call | flops 603979776 | bytes 9996288 | tf_op jit(solution)/shard_map/final/pallas_call | solution.py:328
  120.6 5.7 %collective-permute-start.23 = (bf16[128,1536]{1,0:T(8,128)(2,1)S(1)}, bf16[128,1536]{1,0:T(8,128)(2,1)S(1)}, u32[]{:S(2)}, u32[]{:S(2)}) collective-permute-start(bf16[128,1536]{1,0:T(8,128)(2,1)S(1)} %final.3), channel_id=1, source_target_pairs={{0,240},{1,241},{2,242},{3,243},{4,244},{5,245},{6,246},{7,247},{8... | collective-permute-start | bytes 1179656 | tf_op jit(solution)/shard_map/ppermute | solution.py:371
  126.3 0.1 collective-permute-start.22
  126.3 8.8 %collective-permute-done.23 = bf16[128,1536]{1,0:T(8,128)(2,1)S(1)} collective-permute-done((bf16[128,1536]{1,0:T(8,128)(2,1)S(1)}, bf16[128,1536]{1,0:T(8,128)(2,1)S(1)}, u32[]{:S(2)}, u32[]{:S(2)}) %collective-permute-start.23) | collective-permute-done | bytes 393248 | tf_op jit(solution)/shard_map/ppermute | solution.py:371
  135.2 8.3 %collective-permute-done.22.refs_0_ = bf16[128,1536]{1,0:T(8,128)(2,1)S(1)} collective-permute-done((bf16[128,1536]{1,0:T(8,128)(2,1)S(1)}, bf16[128,1536]{1,0:T(8,128)(2,1)S(1)}, u32[]{:S(2)}, u32[]{:S(2)}) %collective-permute-start.22) | collective-permute-done | bytes 393248 | tf_op jit(solution)/shard_map/ppermute | solution.py:371
  143.5 1.1 settle.1
  144.6 0.7 copy.18
  (35 shorter events, 0.1 us)
Async XLA Ops:
  0.6 17.9 %copy-start.3 = (f32[1,27,1536]{2,0,1:T(1,128)S(1)}, f32[1,27,1536]{2,0,1:T(1,128)}, u32[]{:S(2)}) copy-start(f32[1,27,1536]{2,0,1:T(1,128)} %param.15) | copy-start | bytes 497668
  0.7 17.9 %copy-start = (bf16[1,1536,2304]{2,1,0:T(8,128)(2,1)S(1)}, bf16[1,1536,2304]{2,1,0:T(8,128)(2,1)}, u32[]{:S(2)}) copy-start(bf16[1,1536,2304]{2,1,0:T(8,128)(2,1)} %param.13) | copy-start | bytes 21233668
  1.9 16.6 %collective-permute-start.1 = (bf16[64,1536]{1,0:T(8,128)(2,1)S(1)}, bf16[64,1536]{1,0:T(8,128)(2,1)S(1)}, u32[]{:S(2)}, u32[]{:S(2)}) collective-permute-start(bf16[64,1536]{1,0:T(8,128)(2,1)S(1)} %get-tuple-element.98), channel_id=1, source_target_pairs={{0,1},{1,0},{2,3},{3,2},{4,5},{5,4},{6,7},{7,6},{8,9},{9,8},{10,11... | collective-permute-start | bytes 589832 | tf_op jit(solution)/shard_map/ppermute | solution.py:385
  2.6 15.9 %collective-permute-start = (bf16[64,1536]{1,0:T(8,128)(2,1)S(1)}, bf16[64,1536]{1,0:T(8,128)(2,1)S(1)}, u32[]{:S(2)}, u32[]{:S(2)}) collective-permute-start(bf16[64,1536]{1,0:T(8,128)(2,1)S(1)} %get-tuple-element.99), channel_id=1, source_target_pairs={{1,2},{2,1},{3,4},{4,3},{5,6},{6,5},{7,8},{8,7},{9,10},{10,9},{11,... | collective-permute-start | bytes 589832 | tf_op jit(solution)/shard_map/ppermute | solution.py:380
  5.8 25.0 %collective-permute-start.5 = (bf16[128,1536]{1,0:T(8,128)(2,1)}, bf16[128,1536]{1,0:T(8,128)(2,1)S(1)}, u32[]{:S(2)}, u32[]{:S(2)}) collective-permute-start(bf16[128,1536]{1,0:T(8,128)(2,1)} %bitcast.40), channel_id=1, source_target_pairs={{0,242},{1,243},{2,240},{3,241},{4,246},{5,247},{6,244},{7,245},{8... | collective-permute-start | bytes 1179656 | tf_op jit(solution)/shard_map/ppermute | solution.py:371
  12.4 18.4 %collective-permute-start.4 = (bf16[128,1536]{1,0:T(8,128)(2,1)}, bf16[128,1536]{1,0:T(8,128)(2,1)}, u32[]{:S(2)}, u32[]{:S(2)}) collective-permute-start(bf16[128,1536]{1,0:T(8,128)(2,1)} %bitcast.36), channel_id=1, source_target_pairs={{0,242},{1,243},{2,240},{3,241},{4,246},{5,247},{6,244},{7,245},{8... | collective-permute-start | bytes 1179656 | tf_op jit(solution)/shard_map/ppermute | solution.py:371
  13.1 14.1 %copy-start.12 = (s32[16,2]{0,1:T(2,128)S(1)}, s32[16,2]{0,1:T(2,128)}, u32[]{:S(2)}) copy-start(s32[16,2]{0,1:T(2,128)} %param.17) | copy-start | bytes 388
  17.8 0.7 copy-start.7
  18.5 15.0 %copy-start.11 = (f32[1,12]{1,0:T(1,128)S(1)}, f32[1,12]{1,0:T(1,128)}, u32[]{:S(2)}) copy-start(f32[1,12]{1,0:T(1,128)} %param.16) | copy-start | bytes 148
  18.5 47.2 %slice-start = ((s8[7077888]{0:T(1024)(128)(4,1)}), s8[2883584]{0:T(1024)(128)(4,1)S(1)}, s32[]{:S(2)}) async-start(s8[7077888]{0:T(1024)(128)(4,1)} %bitcast.18), calls=%async_computation | async-start | bytes 5767168
  21.6 0.7 copy-start.9
  22.2 8.6 %collective-permute-start.3 = (bf16[128,1536]{1,0:T(8,128)(2,1)}, bf16[128,1536]{1,0:T(8,128)(2,1)}, u32[]{:S(2)}, u32[]{:S(2)}) collective-permute-start(bf16[128,1536]{1,0:T(8,128)(2,1)} %get-tuple-element.52.refs_3_), channel_id=1, source_target_pairs={{0,1},{1,0},{2,3},{3,2},{4,5},{5,4},{6,7},{7,6},{8,9},{9,8},{10,11... | collective-permute-start | bytes 1179656 | tf_op jit(solution)/shard_map/ppermute | solution.py:385
  23.1 10.4 %collective-permute-start.2 = (bf16[128,1536]{1,0:T(8,128)(2,1)}, bf16[128,1536]{1,0:T(8,128)(2,1)}, u32[]{:S(2)}, u32[]{:S(2)}) collective-permute-start(bf16[128,1536]{1,0:T(8,128)(2,1)} %get-tuple-element.52.refs_3_), channel_id=1, source_target_pairs={{1,2},{2,1},{3,4},{4,3},{5,6},{6,5},{7,8},{8,7},{9,10},{10,9},{11,... | collective-permute-start | bytes 1179656 | tf_op jit(solution)/shard_map/ppermute | solution.py:380
  27.2 1.7 %copy-start.1 = (bf16[1,768,1536]{2,1,0:T(8,128)(2,1)S(1)}, bf16[1,768,1536]{2,1,0:T(8,128)(2,1)}, u32[]{:S(2)}) copy-start(bf16[1,768,1536]{2,1,0:T(8,128)(2,1)} %param.14) | copy-start | bytes 7077892
  28.9 1.0 copy-start.6
  29.9 35.8 %slice-start.1 = ((s8[7077888]{0:T(1024)(128)(4,1)}), s8[4194304]{0:T(1024)(128)(4,1)S(1)}, s32[]{:S(2)}) async-start(s8[7077888]{0:T(1024)(128)(4,1)} %bitcast.18), calls=%async_computation.1 | async-start | bytes 8388608
  33.5 0.9 copy-start.8
  39.3 12.4 %collective-permute-start.6 = (bf16[128,1536]{1,0:T(8,128)(2,1)S(1)}, bf16[128,1536]{1,0:T(8,128)(2,1)S(1)}, u32[]{:S(2)}, u32[]{:S(2)}) collective-permute-start(bf16[128,1536]{1,0:T(8,128)(2,1)S(1)} %get-tuple-element.56), channel_id=1, source_target_pairs={{0,242},{1,243},{2,240},{3,241},{4,246},{5,247},{6,244},{7,245},{8... | collective-permute-start | bytes 1179656 | tf_op jit(solution)/shard_map/ppermute | solution.py:371
  43.4 12.7 %collective-permute-start.10 = (bf16[128,1536]{1,0:T(8,128)(2,1)S(1)}, bf16[128,1536]{1,0:T(8,128)(2,1)S(1)}, u32[]{:S(2)}, u32[]{:S(2)}) collective-permute-start(bf16[128,1536]{1,0:T(8,128)(2,1)S(1)} %get-tuple-element.61), channel_id=1, source_target_pairs={{0,1},{1,0},{2,3},{3,2},{4,5},{5,4},{6,7},{7,6},{8,9},{9,8},{10,11... | collective-permute-start | bytes 1179656 | tf_op jit(solution)/shard_map/ppermute | solution.py:385
  43.4 12.8 %collective-permute-start.9 = (bf16[128,1536]{1,0:T(8,128)(2,1)S(1)}, bf16[128,1536]{1,0:T(8,128)(2,1)S(1)}, u32[]{:S(2)}, u32[]{:S(2)}) collective-permute-start(bf16[128,1536]{1,0:T(8,128)(2,1)S(1)} %get-tuple-element.61), channel_id=1, source_target_pairs={{1,2},{2,1},{3,4},{4,3},{5,6},{6,5},{7,8},{8,7},{9,10},{10,9},{11,... | collective-permute-start | bytes 1179656 | tf_op jit(solution)/shard_map/ppermute | solution.py:380
  51.8 16.3 %collective-permute-start.8 = (bf16[64,1536]{1,0:T(8,128)(2,1)S(1)}, bf16[64,1536]{1,0:T(8,128)(2,1)S(1)}, u32[]{:S(2)}, u32[]{:S(2)}) collective-permute-start(bf16[64,1536]{1,0:T(8,128)(2,1)S(1)} %get-tuple-element.96), channel_id=1, source_target_pairs={{0,1},{1,0},{2,3},{3,2},{4,5},{5,4},{6,7},{7,6},{8,9},{9,8},{10,11... | collective-permute-start | bytes 589832 | tf_op jit(solution)/shard_map/ppermute | solution.py:385
  51.9 16.2 %collective-permute-start.7 = (bf16[64,1536]{1,0:T(8,128)(2,1)S(1)}, bf16[64,1536]{1,0:T(8,128)(2,1)S(1)}, u32[]{:S(2)}, u32[]{:S(2)}) collective-permute-start(bf16[64,1536]{1,0:T(8,128)(2,1)S(1)} %get-tuple-element.97), channel_id=1, source_target_pairs={{1,2},{2,1},{3,4},{4,3},{5,6},{6,5},{7,8},{8,7},{9,10},{10,9},{11,... | collective-permute-start | bytes 589832 | tf_op jit(solution)/shard_map/ppermute | solution.py:380
  56.1 0.9 copy-start.10
  58.7 11.8 %collective-permute-start.11 = (bf16[64,1536]{1,0:T(8,128)(2,1)S(1)}, bf16[64,1536]{1,0:T(8,128)(2,1)S(1)}, u32[]{:S(2)}, u32[]{:S(2)}) collective-permute-start(bf16[64,1536]{1,0:T(8,128)(2,1)S(1)} %get-tuple-element.63), channel_id=1, source_target_pairs={{1,2},{2,1},{3,4},{4,3},{5,6},{6,5},{7,8},{8,7},{9,10},{10,9},{11,... | collective-permute-start | bytes 589832 | tf_op jit(solution)/shard_map/ppermute | solution.py:380
  61.1 9.3 %collective-permute-start.12 = (bf16[64,1536]{1,0:T(8,128)(2,1)S(1)}, bf16[64,1536]{1,0:T(8,128)(2,1)S(1)}, u32[]{:S(2)}, u32[]{:S(2)}) collective-permute-start(bf16[64,1536]{1,0:T(8,128)(2,1)S(1)} %get-tuple-element.64), channel_id=1, source_target_pairs={{0,1},{1,0},{2,3},{3,2},{4,5},{5,4},{6,7},{7,6},{8,9},{9,8},{10,11... | collective-permute-start | bytes 589832 | tf_op jit(solution)/shard_map/ppermute | solution.py:385
  66.7 3.7 %copy-start.4 = (bf16[1,128,1536]{2,1,0:T(8,128)(2,1)S(1)}, bf16[1,128,1536]{2,1,0:T(8,128)(2,1)}, u32[]{:S(2)}) copy-start(bf16[1,128,1536]{2,1,0:T(8,128)(2,1)} %param.9) | copy-start | bytes 1179652
  66.7 3.7 %copy-start.5 = (bf16[1,128,1536]{2,1,0:T(8,128)(2,1)S(1)}, bf16[1,128,1536]{2,1,0:T(8,128)(2,1)}, u32[]{:S(2)}) copy-start(bf16[1,128,1536]{2,1,0:T(8,128)(2,1)} %param.11) | copy-start | bytes 1179652
  70.4 17.1 %copy-start.2 = (bf16[1,768,1536]{2,1,0:T(8,128)(2,1)S(1)}, bf16[1,768,1536]{2,1,0:T(8,128)(2,1)}, u32[]{:S(2)}) copy-start(bf16[1,768,1536]{2,1,0:T(8,128)(2,1)} %param.14) | copy-start | bytes 7077892
  72.6 10.8 %collective-permute-start.15 = (bf16[128,1536]{1,0:T(8,128)(2,1)S(1)}, bf16[128,1536]{1,0:T(8,128)(2,1)S(1)}, u32[]{:S(2)}, u32[]{:S(2)}) collective-permute-start(bf16[128,1536]{1,0:T(8,128)(2,1)S(1)} %final.2), channel_id=1, source_target_pairs={{0,242},{1,243},{2,240},{3,241},{4,246},{5,247},{6,244},{7,245},{8... | collective-permute-start | bytes 1179656 | tf_op jit(solution)/shard_map/ppermute | solution.py:371
  74.7 13.7 %collective-permute-start.14 = (bf16[128,1536]{1,0:T(8,128)(2,1)S(1)}, bf16[128,1536]{1,0:T(8,128)(2,1)S(1)}, u32[]{:S(2)}, u32[]{:S(2)}) collective-permute-start(bf16[128,1536]{1,0:T(8,128)(2,1)S(1)} %get-tuple-element.69.own_ref), channel_id=1, source_target_pairs={{0,1},{1,0},{2,3},{3,2},{4,5},{5,4},{6,7},{7,6},{8,9},{9,8},{10,11... | collective-permute-start | bytes 1179656 | tf_op jit(solution)/shard_map/ppermute | solution.py:385
  74.7 13.7 %collective-permute-start.13 = (bf16[128,1536]{1,0:T(8,128)(2,1)S(1)}, bf16[128,1536]{1,0:T(8,128)(2,1)S(1)}, u32[]{:S(2)}, u32[]{:S(2)}) collective-permute-start(bf16[128,1536]{1,0:T(8,128)(2,1)S(1)} %get-tuple-element.69.own_ref), channel_id=1, source_target_pairs={{1,2},{2,1},{3,4},{4,3},{5,6},{6,5},{7,8},{8,7},{9,10},{10,9},{11,... | collective-permute-start | bytes 1179656 | tf_op jit(solution)/shard_map/ppermute | solution.py:380
  83.4 12.9 %collective-permute-start.18 = (bf16[128,1536]{1,0:T(8,128)(2,1)S(1)}, bf16[128,1536]{1,0:T(8,128)(2,1)S(1)}, u32[]{:S(2)}, u32[]{:S(2)}) collective-permute-start(bf16[128,1536]{1,0:T(8,128)(2,1)S(1)} %collective-permute-done.15.gb_ref), channel_id=1, source_target_pairs={{0,240},{1,241},{2,242},{3,243},{4,244},{5,245},{6,246},{7,247},{8... | collective-permute-start | bytes 1179656 | tf_op jit(solution)/shard_map/ppermute | solution.py:371
  91.8 5.9 %collective-permute-start.17 = (bf16[128,1536]{1,0:T(8,128)(2,1)S(1)}, bf16[128,1536]{1,0:T(8,128)(2,1)S(1)}, u32[]{:S(2)}, u32[]{:S(2)}) collective-permute-start(bf16[128,1536]{1,0:T(8,128)(2,1)S(1)} %get-tuple-element.72), channel_id=1, source_target_pairs={{0,1},{1,0},{2,3},{3,2},{4,5},{5,4},{6,7},{7,6},{8,9},{9,8},{10,11... | collective-permute-start | bytes 1179656 | tf_op jit(solution)/shard_map/ppermute | solution.py:385
  93.7 10.1 %collective-permute-start.16 = (bf16[128,1536]{1,0:T(8,128)(2,1)S(1)}, bf16[128,1536]{1,0:T(8,128)(2,1)S(1)}, u32[]{:S(2)}, u32[]{:S(2)}) collective-permute-start(bf16[128,1536]{1,0:T(8,128)(2,1)S(1)} %get-tuple-element.72), channel_id=1, source_target_pairs={{1,2},{2,1},{3,4},{4,3},{5,6},{6,5},{7,8},{8,7},{9,10},{10,9},{11,... | collective-permute-start | bytes 1179656 | tf_op jit(solution)/shard_map/ppermute | solution.py:380
  103.8 14.6 %collective-permute-start.21 = (bf16[128,1536]{1,0:T(8,128)(2,1)S(1)}, bf16[128,1536]{1,0:T(8,128)(2,1)S(1)}, u32[]{:S(2)}, u32[]{:S(2)}) collective-permute-start(bf16[128,1536]{1,0:T(8,128)(2,1)S(1)} %collective-permute-done.6.a_ref), channel_id=1, source_target_pairs={{0,240},{1,241},{2,242},{3,243},{4,244},{5,245},{6,246},{7,247},{8... | collective-permute-start | bytes 1179656 | tf_op jit(solution)/shard_map/ppermute | solution.py:371
  110.2 7.9 %collective-permute-start.19 = (bf16[64,1536]{1,0:T(8,128)(2,1)S(1)}, bf16[64,1536]{1,0:T(8,128)(2,1)S(1)}, u32[]{:S(2)}, u32[]{:S(2)}) collective-permute-start(bf16[64,1536]{1,0:T(8,128)(2,1)S(1)} %get-tuple-element.79), channel_id=1, source_target_pairs={{1,2},{2,1},{3,4},{4,3},{5,6},{6,5},{7,8},{8,7},{9,10},{10,9},{11,... | collective-permute-start | bytes 589832 | tf_op jit(solution)/shard_map/ppermute | solution.py:380
  114.2 3.9 %collective-permute-start.20 = (bf16[64,1536]{1,0:T(8,128)(2,1)S(1)}, bf16[64,1536]{1,0:T(8,128)(2,1)S(1)}, u32[]{:S(2)}, u32[]{:S(2)}) collective-permute-start(bf16[64,1536]{1,0:T(8,128)(2,1)S(1)} %get-tuple-element.80), channel_id=1, source_target_pairs={{0,1},{1,0},{2,3},{3,2},{4,5},{5,4},{6,7},{7,6},{8,9},{9,8},{10,11... | collective-permute-start | bytes 589832 | tf_op jit(solution)/shard_map/ppermute | solution.py:385
  120.6 14.6 %collective-permute-start.23 = (bf16[128,1536]{1,0:T(8,128)(2,1)S(1)}, bf16[128,1536]{1,0:T(8,128)(2,1)S(1)}, u32[]{:S(2)}, u32[]{:S(2)}) collective-permute-start(bf16[128,1536]{1,0:T(8,128)(2,1)S(1)} %final.3), channel_id=1, source_target_pairs={{0,240},{1,241},{2,242},{3,243},{4,244},{5,245},{6,246},{7,247},{8... | collective-permute-start | bytes 1179656 | tf_op jit(solution)/shard_map/ppermute | solution.py:371
  126.3 17.3 %collective-permute-start.22 = (bf16[128,1536]{1,0:T(8,128)(2,1)S(1)}, bf16[128,1536]{1,0:T(8,128)(2,1)S(1)}, u32[]{:S(2)}, u32[]{:S(2)}) collective-permute-start(bf16[128,1536]{1,0:T(8,128)(2,1)S(1)} %output.1), channel_id=1, source_target_pairs={{0,240},{1,241},{2,242},{3,243},{4,244},{5,245},{6,246},{7,247},{8... | collective-permute-start | bytes 1179656 | tf_op jit(solution)/shard_map/ppermute | solution.py:371
